TPU v7x, 32 devices: a whole 2x2x4 slice. The times are simulated.
32 devices in a mesh: species: 2 (over core), dp: 4 (over z), seq: 4 (over y, x).
Axes of the slice: x: 2, y: 2, z: 4, core: 2. Of those that a mesh axis runs over, the one named last changes fastest.
Arguments:
- inputs: bfloat16 [2, 4, 1536, 1536], P('species', 'dp', 'seq'), may hold values from -30 to 30
- crop_start: int32 [2, 4], P('species', 'dp'), may hold values from 96 to 544, as said below
- rel_bucket: int32 [3071], replicated, may hold values from 0 to 31
- conv_weight: bfloat16 [7680, 1536], P(('species', 'dp', 'seq')), may hold values from -0.125 to 0.125
- query_weight: bfloat16 [1536, 512], P(('species', 'dp', 'seq')), may hold values from -0.15625 to 0.15625
- key_weight: bfloat16 [1536, 512], P(('species', 'dp', 'seq')), may hold values from -0.15625 to 0.15625
- value_weight: bfloat16 [1536, 1536], P(('species', 'dp', 'seq')), may hold values from -0.15625 to 0.15625
- out_weight: bfloat16 [1536, 1536], P(('species', 'dp', 'seq')), may hold values from -2 to 2
- up_weight: bfloat16 [1536, 3072], P(('species', 'dp', 'seq')), may hold values from -0.15625 to 0.15625
- down_weight: bfloat16 [3072, 1536], P(('species', 'dp', 'seq')), may hold values from -0.109375 to 0.109375
- point_weight: bfloat16 [1536, 3072], P(('species', 'dp', 'seq')), may hold values from -0.15625 to 0.15625
- rel_table: bfloat16 [256], P(('species', 'dp', 'seq')), may hold values from -3 to 3
- bn_gain: bfloat16 [1536], P(('species', 'dp', 'seq')), may hold values from 0.5 to 1.5
- bn_shift: bfloat16 [1536], P(('species', 'dp', 'seq')), may hold values from -1 to 1
- conv_bias: bfloat16 [1536], P(('species', 'dp', 'seq')), may hold values from -1 to 1
- attn_gain: bfloat16 [1536], P(('species', 'dp', 'seq')), may hold values from 0.5 to 1.5
- attn_shift: bfloat16 [1536], P(('species', 'dp', 'seq')), may hold values from -1 to 1
- ffn_gain: bfloat16 [1536], P(('species', 'dp', 'seq')), may hold values from 0.5 to 1.5
- ffn_shift: bfloat16 [1536], P(('species', 'dp', 'seq')), may hold values from -1 to 1
- up_bias: bfloat16 [3072], P(('species', 'dp', 'seq')), may hold values from -1 to 1
- down_bias: bfloat16 [1536], P(('species', 'dp', 'seq')), may hold values from -1 to 1
- point_bias: bfloat16 [3072], P(('species', 'dp', 'seq')), may hold values from -1 to 1
- head_weight: bfloat16 [2, 3072, 5313], P('species', ('dp', 'seq')), may hold values from -0.109375 to 0.109375
- pred_grad: bfloat16 [2, 4, 896, 5313], P('species', 'dp', 'seq'), may hold values from -6 to 6
Outputs:
- predictions: bfloat16 [2, 4, 896, 5313], P('species', 'dp', 'seq')
- input_grad: float32 [2, 4, 1536, 1536], P('species', 'dp', 'seq')
- conv_weight_grad: float32 [7680, 1536], P(('species', 'dp', 'seq'))
- query_weight_grad: float32 [1536, 512], P(('species', 'dp', 'seq'))
- key_weight_grad: float32 [1536, 512], P(('species', 'dp', 'seq'))
- value_weight_grad: float32 [1536, 1536], P(('species', 'dp', 'seq'))
- out_weight_grad: float32 [1536, 1536], P(('species', 'dp', 'seq'))
- up_weight_grad: float32 [1536, 3072], P(('species', 'dp', 'seq'))
- down_weight_grad: float32 [3072, 1536], P(('species', 'dp', 'seq'))
- point_weight_grad: float32 [1536, 3072], P(('species', 'dp', 'seq'))
- rel_table_grad: float32 [256], P(('species', 'dp', 'seq'))
- bn_gain_grad: float32 [1536], P(('species', 'dp', 'seq'))
- bn_shift_grad: float32 [1536], P(('species', 'dp', 'seq'))
- conv_bias_grad: float32 [1536], P(('species', 'dp', 'seq'))
- attn_gain_grad: float32 [1536], P(('species', 'dp', 'seq'))
- attn_shift_grad: float32 [1536], P(('species', 'dp', 'seq'))
- ffn_gain_grad: float32 [1536], P(('species', 'dp', 'seq'))
- ffn_shift_grad: float32 [1536], P(('species', 'dp', 'seq'))
- up_bias_grad: float32 [3072], P(('species', 'dp', 'seq'))
- down_bias_grad: float32 [1536], P(('species', 'dp', 'seq'))
- point_bias_grad: float32 [3072], P(('species', 'dp', 'seq'))
- head_weight_grad: float32 [2, 3072, 5313], P('species', ('dp', 'seq'))
Inputs may be any that keep to these rules, and one draw needn't show every extreme that they name: `crop_start`: the crop of 896 bins lies inside its sequence; in each species one sequence starts at the least value and another at the most. `rel_bucket`: entry j - i + 1535 holds the bucket of relative distance j - i.
All inputs are finite; a program needn't handle non-finite values.
Results may differ from a plain program's by a relative error of at most 0.038.
Values may be sent and summed in bfloat16 or wider, within the bound.
No kernel may reach another device: no remote copies, remote signals or barrier semaphores. Data moves between devices by JAX's collectives and lax.ppermute only.
A program may use at most 448 MiB of HBM per device.

v0:
```python
import jax
import jax.numpy as jnp
from jax import lax
from jax.experimental import pallas as pl
from jax.experimental.pallas import tpu as pltpu
from jax.sharding import PartitionSpec as P

HEADS = 8
QK = 64
V = 192
TRK_M = 1643
WIDTH = 5
NB = 32
EPSILON = 1e-05
ROWS = 128
BLOCK = 512
CONV_CHUNKS = 3
EVERYWHERE = ("species", "dp", "seq")


def _head_lanes(e):
    lane = lax.broadcasted_iota(jnp.int32, (1, 2 * QK), 1)
    return (lane >= QK) == (e == 1)

def _toeplitz(u):
    wide = jnp.broadcast_to(u, (ROWS, u.shape[-1]))
    return pltpu.roll(wide, 0, 1, stride=1, stride_axis=0)

def _soft(q, k, bias):
    s = lax.dot_general(q, k, (((1,), (1,)), ((), ())), preferred_element_type=jnp.float32) + bias
    e = jnp.exp(s - jnp.max(s, axis=-1, keepdims=True))
    return e * (1.0 / jnp.sum(e, axis=-1, keepdims=True))

def _join(first, second):
    lane = lax.broadcasted_iota(jnp.int32, (1, 128), 1)
    return jnp.concatenate([first[:, :128], jnp.where(lane < 64, first[:, 128:], second[:, :128]), second[:, 128:]], axis=1)

def attn_fwd_kernel(q_ref, k_ref, v_ref, u_ref, o_ref):
    rows = q_ref.shape[0]
    length = k_ref.shape[0]
    k = k_ref[...]
    tables = [_toeplitz(u_ref[0, e : e + 1, :]) for e in range(2)]
    for a in range(rows // ROWS):
        at = rows - ROWS * a
        span = slice(ROWS * a, ROWS * (a + 1))
        q = q_ref[span, :]
        outs = []
        for e in range(2):
            qe = jnp.where(_head_lanes(e), q, jnp.zeros_like(q))
            p = _soft(qe, k, tables[e][:, at : at + length]).astype(jnp.bfloat16)
            outs.append(jnp.dot(p, v_ref[:, 128 * e : 128 * e + 256], preferred_element_type=jnp.float32))
        o_ref[span, :] = _join(*outs).astype(o_ref.dtype)

def attn_fwd(q, k, v, u):
    rows, length = q.shape[0], k.shape[0]
    pairs = q.shape[1] // (2 * QK)
    return pl.pallas_call(
        attn_fwd_kernel,
        grid=(pairs,),
        in_specs=[
            pl.BlockSpec((rows, 2 * QK), lambda h: (0, h)),
            pl.BlockSpec((length, 2 * QK), lambda h: (0, h)),
            pl.BlockSpec((length, 2 * V), lambda h: (0, h)),
            pl.BlockSpec((1, 2, u.shape[-1]), lambda h: (h, 0, 0)),
        ],
        out_specs=pl.BlockSpec((rows, 2 * V), lambda h: (0, h)),
        out_shape=jax.ShapeDtypeStruct((rows, v.shape[1]), jnp.bfloat16),
        compiler_params=pltpu.CompilerParams(vmem_limit_bytes=48 * 2**20),
        name="attention_forward",
    )(q, k, v, u)

def attn_bwd_kernel(q_ref, k_ref, v_ref, u_ref, g_ref, dq_ref, dk_ref, dv_ref, du_ref, p_scr, s_scr, d_scr):
    rows = q_ref.shape[0]
    length = k_ref.shape[0]
    k = k_ref[...]
    lane2 = lax.broadcasted_iota(jnp.int32, (1, 256), 1)
    dqs, dks, dvs = [], [], []
    for e in range(2):
        table = _toeplitz(u_ref[0, e : e + 1, :])
        d_scr[...] = jnp.zeros_like(d_scr)
        keep = (lane2 < 192) if e == 0 else (lane2 >= 64)
        vcols = slice(128 * e, 128 * e + 256)
        for a in range(rows // ROWS):
            at = rows - ROWS * a
            span = slice(ROWS * a, ROWS * (a + 1))
            q = q_ref[span, :]
            qe = jnp.where(_head_lanes(e), q, jnp.zeros_like(q))
            p = _soft(qe, k, table[:, at : at + length])
            g = g_ref[span, vcols]
            g = jnp.where(keep, g, jnp.zeros_like(g))
            dp = lax.dot_general(g, v_ref[:, vcols], (((1,), (1,)), ((), ())), preferred_element_type=jnp.float32)
            ds = p * (dp - jnp.sum(p * dp, axis=-1, keepdims=True))
            p_scr[span, :] = p.astype(jnp.bfloat16)
            s_scr[span, :] = ds.astype(jnp.bfloat16)
            d_scr[:, at : at + length] += ds
        ds = s_scr[...]
        dqs.append(jnp.dot(ds, k, preferred_element_type=jnp.float32))
        dks.append(lax.dot_general(ds, q_ref[...], (((0,), (0,)), ((), ())), preferred_element_type=jnp.float32))
        dvs.append(lax.dot_general(p_scr[...], g_ref[:, vcols], (((0,), (0,)), ((), ())), preferred_element_type=jnp.float32))
        fold = d_scr[...]
        width = fold.shape[1]
        step = ROWS // 2
        while step:
            fold = fold[:step] + pltpu.roll(fold[step:], width - step, 1)
            step //= 2
        du_ref[0, e : e + 1, :] = fold
    lane = lax.broadcasted_iota(jnp.int32, (1, 128), 1)
    dq_ref[...] = (jnp.where(lane < QK, dqs[0], dqs[1]) * QK ** (-0.5)).astype(dq_ref.dtype)
    dk_ref[...] = jnp.where(lane < QK, dks[0], dks[1]).astype(dk_ref.dtype)
    dv_ref[...] = _join(*dvs).astype(dv_ref.dtype)

def attn_bwd(q, k, v, u, g):
    rows, length = q.shape[0], k.shape[0]
    pairs = q.shape[1] // (2 * QK)
    specs = [
            pl.BlockSpec((rows, 2 * QK), lambda h: (0, h)),
            pl.BlockSpec((length, 2 * QK), lambda h: (0, h)),
            pl.BlockSpec((length, 2 * V), lambda h: (0, h)),
            pl.BlockSpec((1, 2, u.shape[-1]), lambda h: (h, 0, 0)),
            ]
    return pl.pallas_call(
        attn_bwd_kernel,
        grid=(pairs,),
        in_specs=specs + [pl.BlockSpec((rows, 2 * V), lambda h: (0, h))],
        out_specs=specs,
        out_shape=[jax.ShapeDtypeStruct(q.shape, jnp.bfloat16), jax.ShapeDtypeStruct(k.shape, jnp.bfloat16), jax.ShapeDtypeStruct(v.shape, jnp.bfloat16), jax.ShapeDtypeStruct(u.shape, jnp.float32)],
        scratch_shapes=[pltpu.VMEM((rows, length), jnp.bfloat16), pltpu.VMEM((rows, length), jnp.bfloat16), pltpu.VMEM((ROWS, u.shape[-1]), jnp.float32)],
        compiler_params=pltpu.CompilerParams(vmem_limit_bytes=56 * 2**20),
        name="attention_backward",
    )(q, k, v, u, g)


def flip(x, bit):
    peers = lax.axis_size("seq")
    return lax.ppermute(x, "seq", [(i, i ^ bit) for i in range(peers)])


def swap_cores(x):
    return lax.ppermute(x, "species", [(0, 1), (1, 0)])


def to_upper_core(x):
    return lax.ppermute(x, "species", [(0, 1)])


def to_lower_core(x):
    return lax.ppermute(x, "species", [(1, 0)])


def pick(x, index, axis=0):
    return lax.dynamic_index_in_dim(x, index, axis, keepdims=False)


def sort_copies(moves, out_shapes, *pieces):
    def kernel(*refs):
        ins, refs = refs[: len(pieces)], refs[len(pieces) :]
        outs, refs = refs[: len(out_shapes)], refs[len(out_shapes) :]
        stages, (in_sems, out_sems) = refs[: len(out_shapes)], refs[len(out_shapes) :]
        place = {axis: lax.axis_index(axis) for axis in EVERYWHERE}
        arrivals, departures = [], []
        for i, (piece, source, array, target) in enumerate(moves(place)):
            stage = stages[array].at[target]
            arrivals.append(pltpu.make_async_copy(ins[piece].at[source], stage, in_sems.at[i]))
            departures.append(
                pltpu.make_async_copy(stage, outs[array].at[target], out_sems.at[i])
            )
        for copy in arrivals:
            copy.start()
        for arrival, departure in zip(arrivals, departures):
            arrival.wait()
            departure.start()
        for copy in departures:
            copy.wait()

    count = len(moves({axis: 0 for axis in EVERYWHERE}))
    held = sum(x.size * 4 for x in out_shapes) // 2
    return pl.pallas_call(
        kernel,
        in_specs=[pl.BlockSpec(memory_space=pl.ANY)] * len(pieces),
        out_specs=[pl.BlockSpec(memory_space=pl.ANY)] * len(out_shapes),
        out_shape=out_shapes,
        scratch_shapes=[pltpu.VMEM(x.shape, x.dtype) for x in out_shapes]
        + [pltpu.SemaphoreType.DMA((count,))] * 2,
        compiler_params=pltpu.CompilerParams(vmem_limit_bytes=held * 2 + 4 * 2**20),
        cost_estimate=pl.CostEstimate(flops=0, bytes_accessed=held * 2, transcendentals=0),
        name="sort_copies",
    )(*pieces)


def gather_all(shard, first, second, direct, widths=None):
    peers = lax.axis_size("dp")
    rows, columns = shard.shape
    widths = widths or [columns]
    if direct:
        pieces = [shard] + [
            lax.ppermute(shard, "dp", [(i, (i + k) % peers) for i in range(peers)])
            for k in range(1, peers)
        ]
        column = jnp.stack(pieces)
    else:
        column = lax.all_gather(shard, "dp")
    near = jnp.stack([column, flip(column, first)])
    far = flip(near, second)
    near_other = swap_cores(near)
    far_other = swap_cores(far)

    def moves(place):
        mine, seq, z = place["species"], place["seq"], place["dp"]
        found = []
        for piece, core, turn in (
            (0, mine, 0), (1, mine, second), (2, 1 - mine, 0), (3, 1 - mine, second)
        ):
            for m, bit in ((0, 0), (1, first)):
                home = seq ^ (turn ^ bit)
                begin = 0
                for array, width in enumerate(widths):
                    span = pl.ds(begin, width)
                    begin += width
                    if direct:
                        for k in range(peers):
                            at = lax.rem(z + (peers - k), peers)
                            found.append((piece, (m, k, slice(None), span), array, (core, at, home)))
                    else:
                        everything = slice(None)
                        found.append(
                            (piece, (m, everything, everything, span), array, (core, everything, home))
                        )
        return found

    outs = sort_copies(
        moves,
        [jax.ShapeDtypeStruct((2, peers, 4, rows, width), shard.dtype) for width in widths],
        near,
        far,
        near_other,
        far_other,
    )
    return [out.reshape(2 * peers * 4 * rows, out.shape[-1]) for out in outs]


def scatter_all(grad, first, second, direct):
    mine, place, z = lax.axis_index("species"), lax.axis_index("seq"), lax.axis_index("dp")
    peers = lax.axis_size("dp")
    low = jnp.bfloat16
    wide = jnp.float32
    half = (pick(grad, mine).astype(wide) + swap_cores(pick(grad, 1 - mine)).astype(wide)).astype(low)
    for bit in (first, second):
        axis = 1 if bit == 2 or half.ndim == 4 else 2
        here = lax.rem(lax.div(place, bit), 2)
        away = flip(pick(half, 1 - here, axis), bit)
        half = (pick(half, here, axis).astype(wide) + away.astype(wide)).astype(low)
    if direct:
        total = pick(half, z).astype(wide)
        for k in range(1, peers):
            sent = pick(half, lax.rem(z + k, peers))
            total = total + lax.ppermute(
                sent, "dp", [(i, (i + k) % peers) for i in range(peers)]
            ).astype(wide)
        return total
    return lax.psum_scatter(half, "dp", scatter_dimension=0, tiled=False).astype(wide)


def gather_plane(x):
    rows = x.shape[0]
    half = rows // 2
    from_x = flip(x, 1)
    from_y = flip(x, 2)
    top = flip(from_x[:half], 2)
    bottom = flip(from_y[half:], 1)

    def moves(place):
        seq = place["seq"]
        everything = slice(None)
        return [
            (0, (everything,), 0, (seq,)),
            (1, (everything,), 0, (seq ^ 1,)),
            (2, (everything,), 0, (seq ^ 2,)),
            (3, (everything,), 0, (seq ^ 3, pl.ds(0, half))),
            (4, (everything,), 0, (seq ^ 3, pl.ds(half, half))),
        ]

    out = sort_copies(
        moves, [jax.ShapeDtypeStruct((4,) + x.shape, x.dtype)], x, from_x, from_y, top, bottom
    )[0]
    return out.reshape((4 * rows,) + x.shape[1:])


def scatter_plane(x):
    place = lax.axis_index("seq")
    rows, columns = x.shape[0] // 4, x.shape[1]
    half = rows // 2
    low = jnp.bfloat16
    wide = jnp.float32
    parts = x.reshape(4, 2, half, columns)

    def block(toward, which):
        return lax.dynamic_slice(
            parts, (lax.bitwise_xor(place, toward), which, 0, 0), (1, 1, half, columns)
        )[0, 0]

    sums = []
    for which, first, second in ((0, 1, 2), (1, 2, 1)):
        away = flip(jnp.stack([block(first, which), block(3, which)]), first).astype(wide)
        mine = block(0, which).astype(wide) + away[0]
        onward = (block(second, which).astype(wide) + away[1]).astype(low)
        sums.append(mine + flip(onward, second).astype(wide))
    return jnp.concatenate(sums, axis=0)


def exchange_plane(x):
    place = lax.axis_index("seq")
    arrived = [pick(x, place)] + [
        flip(pick(x, lax.bitwise_xor(place, bit)), bit) for bit in (1, 2, 3)
    ]
    stacked = jnp.stack(arrived)
    return jnp.stack([pick(stacked, lax.bitwise_xor(place, j)) for j in range(4)])


def sum_everywhere(x):
    x = x + swap_cores(x)
    x = x + flip(x, 1)
    x = x + flip(x, 2)
    peers = lax.axis_size("dp")
    step = 1
    while step < peers:
        x = x + lax.ppermute(x, "dp", [(i, i ^ step) for i in range(peers)])
        step *= 2
    return x


def with_halo(cells, width):
    count = lax.axis_size("seq")
    head, tail = cells[:width], cells[-width:]
    up = lax.ppermute(tail, "seq", [(i, i + 1) for i in range(count - 1)])
    down = lax.ppermute(head, "seq", [(i + 1, i) for i in range(count - 1)])
    return jnp.concatenate([up, cells, down], axis=0)


def spread_tracks(x):
    rows = x.shape[0]
    lower = lax.axis_index("species") == 0
    human = jnp.pad(x, ((0, 0), (0, 12 * BLOCK - x.shape[1]))).reshape(rows, 4, 3, BLOCK)
    human = human.transpose(1, 2, 0, 3)
    mouse = x[:, : 4 * BLOCK].reshape(rows, 4, BLOCK).transpose(1, 0, 2)
    other = to_upper_core(human[:, 2])
    first = jnp.where(lower, human[:, 0], other)
    second = jnp.where(lower, human[:, 1], mouse)
    return jnp.concatenate([first, second], axis=-1)


def collect_tracks(x, tracks):
    rows = x.shape[1]
    lower = lax.axis_index("species") == 0
    other = to_lower_core(x[:, :, :BLOCK])
    human = jnp.stack([x[:, :, :BLOCK], x[:, :, BLOCK:], other], axis=1)
    human = human.transpose(2, 0, 1, 3).reshape(rows, 12 * BLOCK)[:, :tracks]
    mouse = x[:, :, BLOCK:].transpose(1, 0, 2).reshape(rows, 4 * BLOCK)
    mouse = jnp.pad(mouse, ((0, 0), (0, tracks - 4 * BLOCK)))
    return jnp.where(lower, human, mouse)


def layer_norm(value_entries, gain, shift):
    centre = jnp.mean(value_entries, axis=-1, keepdims=True)
    centred = value_entries - centre
    spread = jnp.mean(centred * centred, axis=-1, keepdims=True)
    return centred * lax.rsqrt(spread + EPSILON) * gain + shift


def gelu_back(pre, upstream):
    _, back = jax.vjp(jax.nn.gelu, pre)
    return back(upstream)[0]


def dense(left, right):
    return jnp.dot(left, right, preferred_element_type=jnp.float32)


def dense_back(left, right):
    return lax.dot_general(
        left, right, (((1,), (1,)), ((), ())), preferred_element_type=jnp.float32
    )


def outer_sum(left, right):
    return lax.dot_general(
        left, right, (((0,), (0,)), ((), ())), preferred_element_type=jnp.float32
    )


def row_sum(value_entries):
    return jnp.sum(value_entries.astype(jnp.float32), axis=0)


def on_device(
    inputs,
    crop_start,
    rel_bucket,
    conv_weight,
    query_weight,
    key_weight,
    value_weight,
    out_weight,
    up_weight,
    down_weight,
    point_weight,
    rel_table,
    bn_gain,
    bn_shift,
    conv_bias,
    attn_gain,
    attn_shift,
    ffn_gain,
    ffn_shift,
    up_bias,
    down_bias,
    point_bias,
    head_weight,
    pred_grad,
):
    low = jnp.bfloat16
    wide = jnp.float32
    bin_count, chans = inputs.shape[2], inputs.shape[3]
    tracks = head_weight.shape[2]
    crop_rows = 4 * pred_grad.shape[2]
    seq_pos = lax.axis_index("seq")
    species_id = lax.axis_index("species")
    lower = species_id == 0
    dp_count = lax.axis_size("dp")
    device_count = 2 * dp_count * 4
    portion_index = lax.axis_index(EVERYWHERE)
    full_len = 4 * bin_count
    element_count = float(device_count * bin_count)
    half_width = WIDTH // 2

    value_entries = inputs[0, 0].astype(wide)
    small = (
        bn_gain, bn_shift, conv_bias, attn_gain, attn_shift, ffn_gain, ffn_shift, up_bias, down_bias,
        point_bias, rel_table,
    )

    def placed(x):
        whole = jnp.zeros((device_count * x.shape[0],), wide)
        return lax.dynamic_update_slice_in_dim(whole, x.astype(wide), portion_index * x.shape[0], 0)

    joined = jnp.concatenate(
        [jnp.sum(value_entries, axis=0), jnp.sum(value_entries * value_entries, axis=0)]
        + [placed(x) for x in small]
    )
    joined = sum_everywhere(joined.reshape(-1, 128)).reshape(-1)
    moment_one, moment_two = joined[:chans], joined[chans : 2 * chans]
    at = 2 * chans
    whole_small = []
    for x in small:
        size = device_count * x.shape[0]
        whole_small.append(joined[at : at + size])
        at += size
    (
        batchnorm_gain, batchnorm_shift, bias_conv, gain_attn, shift_attn, gain_ffn, shift_ffn, bias_up,
        bias_down, bias_point, table_flat,
    ) = whole_small

    chunk = chans // CONV_CHUNKS
    conv_parts = [
        gather_all(conv_weight[:, i * chunk : (i + 1) * chunk], *((2, 1) if i % 2 else (1, 2)), True)[0]
        for i in range(CONV_CHUNKS)
    ]
    w_query, w_key, w_value, w_out = gather_all(
        jnp.concatenate([query_weight, key_weight, value_weight, out_weight], axis=1),
        2,
        1,
        False,
        [x.shape[1] for x in (query_weight, key_weight, value_weight, out_weight)],
    )
    (w_up,) = gather_all(up_weight, 1, 2, False)
    (w_down,) = gather_all(down_weight, 2, 1, False)
    (w_point,) = gather_all(point_weight, 1, 2, False)
    spread = exchange_plane(
        spread_tracks(jnp.concatenate([head_weight[0], pred_grad[0, 0]], axis=0))
    )
    head_rows = head_weight.shape[1]
    w_head = lax.all_gather(spread[:, :head_rows], "dp").reshape(-1, 2 * BLOCK)
    track_grad = spread[:, head_rows:].reshape(crop_rows, 2 * BLOCK)

    channel_average = moment_one / element_count
    inverse_deviation = lax.rsqrt(
        moment_two / element_count - channel_average * channel_average + EPSILON
    )
    standardized_input = (value_entries - channel_average) * inverse_deviation
    normed_rows = standardized_input * batchnorm_gain + batchnorm_shift
    activity = jax.nn.gelu(normed_rows).astype(low)
    act_pad = with_halo(activity, half_width)
    act_taps = jnp.concatenate([act_pad[k : k + bin_count] for k in range(WIDTH)], axis=1)
    conv_out = bias_conv + jnp.concatenate([dense(act_taps, w) for w in conv_parts], axis=1)
    first_sum = value_entries + conv_out
    normed_one = layer_norm(first_sum, gain_attn, shift_attn).astype(low)
    scale = QK ** (-0.5)
    query_rows = (dense(normed_one, w_query).astype(low).astype(wide) * scale).astype(low)
    key_rows = dense(normed_one, w_key).astype(low)
    value_rows = dense(normed_one, w_value).astype(low)
    key_all = gather_plane(key_rows)
    value_all = gather_plane(value_rows)
    bucket_window = lax.dynamic_slice_in_dim(
        jnp.pad(rel_bucket, (1, 0), constant_values=-1),
        full_len - bin_count - seq_pos * bin_count,
        full_len + bin_count,
    )
    window_onehot = (bucket_window[:, None] == jnp.arange(NB)[None, :]).astype(wide)
    distance_bias = lax.dot_general(
        table_flat.reshape(HEADS, NB), window_onehot, (((1,), (1,)), ((), ())),
        precision=lax.Precision.HIGHEST, preferred_element_type=wide,
    ).reshape(HEADS // 2, 2, full_len + bin_count)
    mixed = attn_fwd(query_rows, key_all, value_all, distance_bias)
    second_sum = first_sum + dense(mixed, w_out)
    normed_two = layer_norm(second_sum, gain_ffn, shift_ffn).astype(low)
    up_pre = dense(normed_two, w_up) + bias_up
    up_act = jax.nn.gelu(up_pre).astype(low)
    third_sum = second_sum + dense(up_act, w_down) + bias_down
    third_all = gather_plane(third_sum.astype(low))
    crop_at = crop_start[0, 0]
    cropped = lax.dynamic_slice_in_dim(third_all, crop_at, crop_rows, 0)
    point_pre = dense(cropped, w_point) + bias_point
    point_act = jax.nn.gelu(point_pre).astype(low)

    human_act = jnp.where(lower, point_act, to_upper_core(point_act))
    column = jnp.arange(BLOCK)
    first_valid = 3 * BLOCK * seq_pos + jnp.where(lower, 0, 2 * BLOCK) + column < tracks
    second_valid = jnp.where(
        lower, 3 * BLOCK * seq_pos + BLOCK + column < tracks, BLOCK * seq_pos + column < TRK_M
    )
    preds, head_grads, logit_grads = [], [], []
    for which, act, valid in ((0, human_act, first_valid), (1, point_act, second_valid)):
        span = slice(which * BLOCK, (which + 1) * BLOCK)
        mask = valid.astype(wide)
        logits = dense(act, w_head[:, span])
        preds.append((jax.nn.softplus(logits) * mask).astype(low))
        logit_grad = (track_grad[:, span].astype(wide) * mask * jax.nn.sigmoid(logits)).astype(low)
        logit_grads.append(logit_grad)
        head_grads.append(outer_sum(act, logit_grad).astype(low))
    first_back = dense_back(logit_grads[0], w_head[:, :BLOCK])
    second_back = dense_back(logit_grads[1], w_head[:, BLOCK:])
    point_act_grad = second_back + jnp.where(
        lower, first_back + to_lower_core(first_back.astype(low)).astype(wide), 0.0
    )
    predictions = collect_tracks(
        exchange_plane(jnp.concatenate(preds, axis=1).reshape(4, crop_rows // 4, 2 * BLOCK)), tracks
    )

    point_grad = gelu_back(point_pre, point_act_grad).astype(low)
    crop_grad = dense_back(point_grad, w_point).astype(low)
    third_part = lax.dynamic_update_slice_in_dim(
        jnp.zeros((full_len, chans), low), crop_grad, crop_at, 0
    )
    third_grad = scatter_plane(third_part)
    grid_shape = (2, dp_count, 2, 2)

    def blocks(grad):
        return grad.astype(low).reshape(grid_shape + (grad.shape[0] // device_count, grad.shape[1]))

    head_sum = lax.psum_scatter(
        jnp.concatenate(head_grads, axis=1).reshape(dp_count, 4 * head_rows, 2 * BLOCK),
        "dp", scatter_dimension=0, tiled=False,
    )
    head_grad = collect_tracks(
        exchange_plane(head_sum.reshape(4, head_rows, 2 * BLOCK)), tracks
    ).astype(wide)
    grad_point_w = scatter_all(blocks(outer_sum(cropped, point_grad)), 1, 2, False)
    grad_point_b = row_sum(point_grad)
    down_grad = third_grad.astype(low)
    grad_down_w = scatter_all(blocks(outer_sum(up_act, down_grad)), 2, 1, False)
    grad_down_b = row_sum(down_grad)
    up_grad = gelu_back(up_pre, dense_back(down_grad, w_down)).astype(low)
    grad_up_w = scatter_all(blocks(outer_sum(normed_two, up_grad)), 1, 2, False)
    grad_up_b = row_sum(up_grad)
    _, norm_two_back = jax.vjp(layer_norm, second_sum, gain_ffn, shift_ffn)
    second_part, grad_ffn_gain, grad_ffn_shift = norm_two_back(dense_back(up_grad, w_up))
    second_grad = third_grad + second_part
    out_grad = second_grad.astype(low)
    grad_out_w = outer_sum(mixed, out_grad)
    mixed_grad = dense_back(out_grad, w_out).astype(low)
    query_low, key_part, value_part, distance_grad = attn_bwd(
        query_rows, key_all, value_all, distance_bias, mixed_grad
    )
    grad_table = jnp.dot(
        distance_grad.reshape(HEADS, -1), window_onehot, precision=lax.Precision.HIGHEST,
        preferred_element_type=wide,
    ).reshape(HEADS * NB)
    key_low = scatter_plane(key_part).astype(low)
    value_low = scatter_plane(value_part).astype(low)
    grad_qkvo = scatter_all(
        blocks(
            jnp.concatenate(
                [outer_sum(normed_one, x) for x in (query_low, key_low, value_low)] + [grad_out_w],
                axis=1,
            )
        ),
        2,
        1,
        False,
    )
    normed_one_grad = (
        dense_back(query_low, w_query) + dense_back(key_low, w_key) + dense_back(value_low, w_value)
    )
    _, norm_one_back = jax.vjp(layer_norm, first_sum, gain_attn, shift_attn)
    first_part, grad_attn_gain, grad_attn_shift = norm_one_back(normed_one_grad)
    first_grad = second_grad + first_part
    conv_grad = first_grad.astype(low)
    grad_conv_b = row_sum(conv_grad)
    grad_conv_w = jnp.concatenate(
        [
            scatter_all(
                blocks(outer_sum(act_taps, conv_grad[:, i * chunk : (i + 1) * chunk])),
                *((2, 1) if i % 2 else (1, 2)),
                True,
            )
            for i in range(CONV_CHUNKS)
        ],
        axis=1,
    )
    grad_pad = with_halo(conv_grad, half_width)
    act_grad = jnp.zeros((bin_count, chans), wide)
    for tap_index in range(WIDTH):
        begin = 2 * half_width - tap_index
        rows = grad_pad[begin : begin + bin_count]
        for i, w in enumerate(conv_parts):
            act_grad = act_grad + dense_back(
                rows[:, i * chunk : (i + 1) * chunk], w[tap_index * chans : (tap_index + 1) * chans]
            )
    normed_rows_gradient = gelu_back(normed_rows, act_grad)
    vectors = (
        jnp.sum(normed_rows_gradient * standardized_input, axis=0),
        jnp.sum(normed_rows_gradient, axis=0),
        grad_table,
        grad_conv_b,
        grad_attn_gain,
        grad_attn_shift,
        grad_ffn_gain,
        grad_ffn_shift,
        grad_up_b,
        grad_down_b,
        grad_point_b,
    )
    summed = sum_everywhere(jnp.concatenate(vectors).reshape(-1, 128)).reshape(-1)
    standardized_sum, plain_gradient_sum = summed[:chans], summed[chans : 2 * chans]
    input_grad = first_grad + batchnorm_gain * inverse_deviation * (
        normed_rows_gradient
        - plain_gradient_sum / element_count
        - standardized_input * standardized_sum / element_count
    )
    shares = []
    at = 0
    for x in vectors:
        size = x.shape[0] // device_count
        shares.append(lax.dynamic_slice_in_dim(summed, at + portion_index * size, size))
        at += x.shape[0]
    bn_gain_share, bn_shift_share, table_share, conv_b_share = shares[:4]
    attn_gain_share, attn_shift_share, ffn_gain_share, ffn_shift_share = shares[4:8]
    up_b_share, down_b_share, point_b_share = shares[8:]
    ends = [0]
    for x in (query_weight, key_weight, value_weight, out_weight):
        ends.append(ends[-1] + x.shape[1])
    query_share, key_share, value_share, out_share = (
        grad_qkvo[:, ends[i] : ends[i + 1]] for i in range(4)
    )
    return (
        predictions[None, None],
        input_grad[None, None],
        grad_conv_w,
        query_share,
        key_share,
        value_share,
        out_share,
        grad_up_w,
        grad_down_w,
        grad_point_w,
        table_share,
        bn_gain_share,
        bn_shift_share,
        conv_b_share,
        attn_gain_share,
        attn_shift_share,
        ffn_gain_share,
        ffn_shift_share,
        up_b_share,
        down_b_share,
        point_b_share,
        head_grad[None],
    )


def solution(mesh):
    everywhere = P(EVERYWHERE)
    rows = P(EVERYWHERE, None)
    bins = P("species", "dp", "seq", None)
    head = P("species", ("dp", "seq"), None)
    return jax.shard_map(
        on_device,
        mesh=mesh,
        in_specs=(bins, P("species", "dp"), P()) + (rows,) * 8 + (everywhere,) * 11 + (head, bins),
        out_specs=(bins, bins) + (rows,) * 8 + (everywhere,) * 11 + (head,),
        check_vma=False,
    )
```

profile of v0, /device:TPU:0, one launch (start us, length us, event | category | flops | bytes accessed | tf_op | source)
XLA Modules:
  0.0 1711.6 jit_solution(14740405913073614254)
XLA Ops:
  65.9 15.6 collective-permute-done.8
  96.2 18.8 %collective-permute-start.3 = (f32[170,128]{1,0:T(8,128)S(1)}, f32[170,128]{1,0:T(8,128)S(1)}, u32[]{:S(2)}, u32[]{:S(2)}) collective-permute-start(f32[170,128]{1,0:T(8,128)S(1)} %add.730), channel_id=1, source_target_pairs={{0,4},{4,0},{8,12},{12,8},{1,5},{5,1},{9,13},{13,9},{2,6},{6,2},{1... | collective-permute-start | bytes 261128 | tf_op jit(solution)/shard_map/ppermute | solution.py:326
  138.0 10.6 collective-permute-done.10
  159.3 8.8 collective-permute-done.5
  192.4 49.1 %collective-permute-done.40 = bf16[4,48,3072]{2,1,0:T(8,128)(2,1)} collective-permute-done((bf16[4,48,3072]{2,1,0:T(8,128)(2,1)}, bf16[4,48,3072]{2,1,0:T(8,128)(2,1)}, u32[]{:S(2)}, u32[]{:S(2)}) %collective-permute-start.40) | collective-permute-done | bytes 1179680 | tf_op jit(solution)/shard_map/ppermute | solution.py:135
  241.4 8.8 collective-permute-done.44
  276.3 13.4 sort_copies.10
  294.9 13.4 sort_copies.11
  329.8 17.8 %sort_copies.12 = bf16[2,4,4,240,512]{4,3,2,1,0:T(8,128)(2,1)S(1)} custom-call(bf16[2,4,240,512]{3,2,1,0:T(8,128)(2,1)} %pad_maximum_fusion.12.refs_0_, bf16[2,4,240,512]{3,2,1,0:T(8,128)(2,1)} %collective-permute-done.25.refs_1_, bf16[2,4,240,512]{3,2,1,0:T(8,128)(2,1)S(1)} %collective-permute-done.26.refs_2_, ...), custom_call_target="tpu_custom_call" | custom-call | bytes 15728640 | tf_op jit(solution)/shard_map/sort_copies/pallas_call | solution.py:177
  375.3 25.7 %collective-permute-done.59 = bf16[416,1024]{1,0:T(8,128)(2,1)} collective-permute-done((bf16[416,1024]{1,0:T(8,128)(2,1)}, bf16[416,1024]{1,0:T(8,128)(2,1)}, u32[]{:S(2)}, u32[]{:S(2)}) %collective-permute-start.59) | collective-permute-done | bytes 852000 | tf_op jit(solution)/shard_map/ppermute | solution.py:135
  401.4 58.5 %collective-permute-done.60 = bf16[416,1024]{1,0:T(8,128)(2,1)S(1)} collective-permute-done((bf16[416,1024]{1,0:T(8,128)(2,1)S(1)}, bf16[416,1024]{1,0:T(8,128)(2,1)S(1)}, u32[]{:S(2)}, u32[]{:S(2)}) %collective-permute-start.60) | collective-permute-done | bytes 852000 | tf_op jit(solution)/shard_map/ppermute | solution.py:135
  464.5 22.8 %collective-permute-done.37.refs_2_ = bf16[384,1536]{1,0:T(8,128)(2,1)} collective-permute-done((bf16[384,1536]{1,0:T(8,128)(2,1)}, bf16[384,1536]{1,0:T(8,128)(2,1)}, u32[]{:S(2)}, u32[]{:S(2)}) %collective-permute-start.37) | collective-permute-done | bytes 1179680 | tf_op jit(solution)/shard_map/ppermute | solution.py:135
  526.5 23.4 %collective-permute-done.33.refs_2_ = bf16[384,512]{1,0:T(8,128)(2,1)S(1)} collective-permute-done((bf16[384,512]{1,0:T(8,128)(2,1)S(1)}, bf16[384,512]{1,0:T(8,128)(2,1)S(1)}, u32[]{:S(2)}, u32[]{:S(2)}) %collective-permute-start.33) | collective-permute-done | bytes 393248 | tf_op jit(solution)/shard_map/ppermute | solution.py:135
  552.2 11.8 collective-permute-done.34.refs_3_
  572.3 12.5 attention_forward.1
  615.0 18.3 %collective-permute-done.48.refs_1_ = bf16[384,1536]{1,0:T(8,128)(2,1)S(1)} collective-permute-done((bf16[384,1536]{1,0:T(8,128)(2,1)}, bf16[384,1536]{1,0:T(8,128)(2,1)S(1)}, u32[]{:S(2)}, u32[]{:S(2)}) %collective-permute-start.48) | collective-permute-done | bytes 1179680 | tf_op jit(solution)/shard_map/ppermute | solution.py:135
  655.3 13.8 multiply_convert_fusion
  680.4 47.3 %all-gather.19.cloned.1.call-done = bf16[16,192,1024]{2,1,0:T(8,128)(2,1)} async-done(((bf16[4,192,1024]{2,1,0:T(8,128)(2,1)}), bf16[16,192,1024]{2,1,0:T(8,128)(2,1)}) %all-gather.19.cloned.1.call-update) | async-done | bytes 6291472 | tf_op jit(solution)/shard_map/all_gather | solution.py:481
  735.8 8.0 fusion.277
  746.7 8.9 fusion.101
  773.6 8.3 collective-permute-done.63
  785.9 19.4 %convert_reduce_fusion = (f32[3072]{0:T(1024)}, bf16[896,3072]{1,0:T(8,128)(2,1)}) fusion(f32[896,3072]{1,0:T(8,128)} %get-tuple-element.248, f32[3072]{0:T(1024)S(1)} %copy-done.146, f32[896,3072]{1,0:T(8,128)} %get-tuple-element.250, bf16[896,3072]{1,0:T(8,128)(2,1)} %collective-permute-done.65, pred[]{:T(512)S(6)} %eq.8, ...), kind=kOutput, calls=%fused_computation.18 | convolution fusion | flops 2896098304 | bytes 38955008 | tf_op jit(solution)/shard_map/dot_general | solution.py:379
  805.3 14.2 convolution_convert_fusion.10
  821.9 12.7 dynamic_update_slice.47
  849.6 8.6 copy.190
  876.8 16.9 collective-permute-done.68
  895.2 11.0 collective-permute-done.67
  909.3 15.4 convolution_convert_fusion.3
  926.1 8.9 convert_reduce_fusion.1
  935.0 11.0 convolution_convert_fusion.4
  960.2 11.8 constant_dynamic-slice_fusion.6
  982.3 28.9 %attention_backward.1 = (bf16[384,512]{1,0:T(8,128)(2,1)}, bf16[1536,512]{1,0:T(8,128)(2,1)}, bf16[1536,1536]{1,0:T(8,128)(2,1)}, f32[4,2,1920]{2,1,0:T(2,128)}) custom-call(bf16[384,512]{1,0:T(8,128)(2,1)} %fusion.133.q_ref, bf16[1536,512]{1,0:T(8,128)(2,1)} %bitcast.646, bf16[1536,1536]{1,0:T(8,128)(2,1)} %bitcast.620, f32[4,2,1920]{2,1,0:T(2,128)} %fusion.220.u_ref, ...), custom_call_target="tpu_custom_call" | custom-call | tf_op jit(solution)/shard_map/attention_backward/pallas_call | solution.py:121
  1024.3 26.5 %collective-permute-done.70 = bf16[2,192,512]{2,1,0:T(8,128)(2,1)S(1)} collective-permute-done((bf16[2,192,512]{2,1,0:T(8,128)(2,1)S(1)}, bf16[2,192,512]{2,1,0:T(8,128)(2,1)S(1)}, u32[]{:S(2)}, u32[]{:S(2)}) %collective-permute-start.70) | collective-permute-done | bytes 393248 | tf_op jit(solution)/shard_map/ppermute | solution.py:135
  1058.3 8.5 constant_dynamic-slice_fusion.8
  1088.9 11.7 collective-permute-done.77
  1113.9 9.2 convolution_convert_fusion.2
  1123.0 9.4 convolution_convert_fusion.1
  1132.4 9.2 convolution_convert_fusion
  1226.0 9.7 constant_dynamic-slice_fusion.12
  1309.1 23.6 %collective-permute-done.110 = bf16[4,2,96,1536]{3,2,0,1:T(8,128)(2,1)} collective-permute-done((bf16[4,2,96,1536]{3,2,0,1:T(8,128)(2,1)}, bf16[4,2,96,1536]{3,2,0,1:T(8,128)(2,1)}, u32[]{:S(2)}, u32[]{:S(2)}) %collective-permute-start.110) | collective-permute-done | bytes 2359328 | tf_op jit(solution)/shard_map/ppermute | solution.py:135
  1345.5 45.8 %collective-permute-done.107 = bf16[4,2,48,3072]{3,2,0,1:T(8,128)(2,1)S(1)} collective-permute-done((bf16[4,2,48,3072]{3,2,0,1:T(8,128)(2,1)}, bf16[4,2,48,3072]{3,2,0,1:T(8,128)(2,1)S(1)}, u32[]{:S(2)}, u32[]{:S(2)}) %collective-permute-start.107) | collective-permute-done | bytes 2359328 | tf_op jit(solution)/shard_map/ppermute | solution.py:135
  1396.8 61.8 %collective-permute-done.111 = bf16[4,96,1536]{2,1,0:T(8,128)(2,1)S(1)} collective-permute-done((bf16[4,96,1536]{2,1,0:T(8,128)(2,1)S(1)}, bf16[4,96,1536]{2,1,0:T(8,128)(2,1)S(1)}, u32[]{:S(2)}, u32[]{:S(2)}) %collective-permute-start.111) | collective-permute-done | bytes 1179680 | tf_op jit(solution)/shard_map/ppermute | solution.py:135
  1473.4 14.5 collective-permute-done.114
  1511.1 69.3 %collective-permute-done.108 = bf16[4,48,3072]{2,1,0:T(8,128)(2,1)S(1)} collective-permute-done((bf16[4,48,3072]{2,1,0:T(8,128)(2,1)S(1)}, bf16[4,48,3072]{2,1,0:T(8,128)(2,1)S(1)}, u32[]{:S(2)}, u32[]{:S(2)}) %collective-permute-start.108) | collective-permute-done | bytes 1179680 | tf_op jit(solution)/shard_map/ppermute | solution.py:135
  1612.0 9.6 collective-permute-done.105
  1633.2 18.1 %collective-permute-start.101 = (bf16[240,512]{1,0:T(8,128)(2,1)S(1)}, bf16[240,512]{1,0:T(8,128)(2,1)S(1)}, u32[]{:S(2)}, u32[]{:S(2)}) collective-permute-start(bf16[240,512]{1,0:T(8,128)(2,1)S(1)} %get-tuple-element.203), channel_id=1, source_target_pairs={{0,8},{4,12},{8,0},{12,4},{1,9},{5,13},{9,1},{13,5},{2,10},{6,14},... | collective-permute-start | bytes 737288 | tf_op jit(solution)/shard_map/ppermute | solution.py:256
  1656.1 24.0 %collective-permute-done.95 = bf16[240,512]{1,0:T(8,128)(2,1)S(1)} collective-permute-done((bf16[240,512]{1,0:T(8,128)(2,1)}, bf16[240,512]{1,0:T(8,128)(2,1)S(1)}, u32[]{:S(2)}, u32[]{:S(2)}) %collective-permute-start.95) | collective-permute-done | bytes 245792 | tf_op jit(solution)/shard_map/ppermute | solution.py:256
  1681.4 13.5 collective-permute-done.101
  (962 shorter events, 754.3 us)
Async XLA Ops:
  7.3 128.0 %all-gather.11.cloned.1.call-start = ((), (), s32[]{:S(2)}) async-start(), calls=%async_computation.10 | async-start | bytes 1966080 | tf_op jit(solution)/shard_map/all_gather | solution.py:201
  9.2 171.0 %all-gather.13.cloned.1.call-start = ((), (), s32[]{:S(2)}) async-start(), calls=%async_computation.11 | async-start | bytes 1474560 | tf_op jit(solution)/shard_map/all_gather | solution.py:201
  10.0 170.7 %all-gather.15.cloned.1.call-start = ((), (), s32[]{:S(2)}) async-start(), calls=%async_computation.12 | async-start | bytes 1474560 | tf_op jit(solution)/shard_map/all_gather | solution.py:201
  10.7 351.2 %all-gather.17.cloned.1.call-start = ((), (), s32[]{:S(2)}) async-start(), calls=%async_computation.13 | async-start | bytes 1474560 | tf_op jit(solution)/shard_map/all_gather | solution.py:201
  39.8 687.9 %all-gather.19.cloned.1.call-start = ((), (), s32[]{:S(2)}) async-start(), calls=%async_computation.14 | async-start | bytes 7864320 | tf_op jit(solution)/shard_map/all_gather | solution.py:481
  92.9 87.3 %collective-permute-start.57 = (bf16[4,416,512]{2,1,0:T(8,128)(2,1)}, bf16[4,416,512]{2,1,0:T(8,128)(2,1)}, u32[]{:S(2)}, u32[]{:S(2)}) collective-permute-start(bf16[4,416,512]{2,1,0:T(8,128)(2,1)} %copy.149), channel_id=1, source_target_pairs={{0,16},{1,17},{2,18},{3,19},{4,20},{5,21},{6,22},{7,23},{8,24},{9,... | collective-permute-start | bytes 5111816 | tf_op jit(solution)/shard_map/ppermute | solution.py:143
  168.1 83.8 %collective-permute-start.11 = (bf16[2,4,240,512]{3,2,1,0:T(8,128)(2,1)}, bf16[2,4,240,512]{3,2,1,0:T(8,128)(2,1)}, u32[]{:S(2)}, u32[]{:S(2)}) collective-permute-start(bf16[2,4,240,512]{3,2,1,0:T(8,128)(2,1)} %pad_maximum_fusion.10.refs_0_), channel_id=1, source_target_pairs={{0,2},{1,3},{2,0},{3,1},{4,6},{5,7},{6,4},{7,5},{8,10},{9,11},{10,... | collective-permute-start | bytes 5898248 | tf_op jit(solution)/shard_map/ppermute | solution.py:135
  170.6 81.8 %collective-permute-start.12 = (bf16[2,4,240,512]{3,2,1,0:T(8,128)(2,1)}, bf16[2,4,240,512]{3,2,1,0:T(8,128)(2,1)}, u32[]{:S(2)}, u32[]{:S(2)}) collective-permute-start(bf16[2,4,240,512]{3,2,1,0:T(8,128)(2,1)} %pad_maximum_fusion.10.refs_0_), channel_id=1, source_target_pairs={{0,16},{16,0},{1,17},{17,1},{2,18},{18,2},{3,19},{19,3},{4,20},{20... | collective-permute-start | bytes 5898248 | tf_op jit(solution)/shard_map/ppermute | solution.py:139
  170.6 81.3 %collective-permute-start.18 = (bf16[2,4,240,512]{3,2,1,0:T(8,128)(2,1)}, bf16[2,4,240,512]{3,2,1,0:T(8,128)(2,1)}, u32[]{:S(2)}, u32[]{:S(2)}) collective-permute-start(bf16[2,4,240,512]{3,2,1,0:T(8,128)(2,1)} %pad_maximum_fusion.11.refs_0_), channel_id=1, source_target_pairs={{0,1},{1,0},{2,3},{3,2},{4,5},{5,4},{6,7},{7,6},{8,9},{9,8},{10,11... | collective-permute-start | bytes 5898248 | tf_op jit(solution)/shard_map/ppermute | solution.py:135
  180.2 61.2 %collective-permute-start.40 = (bf16[4,48,3072]{2,1,0:T(8,128)(2,1)}, bf16[4,48,3072]{2,1,0:T(8,128)(2,1)}, u32[]{:S(2)}, u32[]{:S(2)}) collective-permute-start(bf16[4,48,3072]{2,1,0:T(8,128)(2,1)} %bitcast.734), channel_id=1, source_target_pairs={{0,1},{1,0},{2,3},{3,2},{4,5},{5,4},{6,7},{7,6},{8,9},{9,8},{10,11... | collective-permute-start | bytes 3538952 | tf_op jit(solution)/shard_map/ppermute | solution.py:135
  184.0 66.3 %collective-permute-start.44 = (bf16[4,96,1536]{2,1,0:T(8,128)(2,1)}, bf16[4,96,1536]{2,1,0:T(8,128)(2,1)S(1)}, u32[]{:S(2)}, u32[]{:S(2)}) collective-permute-start(bf16[4,96,1536]{2,1,0:T(8,128)(2,1)} %bitcast.738), channel_id=1, source_target_pairs={{0,2},{1,3},{2,0},{3,1},{4,6},{5,7},{6,4},{7,5},{8,10},{9,11},{10,... | collective-permute-start | bytes 3538952 | tf_op jit(solution)/shard_map/ppermute | solution.py:135
  252.4 71.1 %collective-permute-start.29 = (bf16[2,4,48,4096]{3,2,1,0:T(8,128)(2,1)S(1)}, bf16[2,4,48,4096]{3,2,1,0:T(8,128)(2,1)}, u32[]{:S(2)}, u32[]{:S(2)}) collective-permute-start(bf16[2,4,48,4096]{3,2,1,0:T(8,128)(2,1)S(1)} %pad_maximum_fusion.5.refs_0_), channel_id=1, source_target_pairs={{0,1},{1,0},{2,3},{3,2},{4,5},{5,4},{6,7},{7,6},{8,9},{9,8},{10,11... | collective-permute-start | bytes 9437192 | tf_op jit(solution)/shard_map/ppermute | solution.py:135
  289.7 84.7 %collective-permute-start.58 = (bf16[416,1024]{1,0:T(8,128)(2,1)}, bf16[416,1024]{1,0:T(8,128)(2,1)}, u32[]{:S(2)}, u32[]{:S(2)}) collective-permute-start(bf16[416,1024]{1,0:T(8,128)(2,1)} %bitcast.73), channel_id=1, source_target_pairs={{0,1},{1,0},{2,3},{3,2},{4,5},{5,4},{6,7},{7,6},{8,9},{9,8},{10,11... | collective-permute-start | bytes 2555912 | tf_op jit(solution)/shard_map/ppermute | solution.py:135
  294.4 61.8 %collective-permute-start.30 = (bf16[2,4,48,4096]{3,2,1,0:T(8,128)(2,1)S(1)}, bf16[2,4,48,4096]{3,2,1,0:T(8,128)(2,1)S(1)}, u32[]{:S(2)}, u32[]{:S(2)}) collective-permute-start(bf16[2,4,48,4096]{3,2,1,0:T(8,128)(2,1)S(1)} %pad_maximum_fusion.5.refs_0_), channel_id=1, source_target_pairs={{0,16},{16,0},{1,17},{17,1},{2,18},{18,2},{3,19},{19,3},{4,20},{20... | collective-permute-start | bytes 9437192 | tf_op jit(solution)/shard_map/ppermute | solution.py:139
  328.7 132.9 %collective-permute-start.41 = (bf16[2,4,48,3072]{3,2,1,0:T(8,128)(2,1)}, bf16[2,4,48,3072]{3,2,1,0:T(8,128)(2,1)}, u32[]{:S(2)}, u32[]{:S(2)}) collective-permute-start(bf16[2,4,48,3072]{3,2,1,0:T(8,128)(2,1)} %pad_maximum_fusion.6.refs_0_), channel_id=1, source_target_pairs={{0,2},{1,3},{2,0},{3,1},{4,6},{5,7},{6,4},{7,5},{8,10},{9,11},{10,... | collective-permute-start | bytes 7077896 | tf_op jit(solution)/shard_map/ppermute | solution.py:135
  329.3 132.8 %collective-permute-start.45 = (bf16[2,4,96,1536]{3,2,1,0:T(8,128)(2,1)}, bf16[2,4,96,1536]{3,2,1,0:T(8,128)(2,1)}, u32[]{:S(2)}, u32[]{:S(2)}) collective-permute-start(bf16[2,4,96,1536]{3,2,1,0:T(8,128)(2,1)} %pad_maximum_fusion.7.refs_0_), channel_id=1, source_target_pairs={{0,1},{1,0},{2,3},{3,2},{4,5},{5,4},{6,7},{7,6},{8,9},{9,8},{10,11... | collective-permute-start | bytes 7077896 | tf_op jit(solution)/shard_map/ppermute | solution.py:135
  361.9 99.6 %collective-permute-start.52 = (bf16[4,48,3072]{2,1,0:T(8,128)(2,1)}, bf16[4,48,3072]{2,1,0:T(8,128)(2,1)}, u32[]{:S(2)}, u32[]{:S(2)}) collective-permute-start(bf16[4,48,3072]{2,1,0:T(8,128)(2,1)} %bitcast.736), channel_id=1, source_target_pairs={{0,1},{1,0},{2,3},{3,2},{4,5},{5,4},{6,7},{7,6},{8,9},{9,8},{10,11... | collective-permute-start | bytes 3538952 | tf_op jit(solution)/shard_map/ppermute | solution.py:135
  374.4 87.8 %collective-permute-start.36 = (bf16[384,1536]{1,0:T(8,128)(2,1)}, bf16[384,1536]{1,0:T(8,128)(2,1)S(1)}, u32[]{:S(2)}, u32[]{:S(2)}) collective-permute-start(bf16[384,1536]{1,0:T(8,128)(2,1)} %convolution_convert_fusion.12.refs_0_), channel_id=1, source_target_pairs={{0,1},{1,0},{2,3},{3,2},{4,5},{5,4},{6,7},{7,6},{8,9},{9,8},{10,11... | collective-permute-start | bytes 3538952 | tf_op jit(solution)/shard_map/ppermute | solution.py:135
  487.3 64.9 %collective-permute-start.53 = (bf16[2,4,48,3072]{3,2,1,0:T(8,128)(2,1)S(1)}, bf16[2,4,48,3072]{3,2,1,0:T(8,128)(2,1)}, u32[]{:S(2)}, u32[]{:S(2)}) collective-permute-start(bf16[2,4,48,3072]{3,2,1,0:T(8,128)(2,1)S(1)} %pad_maximum_fusion.8.refs_0_), channel_id=1, source_target_pairs={{0,2},{1,3},{2,0},{3,1},{4,6},{5,7},{6,4},{7,5},{8,10},{9,11},{10,... | collective-permute-start | bytes 7077896 | tf_op jit(solution)/shard_map/ppermute | solution.py:135
  505.2 61.1 %collective-permute-start.38 = (bf16[192,1536]{1,0:T(8,128)(2,1)S(1)}, bf16[192,1536]{1,0:T(8,128)(2,1)S(1)}, u32[]{:S(2)}, u32[]{:S(2)}) collective-permute-start(bf16[192,1536]{1,0:T(8,128)(2,1)S(1)} %slice.439), channel_id=1, source_target_pairs={{0,2},{1,3},{2,0},{3,1},{4,6},{5,7},{6,4},{7,5},{8,10},{9,11},{10,... | collective-permute-start | bytes 1769480 | tf_op jit(solution)/shard_map/ppermute | solution.py:135
  506.6 59.6 %collective-permute-start.39 = (bf16[192,1536]{1,0:T(8,128)(2,1)S(1)}, bf16[192,1536]{1,0:T(8,128)(2,1)S(1)}, u32[]{:S(2)}, u32[]{:S(2)}) collective-permute-start(bf16[192,1536]{1,0:T(8,128)(2,1)S(1)} %slice.440), channel_id=1, source_target_pairs={{0,1},{1,0},{2,3},{3,2},{4,5},{5,4},{6,7},{7,6},{8,9},{9,8},{10,11... | collective-permute-start | bytes 1769480 | tf_op jit(solution)/shard_map/ppermute | solution.py:135
  552.2 86.7 %collective-permute-start.54 = (bf16[2,4,48,3072]{3,2,1,0:T(8,128)(2,1)S(1)}, bf16[2,4,48,3072]{3,2,1,0:T(8,128)(2,1)}, u32[]{:S(2)}, u32[]{:S(2)}) collective-permute-start(bf16[2,4,48,3072]{3,2,1,0:T(8,128)(2,1)S(1)} %pad_maximum_fusion.8.refs_0_), channel_id=1, source_target_pairs={{0,16},{16,0},{1,17},{17,1},{2,18},{18,2},{3,19},{19,3},{4,20},{20... | collective-permute-start | bytes 7077896 | tf_op jit(solution)/shard_map/ppermute | solution.py:139
  564.0 74.9 %collective-permute-start.55 = (bf16[2,4,48,3072]{3,2,1,0:T(8,128)(2,1)}, bf16[2,4,48,3072]{3,2,1,0:T(8,128)(2,1)}, u32[]{:S(2)}, u32[]{:S(2)}) collective-permute-start(bf16[2,4,48,3072]{3,2,1,0:T(8,128)(2,1)} %collective-permute-done.53.refs_1_), channel_id=1, source_target_pairs={{0,16},{16,0},{1,17},{17,1},{2,18},{18,2},{3,19},{19,3},{4,20},{20... | collective-permute-start | bytes 7077896 | tf_op jit(solution)/shard_map/ppermute | solution.py:139
  614.9 643.6 %reduce-scatter.14.cloned.1.call-start = ((), (), s32[]{:S(2)}) async-start(), calls=%async_computation.9 | async-start | bytes 7864320 | tf_op jit(solution)/shard_map/reduce_scatter | solution.py:559
  784.2 75.4 %collective-permute-start.64 = (bf16[4,224,512]{2,1,0:T(8,128)(2,1)}, bf16[4,224,512]{2,1,0:T(8,128)(2,1)}, u32[]{:S(2)}, u32[]{:S(2)}) collective-permute-start(bf16[4,224,512]{2,1,0:T(8,128)(2,1)} %get-tuple-element.164), channel_id=1, source_target_pairs={{16,0},{17,1},{18,2},{19,3},{20,4},{21,5},{22,6},{23,7},{24,8},{25... | collective-permute-start | bytes 2752520 | tf_op jit(solution)/shard_map/ppermute | solution.py:147
  858.2 838.0 %reduce-scatter.10.cloned.1.call-start = ((), (), s32[]{:S(2)}) async-start(), calls=%async_computation.7 | async-start | bytes 1474560 | tf_op jit(solution)/shard_map/reduce_scatter | solution.py:260
  974.5 270.2 %collective-permute-start.112 = (bf16[4,2,2,48,3072]{4,3,0,1,2:T(8,128)(2,1)}, bf16[4,2,2,48,3072]{4,3,0,1,2:T(8,128)(2,1)}, u32[]{:S(2)}, u32[]{:S(2)}) collective-permute-start(bf16[4,2,2,48,3072]{4,3,0,1,2:T(8,128)(2,1)} %bitcast.610), channel_id=1, source_target_pairs={{0,16},{16,0},{1,17},{17,1},{2,18},{18,2},{3,19},{19,3},{4,20},{20... | collective-permute-start | bytes 14155784 | tf_op jit(solution)/shard_map/ppermute | solution.py:139
  1016.6 59.1 %collective-permute-start.72 = (bf16[2,192,512]{2,1,0:T(8,128)(2,1)S(1)}, bf16[2,192,512]{2,1,0:T(8,128)(2,1)}, u32[]{:S(2)}, u32[]{:S(2)}) collective-permute-start(bf16[2,192,512]{2,1,0:T(8,128)(2,1)S(1)} %pad_maximum_fusion.37), channel_id=1, source_target_pairs={{0,2},{1,3},{2,0},{3,1},{4,6},{5,7},{6,4},{7,5},{8,10},{9,11},{10,... | collective-permute-start | bytes 1179656 | tf_op jit(solution)/shard_map/ppermute | solution.py:135
  1018.6 60.2 %collective-permute-start.76 = (bf16[2,192,1536]{2,1,0:T(8,128)(2,1)}, bf16[2,192,1536]{2,1,0:T(8,128)(2,1)}, u32[]{:S(2)}, u32[]{:S(2)}) collective-permute-start(bf16[2,192,1536]{2,1,0:T(8,128)(2,1)} %pad_maximum_fusion.24), channel_id=1, source_target_pairs={{0,2},{1,3},{2,0},{3,1},{4,6},{5,7},{6,4},{7,5},{8,10},{9,11},{10,... | collective-permute-start | bytes 3538952 | tf_op jit(solution)/shard_map/ppermute | solution.py:135
  1075.8 185.2 %collective-permute-start.109 = (bf16[4,2,2,96,1536]{4,3,0,2,1:T(8,128)(2,1)}, bf16[4,2,2,96,1536]{4,3,0,2,1:T(8,128)(2,1)}, u32[]{:S(2)}, u32[]{:S(2)}) collective-permute-start(bf16[4,2,2,96,1536]{4,3,0,2,1:T(8,128)(2,1)} %bitcast.711), channel_id=1, source_target_pairs={{0,16},{16,0},{1,17},{17,1},{2,18},{18,2},{3,19},{19,3},{4,20},{20... | collective-permute-start | bytes 14155784 | tf_op jit(solution)/shard_map/ppermute | solution.py:139
  1076.9 175.1 %collective-permute-start.106 = (bf16[4,2,2,48,3072]{4,3,0,1,2:T(8,128)(2,1)}, bf16[4,2,2,48,3072]{4,3,0,1,2:T(8,128)(2,1)}, u32[]{:S(2)}, u32[]{:S(2)}) collective-permute-start(bf16[4,2,2,48,3072]{4,3,0,1,2:T(8,128)(2,1)} %bitcast.712), channel_id=1, source_target_pairs={{0,16},{16,0},{1,17},{17,1},{2,18},{18,2},{3,19},{19,3},{4,20},{20... | collective-permute-start | bytes 14155784 | tf_op jit(solution)/shard_map/ppermute | solution.py:139
  1224.8 71.2 %collective-permute-start.85 = (bf16[4,2,2,240,512]{4,3,0,1,2:T(8,128)(2,1)}, bf16[4,2,2,240,512]{4,3,0,1,2:T(8,128)(2,1)}, u32[]{:S(2)}, u32[]{:S(2)}) collective-permute-start(bf16[4,2,2,240,512]{4,3,0,1,2:T(8,128)(2,1)} %bitcast.615), channel_id=1, source_target_pairs={{0,16},{16,0},{1,17},{17,1},{2,18},{18,2},{3,19},{19,3},{4,20},{20... | collective-permute-start | bytes 11796488 | tf_op jit(solution)/shard_map/ppermute | solution.py:139
  1240.2 62.1 %collective-permute-start.91 = (bf16[4,2,2,240,512]{4,3,0,2,1:T(8,128)(2,1)}, bf16[4,2,2,240,512]{4,3,0,2,1:T(8,128)(2,1)}, u32[]{:S(2)}, u32[]{:S(2)}) collective-permute-start(bf16[4,2,2,240,512]{4,3,0,2,1:T(8,128)(2,1)} %bitcast.614), channel_id=1, source_target_pairs={{0,16},{16,0},{1,17},{17,1},{2,18},{18,2},{3,19},{19,3},{4,20},{20... | collective-permute-start | bytes 11796488 | tf_op jit(solution)/shard_map/ppermute | solution.py:139
  1272.4 189.8 %collective-permute-start.103 = (bf16[4,2,2,48,4096]{4,3,2,1,0:T(8,128)(2,1)}, bf16[4,2,2,48,4096]{4,3,2,1,0:T(8,128)(2,1)}, u32[]{:S(2)}, u32[]{:S(2)}) collective-permute-start(bf16[4,2,2,48,4096]{4,3,2,1,0:T(8,128)(2,1)} %dynamic-slice_bitcast_fusion), channel_id=1, source_target_pairs={{0,16},{16,0},{1,17},{17,1},{2,18},{18,2},{3,19},{19,3},{4,20},{20... | collective-permute-start | bytes 18874376 | tf_op jit(solution)/shard_map/ppermute | solution.py:139
  1296.0 95.3 %collective-permute-start.107 = (bf16[4,2,48,3072]{3,2,0,1:T(8,128)(2,1)}, bf16[4,2,48,3072]{3,2,0,1:T(8,128)(2,1)S(1)}, u32[]{:S(2)}, u32[]{:S(2)}) collective-permute-start(bf16[4,2,48,3072]{3,2,0,1:T(8,128)(2,1)} %dynamic-slice_bitcast_fusion.4), channel_id=1, source_target_pairs={{0,1},{1,0},{2,3},{3,2},{4,5},{5,4},{6,7},{7,6},{8,9},{9,8},{10,11... | collective-permute-start | bytes 7077896 | tf_op jit(solution)/shard_map/ppermute | solution.py:135
  1302.3 190.8 %collective-permute-start.97 = (bf16[4,2,2,240,512]{4,3,0,1,2:T(8,128)(2,1)}, bf16[4,2,2,240,512]{4,3,0,1,2:T(8,128)(2,1)}, u32[]{:S(2)}, u32[]{:S(2)}) collective-permute-start(bf16[4,2,2,240,512]{4,3,0,1,2:T(8,128)(2,1)} %bitcast.613), channel_id=1, source_target_pairs={{0,16},{16,0},{1,17},{17,1},{2,18},{18,2},{3,19},{19,3},{4,20},{20... | collective-permute-start | bytes 11796488 | tf_op jit(solution)/shard_map/ppermute | solution.py:139
  1332.6 168.3 %collective-permute-start.86 = (bf16[4,2,240,512]{3,2,0,1:T(8,128)(2,1)}, bf16[4,2,240,512]{3,2,0,1:T(8,128)(2,1)}, u32[]{:S(2)}, u32[]{:S(2)}) collective-permute-start(bf16[4,2,240,512]{3,2,0,1:T(8,128)(2,1)} %dynamic-slice_bitcast_fusion.7), channel_id=1, source_target_pairs={{0,1},{1,0},{2,3},{3,2},{4,5},{5,4},{6,7},{7,6},{8,9},{9,8},{10,11... | collective-permute-start | bytes 5898248 | tf_op jit(solution)/shard_map/ppermute | solution.py:135
  1340.8 117.9 %collective-permute-start.111 = (bf16[4,96,1536]{2,1,0:T(8,128)(2,1)S(1)}, bf16[4,96,1536]{2,1,0:T(8,128)(2,1)S(1)}, u32[]{:S(2)}, u32[]{:S(2)}) collective-permute-start(bf16[4,96,1536]{2,1,0:T(8,128)(2,1)S(1)} %dynamic-slice_bitcast_fusion.10), channel_id=1, source_target_pairs={{0,1},{1,0},{2,3},{3,2},{4,5},{5,4},{6,7},{7,6},{8,9},{9,8},{10,11... | collective-permute-start | bytes 3538952 | tf_op jit(solution)/shard_map/ppermute | solution.py:135
  1391.2 113.2 %collective-permute-start.92 = (bf16[4,2,240,512]{3,2,0,1:T(8,128)(2,1)}, bf16[4,2,240,512]{3,2,0,1:T(8,128)(2,1)}, u32[]{:S(2)}, u32[]{:S(2)}) collective-permute-start(bf16[4,2,240,512]{3,2,0,1:T(8,128)(2,1)} %dynamic-slice_bitcast_fusion.6), channel_id=1, source_target_pairs={{0,2},{1,3},{2,0},{3,1},{4,6},{5,7},{6,4},{7,5},{8,10},{9,11},{10,... | collective-permute-start | bytes 5898248 | tf_op jit(solution)/shard_map/ppermute | solution.py:135
  1462.1 235.9 %reduce-scatter.12.cloned.1.call-start = ((), (), s32[]{:S(2)}) async-start(), calls=%async_computation.8 | async-start | bytes 1474560 | tf_op jit(solution)/shard_map/reduce_scatter | solution.py:260
  1473.4 108.6 %collective-permute-start.104 = (bf16[4,2,48,4096]{3,2,1,0:T(8,128)(2,1)}, bf16[4,2,48,4096]{3,2,1,0:T(8,128)(2,1)}, u32[]{:S(2)}, u32[]{:S(2)}) collective-permute-start(bf16[4,2,48,4096]{3,2,1,0:T(8,128)(2,1)} %dynamic-slice_bitcast_fusion.1), channel_id=1, source_target_pairs={{0,2},{1,3},{2,0},{3,1},{4,6},{5,7},{6,4},{7,5},{8,10},{9,11},{10,... | collective-permute-start | bytes 9437192 | tf_op jit(solution)/shard_map/ppermute | solution.py:135
  1490.6 209.3 %reduce-scatter.8.cloned.1.call-start = ((), (), s32[]{:S(2)}) async-start(), calls=%async_computation.6 | async-start | bytes 1474560 | tf_op jit(solution)/shard_map/reduce_scatter | solution.py:260
  1491.0 89.4 %collective-permute-start.108 = (bf16[4,48,3072]{2,1,0:T(8,128)(2,1)S(1)}, bf16[4,48,3072]{2,1,0:T(8,128)(2,1)S(1)}, u32[]{:S(2)}, u32[]{:S(2)}) collective-permute-start(bf16[4,48,3072]{2,1,0:T(8,128)(2,1)S(1)} %dynamic-slice_bitcast_fusion.11), channel_id=1, source_target_pairs={{0,2},{1,3},{2,0},{3,1},{4,6},{5,7},{6,4},{7,5},{8,10},{9,11},{10,... | collective-permute-start | bytes 3538952 | tf_op jit(solution)/shard_map/ppermute | solution.py:135
  1499.2 91.4 %collective-permute-start.98 = (bf16[4,2,240,512]{3,2,0,1:T(8,128)(2,1)}, bf16[4,2,240,512]{3,2,0,1:T(8,128)(2,1)}, u32[]{:S(2)}, u32[]{:S(2)}) collective-permute-start(bf16[4,2,240,512]{3,2,0,1:T(8,128)(2,1)} %dynamic-slice_bitcast_fusion.5), channel_id=1, source_target_pairs={{0,1},{1,0},{2,3},{3,2},{4,5},{5,4},{6,7},{7,6},{8,9},{9,8},{10,11... | collective-permute-start | bytes 5898248 | tf_op jit(solution)/shard_map/ppermute | solution.py:135
  1504.4 97.2 %collective-permute-start.87 = (bf16[4,240,512]{2,1,0:T(8,128)(2,1)S(1)}, bf16[4,240,512]{2,1,0:T(8,128)(2,1)}, u32[]{:S(2)}, u32[]{:S(2)}) collective-permute-start(bf16[4,240,512]{2,1,0:T(8,128)(2,1)S(1)} %dynamic-slice_bitcast_fusion.14), channel_id=1, source_target_pairs={{0,2},{1,3},{2,0},{3,1},{4,6},{5,7},{6,4},{7,5},{8,10},{9,11},{10,... | collective-permute-start | bytes 2949128 | tf_op jit(solution)/shard_map/ppermute | solution.py:135
  1509.4 98.3 %collective-permute-start.93 = (bf16[4,240,512]{2,1,0:T(8,128)(2,1)}, bf16[4,240,512]{2,1,0:T(8,128)(2,1)}, u32[]{:S(2)}, u32[]{:S(2)}) collective-permute-start(bf16[4,240,512]{2,1,0:T(8,128)(2,1)} %dynamic-slice_bitcast_fusion.13), channel_id=1, source_target_pairs={{0,1},{1,0},{2,3},{3,2},{4,5},{5,4},{6,7},{7,6},{8,9},{9,8},{10,11... | collective-permute-start | bytes 2949128 | tf_op jit(solution)/shard_map/ppermute | solution.py:135
  1581.9 119.8 %reduce-scatter.6.cloned.1.call-start = ((), (), s32[]{:S(2)}) async-start(), calls=%async_computation.5 | async-start | bytes 1966080 | tf_op jit(solution)/shard_map/reduce_scatter | solution.py:260
  1633.2 61.7 %collective-permute-start.101 = (bf16[240,512]{1,0:T(8,128)(2,1)S(1)}, bf16[240,512]{1,0:T(8,128)(2,1)S(1)}, u32[]{:S(2)}, u32[]{:S(2)}) collective-permute-start(bf16[240,512]{1,0:T(8,128)(2,1)S(1)} %get-tuple-element.203), channel_id=1, source_target_pairs={{0,8},{4,12},{8,0},{12,4},{1,9},{5,13},{9,1},{13,5},{2,10},{6,14},... | collective-permute-start | bytes 737288 | tf_op jit(solution)/shard_map/ppermute | solution.py:256
  (286 other events, 5621.1 us)
Sparse Core Ops, SparseCore 0:
  10.3 67.7 all-gather.10
  79.6 46.3 all-gather.12
  127.5 32.0 all-gather.14
  161.1 29.5 all-gather.16
  615.0 112.6 all-gather.18
  858.3 111.2 reduce-scatter.13
  1462.3 29.2 reduce-scatter.9
  1493.9 27.8 reduce-scatter.11
  1582.0 34.1 reduce-scatter.7
  1625.0 59.4 reduce-scatter.5
where the time goes:
time: 1730 us; the launch traced here: 1710 us
  waiting for transfers between devices  694 us (40%)
  matrix products  277 us (16%)
  local copies, waits for them, and re-layouts  238 us (14%)
  other arithmetic  191 us (11%)
  starting transfers between devices  180 us (10%)
  Pallas kernels  112 us (6%)
  between operations  18.6 us (1%)
    ppermute x65, waiting for transfers between devices, flip(): return lax.ppermute(x, 'seq', [(i, i ^ bit) for i in range(peers)])  571 us
    dot_general x24, matrix products, dense_back(): lax.dot_general(left, right, (((1,), (1,)), ((), ())), preferred_element_...  105 us
    dot_general x12, matrix products, outer_sum(): lax.dot_general(left, right, (((0,), (0,)), ((), ())), preferred_element_...  92.3 us
    dot_general x12, matrix products, dense(): return jnp.dot(left, right, preferred_element_type=jnp.float32)  77.9 us
    ppermute x65, starting transfers between devices, flip(): return lax.ppermute(x, 'seq', [(i, i ^ bit) for i in range(peers)])  77.3 us
    pallas_call x10, Pallas kernels, sort_copies(): pl.pallas_call(kernel, in_specs=[pl.BlockSpec(memory_space=pl.ANY)] * len...  71 us
    dynamic_slice x18, local copies, waits for them, and re-layouts, pick(): return lax.dynamic_index_in_dim(x, index, axis, keepdims=False)  61.2 us
    unnamed x435, local copies, waits for them, and re-layouts  60.6 us
  transfers between devices with their start and end apart: 129, of which 38 were waited for; matrix products, arithmetic and copies ran while one was open for 38% of the time, Pallas kernels for 7%

commit v1 on v0

v1 whole, which is shorter than its diff:
```python
import jax
import jax.numpy as jnp
from jax import lax
from jax.experimental import pallas as pl
from jax.experimental.pallas import tpu as pltpu
from jax.sharding import PartitionSpec as P

HEADS = 8
QK = 64
V = 192
TRK_M = 1643
WIDTH = 5
NB = 32
EPSILON = 1e-05
ROWS = 128
BLOCK = 512
TILE = 256
EVERYWHERE = ("species", "dp", "seq")


def _head_lanes(e):
    lane = lax.broadcasted_iota(jnp.int32, (1, 2 * QK), 1)
    return (lane >= QK) == (e == 1)

def _toeplitz(u):
    wide = jnp.broadcast_to(u, (ROWS, u.shape[-1]))
    return pltpu.roll(wide, 0, 1, stride=1, stride_axis=0)

def _soft(q, k, bias):
    s = lax.dot_general(q, k, (((1,), (1,)), ((), ())), preferred_element_type=jnp.float32) + bias
    e = jnp.exp(s - jnp.max(s, axis=-1, keepdims=True))
    return e * (1.0 / jnp.sum(e, axis=-1, keepdims=True))

def _join(first, second):
    lane = lax.broadcasted_iota(jnp.int32, (1, 128), 1)
    return jnp.concatenate([first[:, :128], jnp.where(lane < 64, first[:, 128:], second[:, :128]), second[:, 128:]], axis=1)

def attn_fwd_kernel(q_ref, kv_ref, u_ref, o_ref):
    rows = q_ref.shape[0]
    length = kv_ref.shape[0]
    k = kv_ref[:, : 2 * QK]
    tables = [_toeplitz(u_ref[0, e : e + 1, :]) for e in range(2)]
    for a in range(rows // ROWS):
        at = rows - ROWS * a
        span = slice(ROWS * a, ROWS * (a + 1))
        q = q_ref[span, :]
        outs = []
        for e in range(2):
            qe = jnp.where(_head_lanes(e), q, jnp.zeros_like(q))
            p = _soft(qe, k, tables[e][:, at : at + length]).astype(jnp.bfloat16)
            outs.append(jnp.dot(p, kv_ref[:, 128 * e + 128 : 128 * e + 384], preferred_element_type=jnp.float32))
        o_ref[span, :] = _join(*outs).astype(o_ref.dtype)

PAIR = 2 * QK + 2 * V


def attn_fwd(q, kv, u):
    rows, length = q.shape[0], kv.shape[0]
    pairs = q.shape[1] // (2 * QK)
    return pl.pallas_call(
        attn_fwd_kernel,
        grid=(pairs,),
        in_specs=[
            pl.BlockSpec((rows, 2 * QK), lambda h: (0, h)),
            pl.BlockSpec((length, PAIR), lambda h: (0, h)),
            pl.BlockSpec((1, 2, u.shape[-1]), lambda h: (h, 0, 0)),
        ],
        out_specs=pl.BlockSpec((rows, 2 * V), lambda h: (0, h)),
        out_shape=jax.ShapeDtypeStruct((rows, pairs * 2 * V), jnp.bfloat16),
        compiler_params=pltpu.CompilerParams(vmem_limit_bytes=48 * 2**20),
        cost_estimate=pl.CostEstimate(
            flops=0, bytes_accessed=0, transcendentals=0
        ),
        name="attention_forward",
    )(q, kv, u)


def attn_bwd_kernel(
    q_ref, kv_ref, u_ref, g_ref, dq_ref, dkv_ref, du_ref, p_scr, s_scr, d_scr
):
    rows = q_ref.shape[0]
    length = kv_ref.shape[0]
    k = kv_ref[:, : 2 * QK]
    lane2 = lax.broadcasted_iota(jnp.int32, (1, 256), 1)
    dqs, dks, dvs = [], [], []
    for e in range(2):
        table = _toeplitz(u_ref[0, e : e + 1, :])
        d_scr[...] = jnp.zeros_like(d_scr)
        keep = (lane2 < 192) if e == 0 else (lane2 >= 64)
        vcols = slice(128 * e, 128 * e + 256)
        for a in range(rows // ROWS):
            at = rows - ROWS * a
            span = slice(ROWS * a, ROWS * (a + 1))
            q = q_ref[span, :]
            qe = jnp.where(_head_lanes(e), q, jnp.zeros_like(q))
            p = _soft(qe, k, table[:, at : at + length])
            g = g_ref[span, vcols]
            g = jnp.where(keep, g, jnp.zeros_like(g))
            dp = lax.dot_general(g, kv_ref[:, 128 * e + 128 : 128 * e + 384], (((1,), (1,)), ((), ())), preferred_element_type=jnp.float32)
            ds = p * (dp - jnp.sum(p * dp, axis=-1, keepdims=True))
            p_scr[span, :] = p.astype(jnp.bfloat16)
            s_scr[span, :] = ds.astype(jnp.bfloat16)
            d_scr[:, at : at + length] += ds
        ds = s_scr[...]
        dqs.append(jnp.dot(ds, k, preferred_element_type=jnp.float32))
        dks.append(lax.dot_general(ds, q_ref[...], (((0,), (0,)), ((), ())), preferred_element_type=jnp.float32))
        dvs.append(lax.dot_general(p_scr[...], g_ref[:, vcols], (((0,), (0,)), ((), ())), preferred_element_type=jnp.float32))
        fold = d_scr[...]
        width = fold.shape[1]
        step = ROWS // 2
        while step:
            fold = fold[:step] + pltpu.roll(fold[step:], width - step, 1)
            step //= 2
        du_ref[0, e : e + 1, :] = fold
    lane = lax.broadcasted_iota(jnp.int32, (1, 128), 1)
    dq_ref[...] = (jnp.where(lane < QK, dqs[0], dqs[1]) * QK ** (-0.5)).astype(dq_ref.dtype)
    dkv_ref[:, : 2 * QK] = jnp.where(lane < QK, dks[0], dks[1]).astype(dkv_ref.dtype)
    dkv_ref[:, 2 * QK :] = _join(*dvs).astype(dkv_ref.dtype)

def attn_bwd(q, kv, u, g):
    rows, length = q.shape[0], kv.shape[0]
    pairs = q.shape[1] // (2 * QK)
    specs = [
        pl.BlockSpec((rows, 2 * QK), lambda h: (0, h)),
        pl.BlockSpec((length, PAIR), lambda h: (0, h)),
        pl.BlockSpec((1, 2, u.shape[-1]), lambda h: (h, 0, 0)),
    ]
    return pl.pallas_call(
        attn_bwd_kernel,
        grid=(pairs,),
        in_specs=specs + [pl.BlockSpec((rows, 2 * V), lambda h: (0, h))],
        out_specs=specs,
        out_shape=[
            jax.ShapeDtypeStruct(q.shape, jnp.bfloat16),
            jax.ShapeDtypeStruct(kv.shape, jnp.bfloat16),
            jax.ShapeDtypeStruct(u.shape, jnp.float32),
        ],
        scratch_shapes=[
            pltpu.VMEM((rows, length), jnp.bfloat16),
            pltpu.VMEM((rows, length), jnp.bfloat16),
            pltpu.VMEM((ROWS, u.shape[-1]), jnp.float32),
        ],
        compiler_params=pltpu.CompilerParams(vmem_limit_bytes=56 * 2**20),
        cost_estimate=pl.CostEstimate(
            flops=0, bytes_accessed=0, transcendentals=0
        ),
        name="attention_backward",
    )(q, kv, u, g)


def flip(x, bit):
    peers = lax.axis_size("seq")
    return lax.ppermute(x, "seq", [(i, i ^ bit) for i in range(peers)])


def swap_cores(x):
    return lax.ppermute(x, "species", [(0, 1), (1, 0)])


def to_upper_core(x):
    return lax.ppermute(x, "species", [(0, 1)])


def to_lower_core(x):
    return lax.ppermute(x, "species", [(1, 0)])


def pick(x, index, axis=0):
    return lax.dynamic_index_in_dim(x, index, axis, keepdims=False)


def sort_copies(moves, out_shapes, *pieces):
    def kernel(*refs):
        ins, refs = refs[: len(pieces)], refs[len(pieces) :]
        outs, refs = refs[: len(out_shapes)], refs[len(out_shapes) :]
        stages, (in_sems, out_sems) = refs[: len(out_shapes)], refs[len(out_shapes) :]
        place = {axis: lax.axis_index(axis) for axis in EVERYWHERE}
        arrivals, departures = [], []
        for i, (piece, source, array, target) in enumerate(moves(place)):
            stage = stages[array].at[target]
            arrivals.append(pltpu.make_async_copy(ins[piece].at[source], stage, in_sems.at[i]))
            departures.append(
                pltpu.make_async_copy(stage, outs[array].at[target], out_sems.at[i])
            )
        for copy in arrivals:
            copy.start()
        for arrival, departure in zip(arrivals, departures):
            arrival.wait()
            departure.start()
        for copy in departures:
            copy.wait()

    count = len(moves({axis: 0 for axis in EVERYWHERE}))
    held = sum(x.size * 4 for x in out_shapes) // 2
    return pl.pallas_call(
        kernel,
        in_specs=[pl.BlockSpec(memory_space=pl.ANY)] * len(pieces),
        out_specs=[pl.BlockSpec(memory_space=pl.ANY)] * len(out_shapes),
        out_shape=out_shapes,
        scratch_shapes=[pltpu.VMEM(x.shape, x.dtype) for x in out_shapes]
        + [pltpu.SemaphoreType.DMA((count,))] * 2,
        compiler_params=pltpu.CompilerParams(vmem_limit_bytes=held * 2 + 4 * 2**20),
        cost_estimate=pl.CostEstimate(flops=0, bytes_accessed=0, transcendentals=0),
        name="sort_copies",
    )(*pieces)


def tie_kernel(*refs):
    del refs


def tie(x, *others):
    if not others:
        return x
    return pl.pallas_call(
        tie_kernel,
        in_specs=[pl.BlockSpec(memory_space=pl.ANY)] * (1 + len(others)),
        out_specs=pl.BlockSpec(memory_space=pl.ANY),
        out_shape=jax.ShapeDtypeStruct(x.shape, x.dtype),
        input_output_aliases={0: 0},
        cost_estimate=pl.CostEstimate(flops=0, bytes_accessed=0, transcendentals=0),
        name="tie",
    )(x, *others)


def beside(column, bit):
    return jnp.stack([column, flip(column, bit)])


def sorted_rows(parts, arrays):
    pieces = []
    for near, far, _, _ in parts:
        pieces += [near, far, swap_cores(near), swap_cores(far)]
    peers, depth = parts[0][0].shape[1:3]

    def moves(place):
        mine, seq = place["species"], place["seq"]
        everything = slice(None)
        found = []
        left = 0
        for part, (near, _, first, second) in enumerate(parts):
            right = left + near.shape[-1]
            runs = []
            for array, (_, _, blocks) in enumerate(arrays):
                for begin, size, which, column in blocks:
                    low, high = max(begin, left), min(begin + size, right)
                    if low < high:
                        source = pl.ds(low - left, high - low)
                        target = pl.ds(column + low - begin, high - low)
                        runs.append((array, source, which, target))
            left = right
            for piece, core, turn in (
                (0, mine, 0), (1, mine, second), (2, 1 - mine, 0), (3, 1 - mine, second)
            ):
                for m, bit in ((0, 0), (1, first)):
                    home = seq ^ (turn ^ bit)
                    for array, source, which, target in runs:
                        found.append(
                            (
                                4 * part + piece,
                                (m, everything, everything, source),
                                array,
                                (core, everything, home, which, everything, target),
                            )
                        )
        return found

    outs = sort_copies(
        moves,
        [
            jax.ShapeDtypeStruct((2, peers, 4, count, depth, width), pieces[0].dtype)
            for count, width, _ in arrays
        ],
        *pieces,
    )
    return [out.reshape(-1, out.shape[-1]) for out in outs]


def place_rows_kernel(at_ref, x_ref, o_ref, padded):
    rows, length, columns = x_ref.shape[0], o_ref.shape[0], o_ref.shape[1]
    margin = length - rows
    padded[...] = jnp.zeros_like(padded)
    padded[margin : margin + rows, :] = x_ref[...].astype(jnp.float32)
    begin = margin - at_ref[0]
    step = lax.rem(begin, 8)
    window = padded[pl.ds(pl.multiple_of(begin - step, 8), length + 8), :]
    turned = pltpu.roll(window.reshape(length // 8 + 1, 8, columns), lax.rem(8 - step, 8), 1)
    row = lax.broadcasted_iota(jnp.int32, (1, 8, columns), 1)
    placed = jnp.where(row < 8 - step, turned[:-1], turned[1:])
    o_ref[...] = placed.reshape(length, columns).astype(o_ref.dtype)


def place_rows(x, at, length):
    rows, columns = x.shape
    wide = 256
    return pl.pallas_call(
        place_rows_kernel,
        grid=(columns // wide,),
        in_specs=[
            pl.BlockSpec(memory_space=pltpu.SMEM),
            pl.BlockSpec((rows, wide), lambda i: (0, i)),
        ],
        out_specs=pl.BlockSpec((length, wide), lambda i: (0, i)),
        out_shape=jax.ShapeDtypeStruct((length, columns), x.dtype),
        scratch_shapes=[pltpu.VMEM((2 * length - rows + 8, wide), jnp.float32)],
        compiler_params=pltpu.CompilerParams(vmem_limit_bytes=32 * 2**20),
        name="place_rows",
    )(at.reshape(1), x)


def both_halves(mine):
    other = swap_cores(mine)

    def moves(place):
        core = place["species"]
        return [(0, (slice(None),), 0, (core,)), (1, (slice(None),), 0, (1 - core,))]

    return sort_copies(moves, [jax.ShapeDtypeStruct((2,) + mine.shape, mine.dtype)], mine, other)[0]


def tracks_grad_kernel(first_ref, second_ref, g_ref, o_ref):
    for which, left in enumerate((first_ref, second_ref)):
        span = slice(which * BLOCK, (which + 1) * BLOCK)
        o_ref[:, span] = lax.dot_general(
            left[...], g_ref[:, span], (((0,), (0,)), ((), ())), preferred_element_type=jnp.float32
        ).astype(o_ref.dtype)


def tracks_grad(first, second, g):
    rows, hidden = first.shape
    return pl.pallas_call(
        tracks_grad_kernel,
        grid=(hidden // TILE,),
        in_specs=[
            pl.BlockSpec((rows, TILE), lambda i: (0, i)),
            pl.BlockSpec((rows, TILE), lambda i: (0, i)),
            pl.BlockSpec((rows, 2 * BLOCK), lambda i: (0, 0)),
        ],
        out_specs=pl.BlockSpec((TILE, 2 * BLOCK), lambda i: (i, 0)),
        out_shape=jax.ShapeDtypeStruct((hidden, 2 * BLOCK), jnp.bfloat16),
        compiler_params=pltpu.CompilerParams(vmem_limit_bytes=32 * 2**20),
        cost_estimate=pl.CostEstimate(flops=0, bytes_accessed=0, transcendentals=0),
        name="tracks_grad",
    )(first, second, g)


def conv_forward_kernel(x_ref, w_ref, o_ref, total):
    length = x_ref.shape[0]
    margin = 8
    total[...] = jnp.zeros_like(total)
    for tap in range(WIDTH):
        for begin in range(0, length, TILE):
            product = jnp.dot(
                x_ref[begin : begin + TILE, :], w_ref[tap], preferred_element_type=jnp.float32
            )
            at = margin + begin + WIDTH // 2 - tap
            total[at : at + TILE, :] += product
    o_ref[...] = total[margin : margin + length, :].astype(o_ref.dtype)


def conv_forward(x, w):
    length, outputs = x.shape[0], w.shape[2]
    return pl.pallas_call(
        conv_forward_kernel,
        out_shape=jax.ShapeDtypeStruct((length, outputs), jnp.bfloat16),
        in_specs=[pl.BlockSpec(memory_space=pltpu.VMEM)] * 2,
        out_specs=pl.BlockSpec(memory_space=pltpu.VMEM),
        scratch_shapes=[pltpu.VMEM((length + 16, outputs), jnp.float32)],
        compiler_params=pltpu.CompilerParams(vmem_limit_bytes=40 * 2**20),
        cost_estimate=pl.CostEstimate(flops=0, bytes_accessed=0, transcendentals=0),
        name="conv_forward",
    )(x, w)


def conv_back_kernel(g_ref, w_ref, o_ref):
    outputs = w_ref.shape[2]
    total = None
    for tap in range(WIDTH):
        term = lax.dot_general(
            g_ref[:, tap * outputs : (tap + 1) * outputs],
            w_ref[tap],
            (((1,), (1,)), ((), ())),
            preferred_element_type=jnp.float32,
        )
        total = term if total is None else total + term
    o_ref[...] = total.astype(o_ref.dtype)


def conv_back(g, w):
    length, chans = g.shape[0], w.shape[1]
    return pl.pallas_call(
        conv_back_kernel,
        grid=(length // TILE,),
        in_specs=[
            pl.BlockSpec((TILE, g.shape[1]), lambda i: (i, 0)),
            pl.BlockSpec(w.shape, lambda i: (0, 0, 0)),
        ],
        out_specs=pl.BlockSpec((TILE, chans), lambda i: (i, 0)),
        out_shape=jax.ShapeDtypeStruct((length, chans), jnp.bfloat16),
        compiler_params=pltpu.CompilerParams(vmem_limit_bytes=40 * 2**20),
        cost_estimate=pl.CostEstimate(flops=0, bytes_accessed=0, transcendentals=0),
        name="conv_back",
    )(g, w)


def outer_kernel(base_ref, left_ref, right_ref, *refs):
    total = lax.dot_general(
        left_ref[...], right_ref[...], (((0,), (0,)), ((), ())), preferred_element_type=jnp.float32
    )
    if len(refs) == 2:
        total = total + refs[0][...].astype(jnp.float32)
    refs[-1][...] = total.astype(refs[-1].dtype)


def outer_half(left, right, which, more=None, taps=1):
    rows, chans = left.shape
    columns = right.shape[1] // taps
    tiles = chans // TILE
    count = taps * tiles // 2
    base = ((lax.axis_index("species") ^ which) * count).reshape(1).astype(jnp.int32)
    out_spec = pl.BlockSpec((TILE, columns), lambda i, at: (i, 0))
    return pl.pallas_call(
        outer_kernel,
        grid_spec=pltpu.PrefetchScalarGridSpec(
            num_scalar_prefetch=1,
            grid=(count,),
            in_specs=[
                pl.BlockSpec((rows, TILE), lambda i, at: (0, lax.rem(at[0] + i, tiles))),
                pl.BlockSpec((rows, columns), lambda i, at: (0, lax.div(at[0] + i, tiles))),
            ]
            + ([] if more is None else [out_spec]),
            out_specs=out_spec,
        ),
        out_shape=jax.ShapeDtypeStruct((count * TILE, columns), jnp.bfloat16),
        compiler_params=pltpu.CompilerParams(vmem_limit_bytes=40 * 2**20),
        cost_estimate=pl.CostEstimate(flops=0, bytes_accessed=0, transcendentals=0),
        name="outer_half",
    )(base, left, right, *([] if more is None else [more]))


def by_device(total):
    peers = lax.axis_size("dp")
    return total.reshape(peers, 2, 2, total.shape[0] // (4 * peers), total.shape[1])


def fold(half, bit):
    axis = 2 if bit == 1 and half.ndim == 5 else 1
    here = lax.rem(lax.div(lax.axis_index("seq"), bit), 2)
    away = flip(pick(half, 1 - here, axis), bit)
    return (pick(half, here, axis).astype(jnp.float32) + away.astype(jnp.float32)).astype(half.dtype)


def fold_both(grads, steps):
    if steps == 0:
        middle = grads.shape[-1] // 2
        return fold(grads[..., :middle], 1), fold(grads[..., middle:], 2)
    return fold(grads[0], 2), fold(grads[1], 1)


def gather_begin(x):
    half = x.shape[0] // 2
    from_x, from_y = flip(x, 1), flip(x, 2)
    return x, from_x, from_y, from_x[:half], from_y[half:]


def gather_end(x, from_x, from_y, top, bottom):
    rows = x.shape[0]
    half = rows // 2
    top, bottom = flip(top, 2), flip(bottom, 1)

    def moves(place):
        seq = place["seq"]
        everything = slice(None)
        return [
            (0, (everything,), 0, (seq,)),
            (1, (everything,), 0, (seq ^ 1,)),
            (2, (everything,), 0, (seq ^ 2,)),
            (3, (everything,), 0, (seq ^ 3, pl.ds(0, half))),
            (4, (everything,), 0, (seq ^ 3, pl.ds(half, half))),
        ]

    out = sort_copies(
        moves, [jax.ShapeDtypeStruct((4,) + x.shape, x.dtype)], x, from_x, from_y, top, bottom
    )[0]
    return out.reshape((4 * rows,) + x.shape[1:])


def scatter_blocks(x):
    place = lax.axis_index("seq")
    rows, columns = x.shape[0] // 4, x.shape[1]
    half = rows // 2
    parts = x.reshape(4, 2, half, columns)

    def block(toward, which):
        return lax.dynamic_slice(
            parts, (lax.bitwise_xor(place, toward), which, 0, 0), (1, 1, half, columns)
        )[0, 0]

    sends = [jnp.stack([block(1, 0), block(3, 0)]), jnp.stack([block(2, 1), block(3, 1)])]
    return sends, [block(0, 0), block(0, 1)], [block(2, 0), block(1, 1)]


def scatter_begin(sends, kept, passed):
    mine, onward = [], []
    for sent, keep, hand, bit in zip(sends, kept, passed, (1, 2)):
        away = flip(sent, bit).astype(jnp.float32)
        mine.append(keep.astype(jnp.float32) + away[0])
        onward.append((hand.astype(jnp.float32) + away[1]).astype(jnp.bfloat16))
    return mine, onward


def scatter_end(mine, onward):
    last = flip(onward[1], 1)
    arrived = [tie(flip(onward[0], 2), last), last]
    return jnp.concatenate([a + b.astype(jnp.float32) for a, b in zip(mine, arrived)], axis=0)


def exchange_plane(x):
    place = lax.axis_index("seq")
    arrived = [pick(x, place)] + [
        flip(pick(x, lax.bitwise_xor(place, bit)), bit) for bit in (1, 2, 3)
    ]
    stacked = jnp.stack(arrived)
    return jnp.stack([pick(stacked, lax.bitwise_xor(place, j)) for j in range(4)])


def sum_chips(x):
    x = x + swap_cores(x)
    x = x + flip(x, 1)
    return x + flip(x, 2)


def sum_column(x):
    peers = lax.axis_size("dp")
    step = 1
    while step < peers:
        x = x + lax.ppermute(x, "dp", [(i, i ^ step) for i in range(peers)])
        step *= 2
    return x


def spread_tracks(x):
    rows = x.shape[0]
    lower = lax.axis_index("species") == 0
    human = jnp.pad(x, ((0, 0), (0, 12 * BLOCK - x.shape[1]))).reshape(rows, 4, 3, BLOCK)
    human = human.transpose(1, 2, 0, 3)
    mouse = x[:, : 4 * BLOCK].reshape(rows, 4, BLOCK).transpose(1, 0, 2)
    other = to_upper_core(human[:, 2])
    first = jnp.where(lower, human[:, 0], other)
    second = jnp.where(lower, human[:, 1], mouse)
    return jnp.concatenate([first, second], axis=-1)


def collect_tracks(x, tracks):
    rows = x.shape[1]
    lower = lax.axis_index("species") == 0
    other = to_lower_core(x[:, :, :BLOCK])
    human = jnp.stack([x[:, :, :BLOCK], x[:, :, BLOCK:], other], axis=1)
    human = human.transpose(2, 0, 1, 3).reshape(rows, 12 * BLOCK)[:, :tracks]
    mouse = x[:, :, BLOCK:].transpose(1, 0, 2).reshape(rows, 4 * BLOCK)
    mouse = jnp.pad(mouse, ((0, 0), (0, tracks - 4 * BLOCK)))
    return jnp.where(lower, human, mouse)


def layer_norm(value_entries, gain, shift):
    centre = jnp.mean(value_entries, axis=-1, keepdims=True)
    centred = value_entries - centre
    spread = jnp.mean(centred * centred, axis=-1, keepdims=True)
    return centred * lax.rsqrt(spread + EPSILON) * gain + shift


def gelu_and_slope(pre):
    act, back = jax.vjp(jax.nn.gelu, pre)
    return act.astype(jnp.bfloat16), back(jnp.ones_like(pre))[0].astype(jnp.bfloat16)


def dense(left, right):
    return jnp.dot(left, right, preferred_element_type=jnp.float32)


def dense_back(left, right):
    return lax.dot_general(
        left, right, (((1,), (1,)), ((), ())), preferred_element_type=jnp.float32
    )


def outer_sum(left, right):
    return lax.dot_general(
        left, right, (((0,), (0,)), ((), ())), preferred_element_type=jnp.float32
    )


def row_sum(value_entries):
    return jnp.sum(value_entries.astype(jnp.float32), axis=0)


def on_device(
    inputs,
    crop_start,
    rel_bucket,
    conv_weight,
    query_weight,
    key_weight,
    value_weight,
    out_weight,
    up_weight,
    down_weight,
    point_weight,
    rel_table,
    bn_gain,
    bn_shift,
    conv_bias,
    attn_gain,
    attn_shift,
    ffn_gain,
    ffn_shift,
    up_bias,
    down_bias,
    point_bias,
    head_weight,
    pred_grad,
):
    low = jnp.bfloat16
    wide = jnp.float32
    bin_count, chans = inputs.shape[2], inputs.shape[3]
    tracks = head_weight.shape[2]
    crop_rows = 4 * pred_grad.shape[2]
    seq_pos = lax.axis_index("seq")
    species_id = lax.axis_index("species")
    lower = species_id == 0
    dp_count = lax.axis_size("dp")
    device_count = 2 * dp_count * 4
    portion_index = lax.axis_index(EVERYWHERE)
    full_len = 4 * bin_count
    element_count = float(device_count * bin_count)
    half_width = WIDTH // 2

    outputs = chans // 4
    conv_share = exchange_plane(
        conv_weight.reshape(conv_weight.shape[0], 4, outputs).transpose(1, 0, 2)
    )
    conv_half = lax.all_gather(conv_share, "dp")

    value_entries = inputs[0, 0].astype(wide)
    small = (
        bn_gain, bn_shift, conv_bias, attn_gain, attn_shift, ffn_gain, ffn_shift, up_bias, down_bias,
        point_bias, rel_table,
    )

    def placed(x):
        whole = jnp.zeros((device_count * x.shape[0],), wide)
        return lax.dynamic_update_slice_in_dim(whole, x.astype(wide), portion_index * x.shape[0], 0)

    joined = jnp.concatenate(
        [jnp.sum(value_entries, axis=0), jnp.sum(value_entries * value_entries, axis=0)]
        + [placed(x) for x in small]
    )
    joined = sum_chips(joined.reshape(-1, 128))
    spread = spread_tracks(
        tie(jnp.concatenate([head_weight[0], pred_grad[0, 0]], axis=0), joined)
    )
    joined = sum_column(joined)
    joined = joined.reshape(-1)
    moment_one, moment_two = joined[:chans], joined[chans : 2 * chans]
    at = 2 * chans
    whole_small = []
    for x in small:
        size = device_count * x.shape[0]
        whole_small.append(joined[at : at + size])
        at += size
    (
        batchnorm_gain, batchnorm_shift, bias_conv, gain_attn, shift_attn, gain_ffn, shift_ffn, bias_up,
        bias_down, bias_point, table_flat,
    ) = whole_small

    pairs = HEADS // 2
    mixer_shard = jnp.concatenate(
        [
            x[:, h * width : (h + 1) * width]
            for h in range(pairs)
            for x, width in ((key_weight, 2 * QK), (value_weight, 2 * V))
        ]
        + [query_weight, out_weight],
        axis=1,
    )
    mixer_column = lax.all_gather(tie(mixer_shard, conv_share), "dp")
    depth = up_weight.shape[0]
    rest_shard = jnp.concatenate(
        [up_weight, down_weight[:depth], down_weight[depth:], point_weight], axis=1
    )
    rest_column = lax.all_gather(tie(rest_shard, mixer_column), "dp")
    head_rows = head_weight.shape[1]
    spread = exchange_plane(spread)
    track_grad = spread[:, head_rows:].reshape(crop_rows, 2 * BLOCK)
    kv_width, q_width, hidden = pairs * PAIR, query_weight.shape[1], up_weight.shape[1]
    ways = ((1, 2), (2, 1))

    def first_step(column, begin, size, *after):
        return [
            beside(tie(column[..., begin + i * size : begin + (i + 1) * size], *after), way[0])
            for i, way in enumerate(ways)
        ]

    def second_step(nears, *after):
        return [flip(tie(near, *after), way[1]) for near, way in zip(nears, ways)]

    def parts(nears, fars):
        return [(near, far) + way for near, far, way in zip(nears, fars, ways)]

    channel_average = moment_one / element_count
    inverse_deviation = lax.rsqrt(
        moment_two / element_count - channel_average * channel_average + EPSILON
    )
    standardized_input = (value_entries - channel_average) * inverse_deviation
    normed_rows = standardized_input * batchnorm_gain + batchnorm_shift
    activity, act_slope = gelu_and_slope(normed_rows)
    act_rows = gather_begin(activity)
    act_rows = act_rows[:3] + tuple(tie(x, spread) for x in act_rows[3:])
    act_all = gather_end(*act_rows)
    w_conv = both_halves(conv_half).reshape(WIDTH, chans, outputs)
    mixer_near = first_step(mixer_column, 0, mixer_column.shape[-1] // 2, act_all)
    mixer_far = second_step(mixer_near)
    conv_slice = conv_forward(act_all, w_conv).reshape(4, bin_count, outputs)
    w_head = lax.all_gather(tie(spread[:, :head_rows], rest_column), "dp").reshape(-1, 2 * BLOCK)
    conv_slice = exchange_plane(conv_slice)
    conv_out = bias_conv + conv_slice.transpose(1, 0, 2).reshape(bin_count, chans).astype(wide)
    first_sum = value_entries + conv_out
    w_kv, w_query, w_out = sorted_rows(
        parts(mixer_near, mixer_far),
        [
            (1, kv_width, [(0, kv_width, 0, 0)]),
            (1, q_width, [(kv_width, q_width, 0, 0)]),
            (1, chans, [(kv_width + q_width, chans, 0, 0)]),
        ],
    )
    normed_one = layer_norm(first_sum, gain_attn, shift_attn).astype(low)
    scale = QK ** (-0.5)
    kv_rows = gather_begin(dense(normed_one, w_kv).astype(low))
    query_rows = (dense(normed_one, w_query).astype(low).astype(wide) * scale).astype(low)
    ffn_near = first_step(rest_column, 0, hidden, *kv_rows[1:3])
    kv_all = gather_end(*kv_rows)
    ffn_far = second_step(ffn_near, kv_all)
    point_near = first_step(rest_column, 2 * hidden, point_weight.shape[1] // 2, kv_all)
    point_far = second_step(point_near, *ffn_far)
    bucket_window = lax.dynamic_slice_in_dim(
        jnp.pad(rel_bucket, (1, 0), constant_values=-1),
        full_len - bin_count - seq_pos * bin_count,
        full_len + bin_count,
    )
    window_onehot = (bucket_window[:, None] == jnp.arange(NB)[None, :]).astype(wide)
    distance_bias = lax.dot_general(
        table_flat.reshape(HEADS, NB), window_onehot, (((1,), (1,)), ((), ())),
        precision=lax.Precision.HIGHEST, preferred_element_type=wide,
    ).reshape(pairs, 2, full_len + bin_count)
    mixed = attn_fwd(query_rows, kv_all, distance_bias)
    second_sum = first_sum + dense(mixed, w_out)
    (w_up, w_down) = sorted_rows(
        parts(ffn_near, ffn_far),
        [
            (1, hidden, [(0, hidden, 0, 0)]),
            (2, chans, [(hidden, chans, 0, 0), (hidden + chans, chans, 1, 0)]),
        ],
    )
    normed_two = layer_norm(second_sum, gain_ffn, shift_ffn).astype(low)
    up_pre = dense(normed_two, w_up) + bias_up
    up_act, up_slope = gelu_and_slope(up_pre)
    third_sum = second_sum + dense(up_act, w_down) + bias_down
    third_rows = gather_begin(tie(third_sum.astype(low), w_head))
    third_all = gather_end(*third_rows)
    (w_point,) = sorted_rows(
        parts(point_near, point_far),
        [(1, point_weight.shape[1], [(0, point_weight.shape[1], 0, 0)])],
    )
    crop_at = crop_start[0, 0]
    cropped = lax.dynamic_slice_in_dim(third_all, crop_at, crop_rows, 0)
    point_pre = dense(cropped, w_point) + bias_point
    point_act, point_slope = gelu_and_slope(point_pre)

    human_act = jnp.where(lower, point_act, to_upper_core(point_act))
    column = jnp.arange(BLOCK)
    first_valid = 3 * BLOCK * seq_pos + jnp.where(lower, 0, 2 * BLOCK) + column < tracks
    second_valid = jnp.where(
        lower, 3 * BLOCK * seq_pos + BLOCK + column < tracks, BLOCK * seq_pos + column < TRK_M
    )
    preds, logit_grads = [], []
    for which, act, valid in ((0, human_act, first_valid), (1, point_act, second_valid)):
        span = slice(which * BLOCK, (which + 1) * BLOCK)
        mask = valid.astype(wide)
        logits = dense(act, w_head[:, span])
        preds.append((jax.nn.softplus(logits) * mask).astype(low))
        logit_grads.append(
            (track_grad[:, span].astype(wide) * mask * jax.nn.sigmoid(logits)).astype(low)
        )
    arrived = to_lower_core(dense_back(logit_grads[0], w_head[:, :BLOCK]).astype(low))
    logit_grad = jnp.concatenate(logit_grads, axis=1)
    own_grad = jnp.concatenate(
        [jnp.where(lower, logit_grads[0], jnp.zeros_like(logit_grads[0])), logit_grads[1]], axis=1
    )
    point_act_grad = dense_back(own_grad, w_head) + jnp.where(lower, arrived.astype(wide), 0.0)

    point_grad = (point_slope.astype(wide) * point_act_grad).astype(low)
    crop_grad = dense_back(point_grad, w_point).astype(low)
    third_blocks = scatter_blocks(place_rows(crop_grad, crop_at, full_len))
    third_mine, third_onward = scatter_begin(*third_blocks)
    head_part = tracks_grad(human_act, point_act, tie(logit_grad, *third_blocks[0])).reshape(
        dp_count, -1, 2 * BLOCK
    )
    point_grad = tie(point_grad, *third_blocks[0])
    point_sent = outer_half(cropped, point_grad, 1)
    point_other = swap_cores(point_sent)
    third_onward = [tie(x, head_part, point_sent) for x in third_onward]
    head_sum = lax.psum_scatter(head_part, "dp", scatter_dimension=0, tiled=False)
    grad_point_b = row_sum(point_grad)
    point_half = by_device(outer_half(cropped, point_grad, 0, point_other))
    third_grad = tie(scatter_end(third_mine, third_onward), point_half)

    preds = exchange_plane(
        tie(jnp.concatenate(preds, axis=1), third_grad).reshape(4, crop_rows // 4, 2 * BLOCK)
    )
    point_once = fold_both(point_half, 0)
    down_grad = third_grad.astype(low)
    down_other = swap_cores(outer_half(up_act, down_grad, 1))
    grad_down_b = row_sum(down_grad)
    up_grad = (up_slope.astype(wide) * dense_back(down_grad, w_down)).astype(low)
    down_half = by_device(outer_half(up_act, down_grad, 0, down_other))
    up_grad = tie(up_grad, down_half, *point_once)

    point_twice = fold_both(point_once, 1)
    down_once = fold_both(down_half, 0)
    up_other = swap_cores(outer_half(normed_two, up_grad, 1))
    grad_up_b = row_sum(up_grad)
    _, norm_two_back = jax.vjp(layer_norm, second_sum, gain_ffn, shift_ffn)
    second_part, grad_ffn_gain, grad_ffn_shift = norm_two_back(dense_back(up_grad, w_up))
    second_grad = third_grad + second_part
    out_grad = second_grad.astype(low)
    mixed_grad = dense_back(out_grad, w_out).astype(low)
    up_half = by_device(outer_half(normed_two, up_grad, 0, up_other))
    mixed_grad = tie(mixed_grad, up_half, *point_twice, *down_once)

    down_twice = fold_both(down_once, 1)
    up_once = fold_both(up_half, 0)
    out_other = swap_cores(outer_half(mixed, out_grad, 1))
    query_low, kv_part, distance_grad = attn_bwd(
        query_rows, kv_all, distance_bias, mixed_grad
    )
    kv_part = tie(kv_part, out_other, *down_twice, *up_once)

    up_twice = fold_both(up_once, 1)
    kv_mine, kv_onward = scatter_begin(*scatter_blocks(kv_part))
    grad_table = jnp.dot(
        distance_grad.reshape(HEADS, -1), window_onehot, precision=lax.Precision.HIGHEST,
        preferred_element_type=wide,
    ).reshape(HEADS * NB)
    out_half = by_device(outer_half(mixed, out_grad, 0, out_other))
    kv_onward = [tie(x, out_half, head_sum, *up_twice) for x in kv_onward]
    rest_sum = lax.psum_scatter(
        jnp.concatenate(
            [*point_twice, *up_twice]
            + [x[:, rows] for rows in (slice(0, depth), slice(depth, None)) for x in down_twice],
            axis=-1,
        ),
        "dp", scatter_dimension=0, tiled=False,
    ).astype(wide)
    kv_low = scatter_end(kv_mine, kv_onward).astype(low)

    mixer_grads = jnp.concatenate([kv_low, query_low], axis=1)
    mixer_other = swap_cores(outer_half(normed_one, mixer_grads, 1))
    normed_one_grad = dense_back(kv_low, w_kv) + dense_back(query_low, w_query)
    _, norm_one_back = jax.vjp(layer_norm, first_sum, gain_attn, shift_attn)
    first_part, grad_attn_gain, grad_attn_shift = norm_one_back(normed_one_grad)
    first_grad = second_grad + first_part
    mixer_half = jnp.concatenate(
        [by_device(outer_half(normed_one, mixer_grads, 0, mixer_other)), out_half], axis=-1
    )
    conv_grad = tie(first_grad.astype(low), mixer_half)
    grad_conv_b = row_sum(conv_grad)
    conv_part = exchange_plane(
        conv_grad.reshape(bin_count, 4, outputs).transpose(1, 0, 2)
    ).reshape(full_len, outputs)

    mixer_once = fold_both(mixer_half, 0)
    padded = jnp.pad(conv_part, ((half_width, half_width), (0, 0)))
    taps = jnp.concatenate(
        [padded[2 * half_width - k : 2 * half_width - k + full_len] for k in range(WIDTH)], axis=1
    )
    conv_sent = outer_half(act_all, taps, 1, taps=WIDTH)
    conv_other = swap_cores(conv_sent)
    act_part = conv_back(tie(taps, conv_sent), w_conv)
    conv_sum = outer_half(act_all, tie(taps, act_part), 0, conv_other, taps=WIDTH)
    act_part = tie(act_part, *mixer_once)
    mixer_twice = fold_both(mixer_once, 1)
    act_mine, act_onward = scatter_begin(*scatter_blocks(act_part))
    act_onward = [tie(x, *mixer_twice) for x in act_onward]
    act_grad = scatter_end(act_mine, act_onward)
    predictions = collect_tracks(tie(preds, *act_onward), tracks)
    grad_mixer = lax.psum_scatter(
        jnp.concatenate(mixer_twice, axis=-1), "dp", scatter_dimension=0, tiled=False
    ).astype(wide)
    conv_sum = lax.psum_scatter(
        conv_sum.reshape(dp_count, -1, outputs), "dp", scatter_dimension=0, tiled=False
    )
    grad_conv_w = exchange_plane(conv_sum.reshape(4, -1, outputs))
    grad_conv_w = grad_conv_w.transpose(1, 0, 2).reshape(-1, chans).astype(wide)
    head_grad = collect_tracks(
        exchange_plane(tie(head_sum, *act_onward).reshape(4, head_rows, 2 * BLOCK)), tracks
    ).astype(wide)
    grad_point_w = rest_sum[:, : point_weight.shape[1]]
    at = point_weight.shape[1]
    grad_up_w = rest_sum[:, at : at + hidden]
    at += hidden
    grad_down_w = jnp.concatenate([rest_sum[:, at : at + chans], rest_sum[:, at + chans :]], axis=0)
    normed_rows_gradient = act_slope.astype(wide) * act_grad
    vectors = (
        jnp.sum(normed_rows_gradient * standardized_input, axis=0),
        jnp.sum(normed_rows_gradient, axis=0),
        grad_table,
        grad_conv_b,
        grad_attn_gain,
        grad_attn_shift,
        grad_ffn_gain,
        grad_ffn_shift,
        grad_up_b,
        grad_down_b,
        grad_point_b,
    )
    summed = sum_column(sum_chips(jnp.concatenate(vectors).reshape(-1, 128))).reshape(-1)
    standardized_sum, plain_gradient_sum = summed[:chans], summed[chans : 2 * chans]
    input_grad = first_grad + batchnorm_gain * inverse_deviation * (
        normed_rows_gradient
        - plain_gradient_sum / element_count
        - standardized_input * standardized_sum / element_count
    )
    shares = []
    at = 0
    for x in vectors:
        size = x.shape[0] // device_count
        shares.append(lax.dynamic_slice_in_dim(summed, at + portion_index * size, size))
        at += x.shape[0]
    bn_gain_share, bn_shift_share, table_share, conv_b_share = shares[:4]
    attn_gain_share, attn_shift_share, ffn_gain_share, ffn_shift_share = shares[4:8]
    up_b_share, down_b_share, point_b_share = shares[8:]
    kv_share = grad_mixer[:, :kv_width].reshape(-1, pairs, PAIR)
    key_share = kv_share[:, :, : 2 * QK].reshape(-1, key_weight.shape[1])
    value_share = kv_share[:, :, 2 * QK :].reshape(-1, value_weight.shape[1])
    query_share = grad_mixer[:, kv_width : kv_width + q_width]
    out_share = grad_mixer[:, kv_width + q_width :]
    return (
        predictions[None, None],
        input_grad[None, None],
        grad_conv_w,
        query_share,
        key_share,
        value_share,
        out_share,
        grad_up_w,
        grad_down_w,
        grad_point_w,
        table_share,
        bn_gain_share,
        bn_shift_share,
        conv_b_share,
        attn_gain_share,
        attn_shift_share,
        ffn_gain_share,
        ffn_shift_share,
        up_b_share,
        down_b_share,
        point_b_share,
        head_grad[None],
    )


def solution(mesh):
    everywhere = P(EVERYWHERE)
    rows = P(EVERYWHERE, None)
    bins = P("species", "dp", "seq", None)
    head = P("species", ("dp", "seq"), None)
    return jax.shard_map(
        on_device,
        mesh=mesh,
        in_specs=(bins, P("species", "dp"), P()) + (rows,) * 8 + (everywhere,) * 11 + (head, bins),
        out_specs=(bins, bins) + (rows,) * 8 + (everywhere,) * 11 + (head,),
        check_vma=False,
    )
```

time: 1730 us -> 1280 us (0.74)
  waiting for transfers between devices: 694 us -> 458 us
  matrix products: 277 us -> 129 us
  Pallas kernels: 112 us -> 192 us
  starting transfers between devices: 180 us -> 108 us
  other arithmetic: 191 us -> 143 us
    ppermute x65 -> x77, waiting for transfers between devices: 571 us -> 448 us  [flip(): return lax.ppermute(x, 'seq', [(i, i ^ bit) for i in range(peers)])]
    pallas_call x0 -> x55, Pallas kernels: none -> 121 us  [the longest x12 77.8 us: outer_half(): pl.pallas_call(outer_kernel, grid_spec=pltpu.PrefetchScalarGridSpec(num_s...]
    dot_general x12 -> x0, matrix products: 92.3 us -> none  [outer_sum(): lax.dot_general(left, right, (((0,), (0,)), ((), ())), preferred_element_...]
    ppermute x26 -> x4, starting transfers between devices: 82.4 us -> 8.87 us  [sum_column(): x = x + lax.ppermute(x, 'dp', [(i, i ^ step) for i in range(peers)])]
    ppermute x26 -> x4, waiting for transfers between devices: 74.3 us -> 4.49 us  [sum_column(): x = x + lax.ppermute(x, 'dp', [(i, i ^ step) for i in range(peers)])]
    unnamed x435 -> x468, local copies, waits for them, and re-layouts: 60.6 us -> 110 us
    dynamic_slice x18 -> x19, local copies, waits for them, and re-layouts: 61.2 us -> 13.2 us  [pick(): return lax.dynamic_index_in_dim(x, index, axis, keepdims=False)]
    all_gather x5 -> x4, waiting for transfers between devices: 47.3 us -> 0.03 us  [the longest x1 0.02 us: on_device(): conv_half = lax.all_gather(conv_share, 'dp')]
  transfers between devices with their start and end apart: 129 -> 115, of which waited for: 38 -> 55; matrix products, arithmetic and copies ran while one was open for 38% -> 27% of each run, Pallas kernels for 7% -> 13%
where the time goes in v1:
time: 1280 us; the launch traced here: 1270 us
  waiting for transfers between devices  458 us (36%)
  local copies, waits for them, and re-layouts  226 us (18%)
  Pallas kernels  192 us (15%)
  other arithmetic  143 us (11%)
  matrix products  129 us (10%)
  starting transfers between devices  108 us (8%)
  between operations  18.1 us (1%)
    ppermute x77, waiting for transfers between devices, flip(): return lax.ppermute(x, 'seq', [(i, i ^ bit) for i in range(peers)])  448 us
    unnamed x468, local copies, waits for them, and re-layouts  110 us
    ppermute x77, starting transfers between devices, flip(): return lax.ppermute(x, 'seq', [(i, i ^ bit) for i in range(peers)])  82.1 us
    pallas_call x12, Pallas kernels, outer_half(): pl.pallas_call(outer_kernel, grid_spec=pltpu.PrefetchScalarGridSpec(num_s...  77.8 us
    dot_general x8, matrix products, dense_back(): lax.dot_general(left, right, (((1,), (1,)), ((), ())), preferred_element_...  71 us
    dot_general x8, matrix products, dense(): return jnp.dot(left, right, preferred_element_type=jnp.float32)  57.2 us
    pallas_call x7, Pallas kernels, sort_copies(): pl.pallas_call(kernel, in_specs=[pl.BlockSpec(memory_space=pl.ANY)] * len...  29.3 us
    pallas_call x1, Pallas kernels, attn_bwd(): pl.pallas_call(attn_bwd_kernel, grid=(pairs,), in_specs=specs + [pl.Block...  29.1 us
  transfers between devices with their start and end apart: 115, of which 55 were waited for; matrix products, arithmetic and copies ran while one was open for 27% of the time, Pallas kernels for 13%

profile of v1, /device:TPU:0, one launch (start us, length us, event | category | flops | bytes accessed | tf_op | source)
XLA Modules:
  0.0 1274.6 jit_solution(7403168550872712375)
XLA Ops:
  39.7 7.4 copy.372
  53.1 8.3 copy.281
  87.0 22.6 %collective-permute-done.5.refs_1_ = bf16[384,1536]{1,0:T(8,128)(2,1)S(1)} collective-permute-done((bf16[384,1536]{1,0:T(8,128)(2,1)S(1)}, bf16[384,1536]{1,0:T(8,128)(2,1)S(1)}, u32[]{:S(2)}, u32[]{:S(2)}) %collective-permute-start.5) | collective-permute-done | bytes 1179680 | tf_op jit(solution)/shard_map/ppermute | solution.py:153
  110.5 17.5 %collective-permute-done.6.refs_2_ = bf16[384,1536]{1,0:T(8,128)(2,1)S(1)} collective-permute-done((bf16[384,1536]{1,0:T(8,128)(2,1)S(1)}, bf16[384,1536]{1,0:T(8,128)(2,1)S(1)}, u32[]{:S(2)}, u32[]{:S(2)}) %collective-permute-start.6) | collective-permute-done | bytes 1179680 | tf_op jit(solution)/shard_map/ppermute | solution.py:153
  128.9 11.6 collective-permute-done.9
  161.8 11.6 collective-permute-done.20
  188.4 18.8 %collective-permute-done.21.refs_1_ = bf16[2,4,48,2048]{3,2,1,0:T(8,128)(2,1)} collective-permute-done((bf16[2,4,48,2048]{3,2,1,0:T(8,128)(2,1)S(1)}, bf16[2,4,48,2048]{3,2,1,0:T(8,128)(2,1)}, u32[]{:S(2)}, u32[]{:S(2)}) %collective-permute-start.21) | collective-permute-done | bytes 1572896 | tf_op jit(solution)/shard_map/ppermute | solution.py:153
  207.2 7.9 collective-permute-done.25.refs_5_
  224.1 12.8 %conv_forward.1 = bf16[1536,384]{1,0:T(8,128)(2,1)S(1)} custom-call(bf16[1536,1536]{1,0:T(8,128)(2,1)S(1)} %bitcast.596, bf16[5,1536,384]{2,1,0:T(8,128)(2,1)S(1)} %bitcast.613), custom_call_target="tpu_custom_call" | custom-call | tf_op jit(solution)/shard_map/conv_forward/pallas_call | solution.py:363
  277.5 31.4 %collective-permute-done.28.refs_1_ = bf16[384,2048]{1,0:T(8,128)(2,1)S(1)} collective-permute-done((bf16[384,2048]{1,0:T(8,128)(2,1)}, bf16[384,2048]{1,0:T(8,128)(2,1)S(1)}, u32[]{:S(2)}, u32[]{:S(2)}) %collective-permute-start.28) | collective-permute-done | bytes 1572896 | tf_op jit(solution)/shard_map/ppermute | solution.py:153
  320.7 17.0 %collective-permute-done.30.refs_3_ = bf16[192,2048]{1,0:T(8,128)(2,1)} collective-permute-done((bf16[192,2048]{1,0:T(8,128)(2,1)}, bf16[192,2048]{1,0:T(8,128)(2,1)}, u32[]{:S(2)}, u32[]{:S(2)}) %collective-permute-start.30) | collective-permute-done | bytes 786464 | tf_op jit(solution)/shard_map/ppermute | solution.py:153
  337.6 17.0 %collective-permute-done.31.refs_4_ = bf16[192,2048]{1,0:T(8,128)(2,1)} collective-permute-done((bf16[192,2048]{1,0:T(8,128)(2,1)}, bf16[192,2048]{1,0:T(8,128)(2,1)}, u32[]{:S(2)}, u32[]{:S(2)}) %collective-permute-start.31) | collective-permute-done | bytes 786464 | tf_op jit(solution)/shard_map/ppermute | solution.py:153
  377.6 12.2 attention_forward.1.left_ref
  390.4 23.6 %collective-permute-done.33.refs_1_ = bf16[2,4,48,3072]{3,2,1,0:T(8,128)(2,1)} collective-permute-done((bf16[2,4,48,3072]{3,2,1,0:T(8,128)(2,1)}, bf16[2,4,48,3072]{3,2,1,0:T(8,128)(2,1)}, u32[]{:S(2)}, u32[]{:S(2)}) %collective-permute-start.33) | collective-permute-done | bytes 2359328 | tf_op jit(solution)/shard_map/ppermute | solution.py:153
  414.0 10.5 collective-permute-done.37.refs_5_.refs_2_
  439.1 7.1 collective-permute-done.48
  451.8 13.1 %sort_copies.11 = (bf16[2,4,4,1,48,3072]{5,4,3,2,1,0:T(8,128)(2,1)}, bf16[2,4,4,2,48,1536]{5,4,3,2,1,0:T(8,128)(2,1)}) custom-call(bf16[2,4,48,3072]{3,2,1,0:T(8,128)(2,1)S(1)} %pad_maximum_fusion.4.refs_0_, bf16[2,4,48,3072]{3,2,1,0:T(8,128)(2,1)} %collective-permute-done.33.refs_1_, bf16[2,4,48,3072]{3,2,1,0:T(8,128)(2,1)} %collective-permute-done.34.refs_2_, ...), custom_call_target="tpu_custom_call" | custom-call | tf_op jit(solution)/shard_map/sort_copies/pallas_call | solution.py:195
  465.0 10.7 multiply_convert_fusion.3
  483.9 22.3 %collective-permute-done.40.refs_1_ = bf16[384,1536]{1,0:T(8,128)(2,1)S(1)} collective-permute-done((bf16[384,1536]{1,0:T(8,128)(2,1)}, bf16[384,1536]{1,0:T(8,128)(2,1)S(1)}, u32[]{:S(2)}, u32[]{:S(2)}) %collective-permute-start.40) | collective-permute-done | bytes 1179680 | tf_op jit(solution)/shard_map/ppermute | solution.py:153
  515.5 7.6 collective-permute-done.42.refs_3_
  528.2 13.7 %multiply_convert_fusion.1 = (bf16[896,3072]{1,0:T(8,128)(2,1)}, f32[896,3072]{1,0:T(8,128)}) fusion(f32[3072]{0:T(1024)S(1)} %copy-done.172, bf16[896,1536]{1,0:T(8,128)(2,1)S(1)} %constant_dynamic-slice_fusion.39.left_ref, bf16[1536,3072]{1,0:T(8,128)(2,1)S(1)} %bitcast.625), kind=kOutput, calls=%fused_computation.11 | convolution fusion | flops 8483241984 | bytes 28717056 | tf_op jit(solution)/shard_map/dot_general | solution.py:578
  555.8 8.9 broadcast_select_fusion.1
  571.0 8.9 multiply_convert_fusion.4
  581.0 18.9 %multiply_convert_fusion.refs_0_ = bf16[896,3072]{1,0:T(8,128)(2,1)S(1)} fusion(bf16[896,3072]{1,0:T(8,128)(2,1)} %collective-permute-done.53, f32[896,3072]{1,0:T(8,128)} %get-tuple-element.316, f32[3072]{0:T(1024)S(1)} %copy-done.172, pred[]{:T(512)S(6)} %eq.8, bf16[3072,1024]{1,0:T(8,128)(2,1)} %bitcast.673, ...), kind=kOutput, calls=%fused_computation.10 | convolution fusion | flops 5709627392 | bytes 30158848 | tf_op jit(solution)/shard_map/dot_general | solution.py:582
  599.9 13.3 %convolution_convert_fusion.1.x_ref = bf16[896,1536]{1,0:T(8,128)(2,1)S(1)} fusion(bf16[896,3072]{1,0:T(8,128)(2,1)S(1)} %multiply_convert_fusion.refs_0_, bf16[1536,3072]{1,0:T(8,128)(2,1)} %bitcast.626), kind=kOutput, calls=%fused_computation.41 | convolution fusion | flops 8457093120 | bytes 17694720 | tf_op jit(solution)/shard_map/dot_general | solution.py:582
  624.7 7.2 outer_half.12.refs_2_
  643.2 12.0 tracks_grad.1
  655.2 7.5 collective-permute-done.54
  671.6 13.4 %collective-permute-done.55.refs_0_ = bf16[192,1536]{1,0:T(8,128)(2,1)S(1)} collective-permute-done((bf16[192,1536]{1,0:T(8,128)(2,1)}, bf16[192,1536]{1,0:T(8,128)(2,1)S(1)}, u32[]{:S(2)}, u32[]{:S(2)}) %collective-permute-start.55) | collective-permute-done | bytes 589856 | tf_op jit(solution)/shard_map/ppermute | solution.py:153
  688.6 8.8 outer_half.13
  717.7 11.5 collective-permute-done.63
  732.3 13.4 %collective-permute-done.64 = bf16[4,2,48,1536]{3,2,0,1:T(8,128)(2,1)} collective-permute-done((bf16[4,2,48,1536]{3,2,0,1:T(8,128)(2,1)}, bf16[4,2,48,1536]{3,2,0,1:T(8,128)(2,1)}, u32[]{:S(2)}, u32[]{:S(2)}) %collective-permute-start.64) | collective-permute-done | bytes 1179680 | tf_op jit(solution)/shard_map/ppermute | solution.py:153
  749.7 13.1 %multiply_convert_fusion.2.refs_0_ = bf16[384,3072]{1,0:T(8,128)(2,1)} fusion(bf16[384,1536]{1,0:T(8,128)(2,1)S(1)} %get-tuple-element.143.right_ref, bf16[3072,1536]{1,0:T(8,128)(2,1)} %bitcast.725, f32[384,3072]{1,0:T(8,128)} %get-tuple-element.314), kind=kOutput, calls=%fused_computation.37 | convolution fusion | flops 3648651264 | bytes 17694720 | tf_op jit(solution)/shard_map/dot_general | solution.py:582
  766.3 6.2 outer_half.15
  789.5 10.2 multiply_reduce_fusion
  807.8 7.1 collective-permute-done.68
  839.8 29.1 %attention_backward.1 = (bf16[384,512]{1,0:T(8,128)(2,1)}, bf16[1536,2048]{1,0:T(8,128)(2,1)}, f32[4,2,1920]{2,1,0:T(2,128)}) custom-call(bf16[384,512]{1,0:T(8,128)(2,1)} %copy-done.49, bf16[1536,2048]{1,0:T(8,128)(2,1)} %bitcast.593, f32[4,2,1920]{2,1,0:T(2,128)} %copy-done.55, bf16[384,1536]{1,0:T(8,128)(2,1)} %tie.64.g_ref), custom_call_target="tpu_custom_call" | custom-call | tf_op jit(solution)/shard_map/attention_backward/pallas_call | solution.py:128
  886.4 8.4 collective-permute-done.76
  896.0 29.5 %collective-permute-done.77 = bf16[4,48,1536]{2,1,0:T(8,128)(2,1)S(1)} collective-permute-done((bf16[4,48,1536]{2,1,0:T(8,128)(2,1)S(1)}, bf16[4,48,1536]{2,1,0:T(8,128)(2,1)S(1)}, u32[]{:S(2)}, u32[]{:S(2)}) %collective-permute-start.77) | collective-permute-done | bytes 589856 | tf_op jit(solution)/shard_map/ppermute | solution.py:153
  938.2 12.7 collective-permute-done.78.refs_0_
  982.6 6.3 collective-permute-done.61
  988.9 9.1 collective-permute-done.60
  1041.0 11.7 outer_half.22.refs_1_
  1065.6 16.0 %conv_back.1.refs_0_.refs_1_ = bf16[1536,1536]{1,0:T(8,128)(2,1)S(1)} custom-call(bf16[1536,1920]{1,0:T(8,128)(2,1)S(1)} %copy-done.5, bf16[5,1536,384]{2,1,0:T(8,128)(2,1)} %bitcast.614), custom_call_target="tpu_custom_call" | custom-call | tf_op jit(solution)/shard_map/conv_back/pallas_call | solution.py:391
  1087.4 15.2 %outer_half.23 = bf16[3840,384]{1,0:T(8,128)(2,1)} custom-call(s32[1]{0:T(128)} %bitcast.184.base_ref, bf16[1536,1536]{1,0:T(8,128)(2,1)S(1)} %bitcast.600, bf16[1536,1920]{1,0:T(8,128)(2,1)} %tie.76.right_ref, bf16[3840,384]{1,0:T(8,128)(2,1)} %collective-permute-done.99.refs_0_), custom_call_target="tpu_custom_call" | custom-call | tf_op jit(solution)/shard_map/outer_half/pallas_call | solution.py:422
  1120.2 13.6 %collective-permute-done.88 = bf16[4,48,2048]{2,1,0:T(8,128)(2,1)} collective-permute-done((bf16[4,48,2048]{2,1,0:T(8,128)(2,1)}, bf16[4,48,2048]{2,1,0:T(8,128)(2,1)}, u32[]{:S(2)}, u32[]{:S(2)}) %collective-permute-start.88) | collective-permute-done | bytes 786464 | tf_op jit(solution)/shard_map/ppermute | solution.py:153
  1138.8 19.0 %collective-permute-done.90 = bf16[2,192,1536]{2,1,0:T(8,128)(2,1)S(1)} collective-permute-done((bf16[2,192,1536]{2,1,0:T(8,128)(2,1)S(1)}, bf16[2,192,1536]{2,1,0:T(8,128)(2,1)S(1)}, u32[]{:S(2)}, u32[]{:S(2)}) %collective-permute-start.90) | collective-permute-done | bytes 1179680 | tf_op jit(solution)/shard_map/ppermute | solution.py:153
  1188.9 9.4 collective-permute-done.104
  (978 shorter events, 611.5 us)
Async XLA Ops:
  7.3 138.0 %all-gather.11.cloned.1.call-start = ((), (), s32[]{:S(2)}) async-start(), calls=%async_computation.9 | async-start | bytes 1966080 | tf_op jit(solution)/shard_map/all_gather | solution.py:686
  28.7 146.9 %all-gather.9.cloned.1.call-start = ((), (), s32[]{:S(2)}) async-start(), calls=%async_computation.8 | async-start | bytes 3686400 | tf_op jit(solution)/shard_map/all_gather | solution.py:642
  74.8 199.5 %all-gather.13.cloned.1.call-start = ((), (), s32[]{:S(2)}) async-start(), calls=%async_computation.10 | async-start | bytes 4423680 | tf_op jit(solution)/shard_map/all_gather | solution.py:691
  80.8 47.2 %collective-permute-start.6 = (bf16[384,1536]{1,0:T(8,128)(2,1)S(1)}, bf16[384,1536]{1,0:T(8,128)(2,1)S(1)}, u32[]{:S(2)}, u32[]{:S(2)}) collective-permute-start(bf16[384,1536]{1,0:T(8,128)(2,1)S(1)} %fusion.44.refs_0_), channel_id=1, source_target_pairs={{0,2},{1,3},{2,0},{3,1},{4,6},{5,7},{6,4},{7,5},{8,10},{9,11},{10,... | collective-permute-start | bytes 3538952 | tf_op jit(solution)/shard_map/ppermute | solution.py:153
  83.5 45.4 %collective-permute-start.10 = (bf16[416,1024]{1,0:T(8,128)(2,1)S(1)}, bf16[416,1024]{1,0:T(8,128)(2,1)S(1)}, u32[]{:S(2)}, u32[]{:S(2)}) collective-permute-start(bf16[416,1024]{1,0:T(8,128)(2,1)S(1)} %get-tuple-element.200), channel_id=1, source_target_pairs={{0,3},{1,2},{2,1},{3,0},{4,7},{5,6},{6,5},{7,4},{8,11},{9,10},{10,... | collective-permute-start | bytes 2555912 | tf_op jit(solution)/shard_map/ppermute | solution.py:153
  85.2 55.2 %collective-permute-start.9 = (bf16[416,1024]{1,0:T(8,128)(2,1)S(1)}, bf16[416,1024]{1,0:T(8,128)(2,1)S(1)}, u32[]{:S(2)}, u32[]{:S(2)}) collective-permute-start(bf16[416,1024]{1,0:T(8,128)(2,1)S(1)} %get-tuple-element.199), channel_id=1, source_target_pairs={{0,2},{1,3},{2,0},{3,1},{4,6},{5,7},{6,4},{7,5},{8,10},{9,11},{10,... | collective-permute-start | bytes 2555912 | tf_op jit(solution)/shard_map/ppermute | solution.py:153
  85.7 54.8 %collective-permute-start.8 = (bf16[416,1024]{1,0:T(8,128)(2,1)S(1)}, bf16[416,1024]{1,0:T(8,128)(2,1)S(1)}, u32[]{:S(2)}, u32[]{:S(2)}) collective-permute-start(bf16[416,1024]{1,0:T(8,128)(2,1)S(1)} %get-tuple-element.198), channel_id=1, source_target_pairs={{0,1},{1,0},{2,3},{3,2},{4,5},{5,4},{6,7},{7,6},{8,9},{9,8},{10,11... | collective-permute-start | bytes 2555912 | tf_op jit(solution)/shard_map/ppermute | solution.py:153
  175.7 39.5 %collective-permute-start.16 = (bf16[4,4,240,384]{3,2,1,0:T(8,128)(2,1)}, bf16[4,4,240,384]{3,2,1,0:T(8,128)(2,1)}, u32[]{:S(2)}, u32[]{:S(2)}) collective-permute-start(bf16[4,4,240,384]{3,2,1,0:T(8,128)(2,1)} %bitcast.628), channel_id=1, source_target_pairs={{0,16},{16,0},{1,17},{17,1},{2,18},{18,2},{3,19},{19,3},{4,20},{20... | collective-permute-start | bytes 8847368 | tf_op jit(solution)/shard_map/ppermute | solution.py:157
  180.9 34.2 %collective-permute-start.25 = (bf16[2,4,48,2048]{3,2,1,0:T(8,128)(2,1)S(1)}, bf16[2,4,48,2048]{3,2,1,0:T(8,128)(2,1)}, u32[]{:S(2)}, u32[]{:S(2)}) collective-permute-start(bf16[2,4,48,2048]{3,2,1,0:T(8,128)(2,1)S(1)} %pad_maximum_fusion.17.refs_4_), channel_id=1, source_target_pairs={{0,1},{1,0},{2,3},{3,2},{4,5},{5,4},{6,7},{7,6},{8,9},{9,8},{10,11... | collective-permute-start | bytes 4718600 | tf_op jit(solution)/shard_map/ppermute | solution.py:153
  185.8 53.1 %collective-permute-start.22 = (bf16[2,4,48,2048]{3,2,1,0:T(8,128)(2,1)S(1)}, bf16[2,4,48,2048]{3,2,1,0:T(8,128)(2,1)}, u32[]{:S(2)}, u32[]{:S(2)}) collective-permute-start(bf16[2,4,48,2048]{3,2,1,0:T(8,128)(2,1)S(1)} %pad_maximum_fusion.16.refs_0_), channel_id=1, source_target_pairs={{0,16},{16,0},{1,17},{17,1},{2,18},{18,2},{3,19},{19,3},{4,20},{20... | collective-permute-start | bytes 4718600 | tf_op jit(solution)/shard_map/ppermute | solution.py:157
  185.9 53.3 %collective-permute-start.26 = (bf16[2,4,48,2048]{3,2,1,0:T(8,128)(2,1)S(1)}, bf16[2,4,48,2048]{3,2,1,0:T(8,128)(2,1)}, u32[]{:S(2)}, u32[]{:S(2)}) collective-permute-start(bf16[2,4,48,2048]{3,2,1,0:T(8,128)(2,1)S(1)} %pad_maximum_fusion.17.refs_4_), channel_id=1, source_target_pairs={{0,16},{16,0},{1,17},{17,1},{2,18},{18,2},{3,19},{19,3},{4,20},{20... | collective-permute-start | bytes 4718600 | tf_op jit(solution)/shard_map/ppermute | solution.py:157
  188.3 293.8 %all-gather.15.cloned.1.call-start = ((), (), s32[]{:S(2)}) async-start(), calls=%async_computation.11 | async-start | bytes 7864320 | tf_op jit(solution)/shard_map/all_gather | solution.py:724
  207.2 33.5 %collective-permute-start.23 = (bf16[2,4,48,2048]{3,2,1,0:T(8,128)(2,1)}, bf16[2,4,48,2048]{3,2,1,0:T(8,128)(2,1)S(1)}, u32[]{:S(2)}, u32[]{:S(2)}) collective-permute-start(bf16[2,4,48,2048]{3,2,1,0:T(8,128)(2,1)} %collective-permute-done.21.refs_1_), channel_id=1, source_target_pairs={{0,16},{16,0},{1,17},{17,1},{2,18},{18,2},{3,19},{19,3},{4,20},{20... | collective-permute-start | bytes 4718600 | tf_op jit(solution)/shard_map/ppermute | solution.py:157
  272.6 36.3 %collective-permute-start.28 = (bf16[384,2048]{1,0:T(8,128)(2,1)}, bf16[384,2048]{1,0:T(8,128)(2,1)S(1)}, u32[]{:S(2)}, u32[]{:S(2)}) collective-permute-start(bf16[384,2048]{1,0:T(8,128)(2,1)} %convolution_convert_fusion.3.refs_0_), channel_id=1, source_target_pairs={{0,1},{1,0},{2,3},{3,2},{4,5},{5,4},{6,7},{7,6},{8,9},{9,8},{10,11... | collective-permute-start | bytes 4718600 | tf_op jit(solution)/shard_map/ppermute | solution.py:153
  272.9 36.3 %collective-permute-start.29 = (bf16[384,2048]{1,0:T(8,128)(2,1)}, bf16[384,2048]{1,0:T(8,128)(2,1)S(1)}, u32[]{:S(2)}, u32[]{:S(2)}) collective-permute-start(bf16[384,2048]{1,0:T(8,128)(2,1)} %convolution_convert_fusion.3.refs_0_), channel_id=1, source_target_pairs={{0,2},{1,3},{2,0},{3,1},{4,6},{5,7},{6,4},{7,5},{8,10},{9,11},{10,... | collective-permute-start | bytes 4718600 | tf_op jit(solution)/shard_map/ppermute | solution.py:153
  310.6 48.9 %collective-permute-start.32 = (bf16[4,48,3072]{2,1,0:T(8,128)(2,1)}, bf16[4,48,3072]{2,1,0:T(8,128)(2,1)}, u32[]{:S(2)}, u32[]{:S(2)}) collective-permute-start(bf16[4,48,3072]{2,1,0:T(8,128)(2,1)} %tie.46), channel_id=1, source_target_pairs={{0,1},{1,0},{2,3},{3,2},{4,5},{5,4},{6,7},{7,6},{8,9},{9,8},{10,11... | collective-permute-start | bytes 3538952 | tf_op jit(solution)/shard_map/ppermute | solution.py:153
  314.5 618.9 %reduce-scatter.5.cloned.1.call-start = ((), (), s32[]{:S(2)}) async-start(), calls=%async_computation.4 | async-start | bytes 7864320 | tf_op jit(solution)/shard_map/reduce_scatter | solution.py:812
  318.7 35.9 %collective-permute-start.31 = (bf16[192,2048]{1,0:T(8,128)(2,1)}, bf16[192,2048]{1,0:T(8,128)(2,1)}, u32[]{:S(2)}, u32[]{:S(2)}) collective-permute-start(bf16[192,2048]{1,0:T(8,128)(2,1)} %slice.397), channel_id=1, source_target_pairs={{0,1},{1,0},{2,3},{3,2},{4,5},{5,4},{6,7},{7,6},{8,9},{9,8},{10,11... | collective-permute-start | bytes 2359304 | tf_op jit(solution)/shard_map/ppermute | solution.py:153
  319.9 43.9 %collective-permute-start.36 = (bf16[4,48,3072]{2,1,0:T(8,128)(2,1)}, bf16[4,48,3072]{2,1,0:T(8,128)(2,1)}, u32[]{:S(2)}, u32[]{:S(2)}) collective-permute-start(bf16[4,48,3072]{2,1,0:T(8,128)(2,1)} %tie.48), channel_id=1, source_target_pairs={{0,2},{1,3},{2,0},{3,1},{4,6},{5,7},{6,4},{7,5},{8,10},{9,11},{10,... | collective-permute-start | bytes 3538952 | tf_op jit(solution)/shard_map/ppermute | solution.py:153
  362.5 51.5 %collective-permute-start.33 = (bf16[2,4,48,3072]{3,2,1,0:T(8,128)(2,1)}, bf16[2,4,48,3072]{3,2,1,0:T(8,128)(2,1)}, u32[]{:S(2)}, u32[]{:S(2)}) collective-permute-start(bf16[2,4,48,3072]{3,2,1,0:T(8,128)(2,1)} %tie.47), channel_id=1, source_target_pairs={{0,2},{1,3},{2,0},{3,1},{4,6},{5,7},{6,4},{7,5},{8,10},{9,11},{10,... | collective-permute-start | bytes 7077896 | tf_op jit(solution)/shard_map/ppermute | solution.py:153
  369.9 54.6 %collective-permute-start.37 = (bf16[2,4,48,3072]{3,2,1,0:T(8,128)(2,1)}, bf16[2,4,48,3072]{3,2,1,0:T(8,128)(2,1)}, u32[]{:S(2)}, u32[]{:S(2)}) collective-permute-start(bf16[2,4,48,3072]{3,2,1,0:T(8,128)(2,1)} %tie.49), channel_id=1, source_target_pairs={{0,1},{1,0},{2,3},{3,2},{4,5},{5,4},{6,7},{7,6},{8,9},{9,8},{10,11... | collective-permute-start | bytes 7077896 | tf_op jit(solution)/shard_map/ppermute | solution.py:153
  376.6 57.4 %collective-permute-start.44 = (bf16[4,48,1536]{2,1,0:T(8,128)(2,1)}, bf16[4,48,1536]{2,1,0:T(8,128)(2,1)S(1)}, u32[]{:S(2)}, u32[]{:S(2)}) collective-permute-start(bf16[4,48,1536]{2,1,0:T(8,128)(2,1)} %tie.52), channel_id=1, source_target_pairs={{0,1},{1,0},{2,3},{3,2},{4,5},{5,4},{6,7},{7,6},{8,9},{9,8},{10,11... | collective-permute-start | bytes 1769480 | tf_op jit(solution)/shard_map/ppermute | solution.py:153
  389.8 60.2 %collective-permute-start.34 = (bf16[2,4,48,3072]{3,2,1,0:T(8,128)(2,1)S(1)}, bf16[2,4,48,3072]{3,2,1,0:T(8,128)(2,1)}, u32[]{:S(2)}, u32[]{:S(2)}) collective-permute-start(bf16[2,4,48,3072]{3,2,1,0:T(8,128)(2,1)S(1)} %pad_maximum_fusion.4.refs_0_), channel_id=1, source_target_pairs={{0,16},{16,0},{1,17},{17,1},{2,18},{18,2},{3,19},{19,3},{4,20},{20... | collective-permute-start | bytes 7077896 | tf_op jit(solution)/shard_map/ppermute | solution.py:157
  389.9 61.9 %collective-permute-start.38 = (bf16[2,4,48,3072]{3,2,1,0:T(8,128)(2,1)}, bf16[2,4,48,3072]{3,2,1,0:T(8,128)(2,1)}, u32[]{:S(2)}, u32[]{:S(2)}) collective-permute-start(bf16[2,4,48,3072]{3,2,1,0:T(8,128)(2,1)} %pad_maximum_fusion.5.refs_4_), channel_id=1, source_target_pairs={{0,16},{16,0},{1,17},{17,1},{2,18},{18,2},{3,19},{19,3},{4,20},{20... | collective-permute-start | bytes 7077896 | tf_op jit(solution)/shard_map/ppermute | solution.py:157
  414.0 37.9 %collective-permute-start.35 = (bf16[2,4,48,3072]{3,2,1,0:T(8,128)(2,1)}, bf16[2,4,48,3072]{3,2,1,0:T(8,128)(2,1)}, u32[]{:S(2)}, u32[]{:S(2)}) collective-permute-start(bf16[2,4,48,3072]{3,2,1,0:T(8,128)(2,1)} %collective-permute-done.33.refs_1_), channel_id=1, source_target_pairs={{0,16},{16,0},{1,17},{17,1},{2,18},{18,2},{3,19},{19,3},{4,20},{20... | collective-permute-start | bytes 7077896 | tf_op jit(solution)/shard_map/ppermute | solution.py:157
  448.4 34.4 %collective-permute-start.45 = (bf16[2,4,48,1536]{3,2,1,0:T(8,128)(2,1)}, bf16[2,4,48,1536]{3,2,1,0:T(8,128)(2,1)}, u32[]{:S(2)}, u32[]{:S(2)}) collective-permute-start(bf16[2,4,48,1536]{3,2,1,0:T(8,128)(2,1)} %tie.53), channel_id=1, source_target_pairs={{0,2},{1,3},{2,0},{3,1},{4,6},{5,7},{6,4},{7,5},{8,10},{9,11},{10,... | collective-permute-start | bytes 3538952 | tf_op jit(solution)/shard_map/ppermute | solution.py:153
  450.0 33.4 %collective-permute-start.49 = (bf16[2,4,48,1536]{3,2,1,0:T(8,128)(2,1)}, bf16[2,4,48,1536]{3,2,1,0:T(8,128)(2,1)}, u32[]{:S(2)}, u32[]{:S(2)}) collective-permute-start(bf16[2,4,48,1536]{3,2,1,0:T(8,128)(2,1)} %tie.55), channel_id=1, source_target_pairs={{0,1},{1,0},{2,3},{3,2},{4,5},{5,4},{6,7},{7,6},{8,9},{9,8},{10,11... | collective-permute-start | bytes 3538952 | tf_op jit(solution)/shard_map/ppermute | solution.py:153
  631.9 56.7 %collective-permute-start.58 = (bf16[768,3072]{1,0:T(8,128)(2,1)}, bf16[768,3072]{1,0:T(8,128)(2,1)}, u32[]{:S(2)}, u32[]{:S(2)}) collective-permute-start(bf16[768,3072]{1,0:T(8,128)(2,1)} %outer_half.12.refs_2_), channel_id=1, source_target_pairs={{0,16},{16,0},{1,17},{17,1},{2,18},{18,2},{3,19},{19,3},{4,20},{20... | collective-permute-start | bytes 14155784 | tf_op jit(solution)/shard_map/ppermute | solution.py:157
  712.6 53.7 %collective-permute-start.62 = (bf16[1536,1536]{1,0:T(8,128)(2,1)}, bf16[1536,1536]{1,0:T(8,128)(2,1)}, u32[]{:S(2)}, u32[]{:S(2)}) collective-permute-start(bf16[1536,1536]{1,0:T(8,128)(2,1)} %outer_half.14), channel_id=1, source_target_pairs={{0,16},{16,0},{1,17},{17,1},{2,18},{18,2},{3,19},{19,3},{4,20},{20... | collective-permute-start | bytes 14155784 | tf_op jit(solution)/shard_map/ppermute | solution.py:157
  717.7 366.2 %reduce-scatter.11.cloned.1.call-start = ((), (), s32[]{:S(2)}) async-start(), calls=%async_computation.7 | async-start | bytes 4423680 | tf_op jit(solution)/shard_map/reduce_scatter | solution.py:856
  731.3 33.8 %collective-permute-start.66 = (bf16[4,48,1536]{2,1,0:T(8,128)(2,1)S(1)}, bf16[4,48,1536]{2,1,0:T(8,128)(2,1)S(1)}, u32[]{:S(2)}, u32[]{:S(2)}) collective-permute-start(bf16[4,48,1536]{2,1,0:T(8,128)(2,1)S(1)} %dynamic-slice_bitcast_fusion.15), channel_id=1, source_target_pairs={{0,2},{1,3},{2,0},{3,1},{4,6},{5,7},{6,4},{7,5},{8,10},{9,11},{10,... | collective-permute-start | bytes 1769480 | tf_op jit(solution)/shard_map/ppermute | solution.py:153
  748.2 33.8 %collective-permute-start.67 = (bf16[4,48,1536]{2,1,0:T(8,128)(2,1)}, bf16[4,48,1536]{2,1,0:T(8,128)(2,1)}, u32[]{:S(2)}, u32[]{:S(2)}) collective-permute-start(bf16[4,48,1536]{2,1,0:T(8,128)(2,1)} %dynamic-slice_bitcast_fusion.14), channel_id=1, source_target_pairs={{0,1},{1,0},{2,3},{3,2},{4,5},{5,4},{6,7},{7,6},{8,9},{9,8},{10,11... | collective-permute-start | bytes 1769480 | tf_op jit(solution)/shard_map/ppermute | solution.py:153
  782.0 37.7 %collective-permute-start.65 = (bf16[768,3072]{1,0:T(8,128)(2,1)}, bf16[768,3072]{1,0:T(8,128)(2,1)S(1)}, u32[]{:S(2)}, u32[]{:S(2)}) collective-permute-start(bf16[768,3072]{1,0:T(8,128)(2,1)} %outer_half.16), channel_id=1, source_target_pairs={{0,16},{16,0},{1,17},{17,1},{2,18},{18,2},{3,19},{19,3},{4,20},{20... | collective-permute-start | bytes 14155784 | tf_op jit(solution)/shard_map/ppermute | solution.py:157
  807.5 67.9 %collective-permute-start.70 = (bf16[768,1536]{1,0:T(8,128)(2,1)}, bf16[768,1536]{1,0:T(8,128)(2,1)}, u32[]{:S(2)}, u32[]{:S(2)}) collective-permute-start(bf16[768,1536]{1,0:T(8,128)(2,1)} %outer_half.18), channel_id=1, source_target_pairs={{0,16},{16,0},{1,17},{17,1},{2,18},{18,2},{3,19},{19,3},{4,20},{20... | collective-permute-start | bytes 7077896 | tf_op jit(solution)/shard_map/ppermute | solution.py:157
  827.7 41.2 %collective-permute-start.73 = (bf16[4,2,48,1536]{3,2,0,1:T(8,128)(2,1)}, bf16[4,2,48,1536]{3,2,0,1:T(8,128)(2,1)}, u32[]{:S(2)}, u32[]{:S(2)}) collective-permute-start(bf16[4,2,48,1536]{3,2,0,1:T(8,128)(2,1)} %bitcast.570), channel_id=1, source_target_pairs={{0,1},{1,0},{2,3},{3,2},{4,5},{5,4},{6,7},{7,6},{8,9},{9,8},{10,11... | collective-permute-start | bytes 3538952 | tf_op jit(solution)/shard_map/ppermute | solution.py:153
  831.6 40.1 %collective-permute-start.74 = (bf16[4,2,48,1536]{3,2,0,1:T(8,128)(2,1)}, bf16[4,2,48,1536]{3,2,0,1:T(8,128)(2,1)}, u32[]{:S(2)}, u32[]{:S(2)}) collective-permute-start(bf16[4,2,48,1536]{3,2,0,1:T(8,128)(2,1)} %bitcast.569), channel_id=1, source_target_pairs={{0,2},{1,3},{2,0},{3,1},{4,6},{5,7},{6,4},{7,5},{8,10},{9,11},{10,... | collective-permute-start | bytes 3538952 | tf_op jit(solution)/shard_map/ppermute | solution.py:153
  877.8 48.8 %collective-permute-start.75 = (bf16[2,192,2048]{2,1,0:T(8,128)(2,1)S(1)}, bf16[2,192,2048]{2,1,0:T(8,128)(2,1)S(1)}, u32[]{:S(2)}, u32[]{:S(2)}) collective-permute-start(bf16[2,192,2048]{2,1,0:T(8,128)(2,1)S(1)} %pad_maximum_fusion.18), channel_id=1, source_target_pairs={{0,1},{1,0},{2,3},{3,2},{4,5},{5,4},{6,7},{7,6},{8,9},{9,8},{10,11... | collective-permute-start | bytes 4718600 | tf_op jit(solution)/shard_map/ppermute | solution.py:153
  879.6 47.4 %collective-permute-start.79 = (bf16[2,192,2048]{2,1,0:T(8,128)(2,1)S(1)}, bf16[2,192,2048]{2,1,0:T(8,128)(2,1)S(1)}, u32[]{:S(2)}, u32[]{:S(2)}) collective-permute-start(bf16[2,192,2048]{2,1,0:T(8,128)(2,1)S(1)} %pad_maximum_fusion.19), channel_id=1, source_target_pairs={{0,2},{1,3},{2,0},{3,1},{4,6},{5,7},{6,4},{7,5},{8,10},{9,11},{10,... | collective-permute-start | bytes 4718600 | tf_op jit(solution)/shard_map/ppermute | solution.py:153
  880.8 44.6 %collective-permute-start.77 = (bf16[4,48,1536]{2,1,0:T(8,128)(2,1)S(1)}, bf16[4,48,1536]{2,1,0:T(8,128)(2,1)S(1)}, u32[]{:S(2)}, u32[]{:S(2)}) collective-permute-start(bf16[4,48,1536]{2,1,0:T(8,128)(2,1)S(1)} %dynamic-slice_bitcast_fusion.10), channel_id=1, source_target_pairs={{0,1},{1,0},{2,3},{3,2},{4,5},{5,4},{6,7},{7,6},{8,9},{9,8},{10,11... | collective-permute-start | bytes 1769480 | tf_op jit(solution)/shard_map/ppermute | solution.py:153
  967.1 38.9 %collective-permute-start.81 = (bf16[768,2560]{1,0:T(8,128)(2,1)}, bf16[768,2560]{1,0:T(8,128)(2,1)}, u32[]{:S(2)}, u32[]{:S(2)}) collective-permute-start(bf16[768,2560]{1,0:T(8,128)(2,1)} %outer_half.20), channel_id=1, source_target_pairs={{0,16},{16,0},{1,17},{17,1},{2,18},{18,2},{3,19},{19,3},{4,20},{20... | collective-permute-start | bytes 11796488 | tf_op jit(solution)/shard_map/ppermute | solution.py:157
  973.3 278.9 %reduce-scatter.7.cloned.1.call-start = ((), (), s32[]{:S(2)}) async-start(), calls=%async_computation.5 | async-start | bytes 3686400 | tf_op jit(solution)/shard_map/reduce_scatter | solution.py:899
  1052.7 32.4 %collective-permute-start.99 = (bf16[3840,384]{1,0:T(8,128)(2,1)}, bf16[3840,384]{1,0:T(8,128)(2,1)}, u32[]{:S(2)}, u32[]{:S(2)}) collective-permute-start(bf16[3840,384]{1,0:T(8,128)(2,1)} %outer_half.22.refs_1_), channel_id=1, source_target_pairs={{0,16},{16,0},{1,17},{17,1},{2,18},{18,2},{3,19},{19,3},{4,20},{20... | collective-permute-start | bytes 8847368 | tf_op jit(solution)/shard_map/ppermute | solution.py:157
  1055.4 49.4 %collective-permute-start.85 = (bf16[4,2,48,2048]{3,2,0,1:T(8,128)(2,1)}, bf16[4,2,48,2048]{3,2,0,1:T(8,128)(2,1)}, u32[]{:S(2)}, u32[]{:S(2)}) collective-permute-start(bf16[4,2,48,2048]{3,2,0,1:T(8,128)(2,1)} %bitcast.568), channel_id=1, source_target_pairs={{0,1},{1,0},{2,3},{3,2},{4,5},{5,4},{6,7},{7,6},{8,9},{9,8},{10,11... | collective-permute-start | bytes 4718600 | tf_op jit(solution)/shard_map/ppermute | solution.py:153
  1059.2 48.8 %collective-permute-start.86 = (bf16[4,2,48,2048]{3,2,0,1:T(8,128)(2,1)}, bf16[4,2,48,2048]{3,2,0,1:T(8,128)(2,1)}, u32[]{:S(2)}, u32[]{:S(2)}) collective-permute-start(bf16[4,2,48,2048]{3,2,0,1:T(8,128)(2,1)} %bitcast.567), channel_id=1, source_target_pairs={{0,2},{1,3},{2,0},{3,1},{4,6},{5,7},{6,4},{7,5},{8,10},{9,11},{10,... | collective-permute-start | bytes 4718600 | tf_op jit(solution)/shard_map/ppermute | solution.py:153
  1102.7 154.3 %reduce-scatter.9.cloned.1.call-start = ((), (), s32[]{:S(2)}) async-start(), calls=%async_computation.6 | async-start | bytes 1966080 | tf_op jit(solution)/shard_map/reduce_scatter | solution.py:896
  1116.2 41.6 %collective-permute-start.90 = (bf16[2,192,1536]{2,1,0:T(8,128)(2,1)S(1)}, bf16[2,192,1536]{2,1,0:T(8,128)(2,1)S(1)}, u32[]{:S(2)}, u32[]{:S(2)}) collective-permute-start(bf16[2,192,1536]{2,1,0:T(8,128)(2,1)S(1)} %pad_maximum_fusion.32), channel_id=1, source_target_pairs={{0,2},{1,3},{2,0},{3,1},{4,6},{5,7},{6,4},{7,5},{8,10},{9,11},{10,... | collective-permute-start | bytes 3538952 | tf_op jit(solution)/shard_map/ppermute | solution.py:153
  1118.5 42.6 %collective-permute-start.87 = (bf16[2,192,1536]{2,1,0:T(8,128)(2,1)S(1)}, bf16[2,192,1536]{2,1,0:T(8,128)(2,1)S(1)}, u32[]{:S(2)}, u32[]{:S(2)}) collective-permute-start(bf16[2,192,1536]{2,1,0:T(8,128)(2,1)S(1)} %pad_maximum_fusion.31), channel_id=1, source_target_pairs={{0,1},{1,0},{2,3},{3,2},{4,5},{5,4},{6,7},{7,6},{8,9},{9,8},{10,11... | collective-permute-start | bytes 3538952 | tf_op jit(solution)/shard_map/ppermute | solution.py:153
  1172.6 44.3 %collective-permute-start.91 = (bf16[4,224,512]{2,1,0:T(8,128)(2,1)}, bf16[4,224,512]{2,1,0:T(8,128)(2,1)}, u32[]{:S(2)}, u32[]{:S(2)}) collective-permute-start(bf16[4,224,512]{2,1,0:T(8,128)(2,1)} %get-tuple-element.223), channel_id=1, source_target_pairs={{16,0},{17,1},{18,2},{19,3},{20,4},{21,5},{22,6},{23,7},{24,8},{25... | collective-permute-start | bytes 2752520 | tf_op jit(solution)/shard_map/ppermute | solution.py:165
  (270 other events, 2881.0 us)
Sparse Core Ops, SparseCore 0:
  28.9 37.6 all-gather.10
  74.9 57.7 all-gather.8
  188.4 69.6 all-gather.12
  314.7 114.9 all-gather.14
  717.8 110.8 reduce-scatter.4
  973.4 65.8 reduce-scatter.10
  1102.8 56.8 reduce-scatter.6
  1169.3 35.4 reduce-scatter.8

commit v2 on v1

--- a/solution.py
+++ b/solution.py
@@ -1,3 +1,5 @@
+import functools
+
 import jax
 import jax.numpy as jnp
 from jax import lax
@@ -69,7 +71,7 @@
         out_shape=jax.ShapeDtypeStruct((rows, pairs * 2 * V), jnp.bfloat16),
         compiler_params=pltpu.CompilerParams(vmem_limit_bytes=48 * 2**20),
         cost_estimate=pl.CostEstimate(
-            flops=0, bytes_accessed=0, transcendentals=0
+            flops=14_000_000_000, bytes_accessed=0, transcendentals=0
         ),
         name="attention_forward",
     )(q, kv, u)
@@ -142,7 +144,7 @@
         ],
         compiler_params=pltpu.CompilerParams(vmem_limit_bytes=56 * 2**20),
         cost_estimate=pl.CostEstimate(
-            flops=0, bytes_accessed=0, transcendentals=0
+            flops=32_000_000_000, bytes_accessed=0, transcendentals=0
         ),
         name="attention_backward",
     )(q, kv, u, g)
@@ -200,7 +202,7 @@
         scratch_shapes=[pltpu.VMEM(x.shape, x.dtype) for x in out_shapes]
         + [pltpu.SemaphoreType.DMA((count,))] * 2,
         compiler_params=pltpu.CompilerParams(vmem_limit_bytes=held * 2 + 4 * 2**20),
-        cost_estimate=pl.CostEstimate(flops=0, bytes_accessed=0, transcendentals=0),
+        cost_estimate=pl.CostEstimate(flops=0, bytes_accessed=held * 4, transcendentals=0),
         name="sort_copies",
     )(*pieces)
 
@@ -339,7 +341,7 @@
         out_specs=pl.BlockSpec((TILE, 2 * BLOCK), lambda i: (i, 0)),
         out_shape=jax.ShapeDtypeStruct((hidden, 2 * BLOCK), jnp.bfloat16),
         compiler_params=pltpu.CompilerParams(vmem_limit_bytes=32 * 2**20),
-        cost_estimate=pl.CostEstimate(flops=0, bytes_accessed=0, transcendentals=0),
+        cost_estimate=pl.CostEstimate(flops=4 * rows * hidden * 2 * BLOCK, bytes_accessed=0, transcendentals=0),
         name="tracks_grad",
     )(first, second, g)
 
@@ -367,7 +369,7 @@
         out_specs=pl.BlockSpec(memory_space=pltpu.VMEM),
         scratch_shapes=[pltpu.VMEM((length + 16, outputs), jnp.float32)],
         compiler_params=pltpu.CompilerParams(vmem_limit_bytes=40 * 2**20),
-        cost_estimate=pl.CostEstimate(flops=0, bytes_accessed=0, transcendentals=0),
+        cost_estimate=pl.CostEstimate(flops=3 * length * w.size, bytes_accessed=0, transcendentals=0),
         name="conv_forward",
     )(x, w)
 
@@ -398,7 +400,7 @@
         out_specs=pl.BlockSpec((TILE, chans), lambda i: (i, 0)),
         out_shape=jax.ShapeDtypeStruct((length, chans), jnp.bfloat16),
         compiler_params=pltpu.CompilerParams(vmem_limit_bytes=40 * 2**20),
-        cost_estimate=pl.CostEstimate(flops=0, bytes_accessed=0, transcendentals=0),
+        cost_estimate=pl.CostEstimate(flops=3 * length * w.size, bytes_accessed=0, transcendentals=0),
         name="conv_back",
     )(g, w)
 
@@ -433,7 +435,7 @@
         ),
         out_shape=jax.ShapeDtypeStruct((count * TILE, columns), jnp.bfloat16),
         compiler_params=pltpu.CompilerParams(vmem_limit_bytes=40 * 2**20),
-        cost_estimate=pl.CostEstimate(flops=0, bytes_accessed=0, transcendentals=0),
+        cost_estimate=pl.CostEstimate(flops=3 * rows * count * TILE * columns, bytes_accessed=0, transcendentals=0),
         name="outer_half",
     )(base, left, right, *([] if more is None else [more]))
 
@@ -443,18 +445,18 @@
     return total.reshape(peers, 2, 2, total.shape[0] // (4 * peers), total.shape[1])
 
 
-def fold(half, bit):
+def fold(half, bit, after=()):
     axis = 2 if bit == 1 and half.ndim == 5 else 1
     here = lax.rem(lax.div(lax.axis_index("seq"), bit), 2)
-    away = flip(pick(half, 1 - here, axis), bit)
+    away = tie(flip(pick(half, 1 - here, axis), bit), *after)
     return (pick(half, here, axis).astype(jnp.float32) + away.astype(jnp.float32)).astype(half.dtype)
 
 
-def fold_both(grads, steps):
+def fold_both(grads, steps, after=()):
     if steps == 0:
         middle = grads.shape[-1] // 2
-        return fold(grads[..., :middle], 1), fold(grads[..., middle:], 2)
-    return fold(grads[0], 2), fold(grads[1], 1)
+        return fold(grads[..., :middle], 1, after), fold(grads[..., middle:], 2, after)
+    return fold(grads[0], 2, after), fold(grads[1], 1, after)
 
 
 def gather_begin(x):
@@ -515,10 +517,10 @@
     return jnp.concatenate([a + b.astype(jnp.float32) for a, b in zip(mine, arrived)], axis=0)
 
 
-def exchange_plane(x):
+def exchange_plane(x, after=()):
     place = lax.axis_index("seq")
     arrived = [pick(x, place)] + [
-        flip(pick(x, lax.bitwise_xor(place, bit)), bit) for bit in (1, 2, 3)
+        tie(flip(pick(x, lax.bitwise_xor(place, bit)), bit), *after) for bit in (1, 2, 3)
     ]
     stacked = jnp.stack(arrived)
     return jnp.stack([pick(stacked, lax.bitwise_xor(place, j)) for j in range(4)])
@@ -539,27 +541,96 @@
     return x
 
 
-def spread_tracks(x):
-    rows = x.shape[0]
-    lower = lax.axis_index("species") == 0
-    human = jnp.pad(x, ((0, 0), (0, 12 * BLOCK - x.shape[1]))).reshape(rows, 4, 3, BLOCK)
-    human = human.transpose(1, 2, 0, 3)
-    mouse = x[:, : 4 * BLOCK].reshape(rows, 4, BLOCK).transpose(1, 0, 2)
-    other = to_upper_core(human[:, 2])
-    first = jnp.where(lower, human[:, 0], other)
-    second = jnp.where(lower, human[:, 1], mouse)
-    return jnp.concatenate([first, second], axis=-1)
-
-
-def collect_tracks(x, tracks):
-    rows = x.shape[1]
-    lower = lax.axis_index("species") == 0
+def cut_tracks_kernel(steps, upper_ref, lower_ref, sent_ref, human_ref, mouse_ref):
+    x = jnp.where(pl.program_id(0) < steps, upper_ref[...], lower_ref[...])
+    tracks = x.shape[1]
+
+    def columns(block):
+        begin = block * BLOCK
+        end = min(begin + BLOCK, tracks)
+        if end <= begin:
+            return jnp.zeros((x.shape[0], BLOCK), x.dtype)
+        part = x[:, begin:end]
+        if end < begin + BLOCK:
+            part = jnp.concatenate(
+                [part, jnp.zeros((x.shape[0], begin + BLOCK - end), x.dtype)], axis=1
+            )
+        return part
+
+    for chip in range(4):
+        human_ref[chip] = jnp.concatenate([columns(3 * chip), columns(3 * chip + 1)], axis=1)
+        sent_ref[chip] = columns(3 * chip + 2)
+        mouse_ref[chip] = columns(chip)
+
+
+def spread_tracks(upper, lower):
+    step = 16
+    steps, more = upper.shape[0] // step, lower.shape[0] // step
+    rows, tracks = upper.shape[0] + lower.shape[0], upper.shape[1]
+    specs = [
+        pl.BlockSpec((4, step, width), lambda i: (0, i, 0)) for width in (BLOCK, 2 * BLOCK, BLOCK)
+    ]
+    sent, human, mouse = pl.pallas_call(
+        functools.partial(cut_tracks_kernel, steps),
+        grid=(steps + more,),
+        in_specs=[
+            pl.BlockSpec((step, tracks), lambda i: (jnp.minimum(i, steps - 1), 0)),
+            pl.BlockSpec((step, tracks), lambda i: (jnp.maximum(i - steps, 0), 0)),
+        ],
+        out_specs=specs,
+        out_shape=[
+            jax.ShapeDtypeStruct((4, rows, width), upper.dtype) for width in (BLOCK, 2 * BLOCK, BLOCK)
+        ],
+        compiler_params=pltpu.CompilerParams(vmem_limit_bytes=32 * 2**20),
+        cost_estimate=pl.CostEstimate(flops=0, bytes_accessed=0, transcendentals=0),
+        name="cut_tracks",
+    )(upper, lower)
+    other = to_upper_core(sent)
+    return jnp.where(
+        lax.axis_index("species") == 0, human, jnp.concatenate([other, mouse], axis=-1)
+    )
+
+
+def join_tracks_kernel(core_ref, x_ref, other_ref, o_ref):
+    tracks = o_ref.shape[1]
+
+    def put(block, value):
+        begin = block * BLOCK
+        width = min(BLOCK, tracks - begin)
+        if width > 0:
+            o_ref[:, begin : begin + width] = value[:, :width].astype(o_ref.dtype)
+
+    @pl.when(core_ref[0] == 0)
+    def _():
+        for chip in range(4):
+            put(3 * chip, x_ref[chip, :, :BLOCK])
+            put(3 * chip + 1, x_ref[chip, :, BLOCK:])
+            put(3 * chip + 2, other_ref[chip])
+
+    @pl.when(core_ref[0] != 0)
+    def _():
+        o_ref[...] = jnp.zeros_like(o_ref)
+        for chip in range(4):
+            put(chip, x_ref[chip, :, BLOCK:])
+
+
+def collect_tracks(x, tracks, dtype):
+    rows, step = x.shape[1], 16
     other = to_lower_core(x[:, :, :BLOCK])
-    human = jnp.stack([x[:, :, :BLOCK], x[:, :, BLOCK:], other], axis=1)
-    human = human.transpose(2, 0, 1, 3).reshape(rows, 12 * BLOCK)[:, :tracks]
-    mouse = x[:, :, BLOCK:].transpose(1, 0, 2).reshape(rows, 4 * BLOCK)
-    mouse = jnp.pad(mouse, ((0, 0), (0, tracks - 4 * BLOCK)))
-    return jnp.where(lower, human, mouse)
+    return pl.pallas_call(
+        join_tracks_kernel,
+        grid=(rows // step,),
+        in_specs=[
+            pl.BlockSpec(memory_space=pltpu.SMEM),
+            pl.BlockSpec((4, step, 2 * BLOCK), lambda i: (0, i, 0)),
+            pl.BlockSpec((4, step, BLOCK), lambda i: (0, i, 0)),
+        ],
+        out_specs=pl.BlockSpec((step, tracks), lambda i: (i, 0)),
+        out_shape=jax.ShapeDtypeStruct((rows, tracks), dtype),
+        compiler_params=pltpu.CompilerParams(vmem_limit_bytes=32 * 2**20),
+        cost_estimate=pl.CostEstimate(flops=0, bytes_accessed=0, transcendentals=0),
+        name="join_tracks",
+    )(lax.axis_index("species").reshape(1).astype(jnp.int32), x, other)
 
 
 def layer_norm(value_entries, gain, shift):
@@ -656,9 +727,7 @@
         + [placed(x) for x in small]
     )
     joined = sum_chips(joined.reshape(-1, 128))
-    spread = spread_tracks(
-        tie(jnp.concatenate([head_weight[0], pred_grad[0, 0]], axis=0), joined)
-    )
+    spread = spread_tracks(head_weight[0], pred_grad[0, 0])
     joined = sum_column(joined)
     joined = joined.reshape(-1)
     moment_one, moment_two = joined[:chans], joined[chans : 2 * chans]
@@ -690,8 +759,6 @@
     )
     rest_column = lax.all_gather(tie(rest_shard, mixer_column), "dp")
     head_rows = head_weight.shape[1]
-    spread = exchange_plane(spread)
-    track_grad = spread[:, head_rows:].reshape(crop_rows, 2 * BLOCK)
     kv_width, q_width, hidden = pairs * PAIR, query_weight.shape[1], up_weight.shape[1]
     ways = ((1, 2), (2, 1))
 
@@ -702,7 +769,8 @@
         ]
 
     def second_step(nears, *after):
-        return [flip(tie(near, *after), way[1]) for near, way in zip(nears, ways)]
+        nears[:] = [tie(near, *after) for near in nears]
+        return [flip(near, way[1]) for near, way in zip(nears, ways)]
 
     def parts(nears, fars):
         return [(near, far) + way for near, far, way in zip(nears, fars, ways)]
@@ -715,12 +783,14 @@
     normed_rows = standardized_input * batchnorm_gain + batchnorm_shift
     activity, act_slope = gelu_and_slope(normed_rows)
     act_rows = gather_begin(activity)
-    act_rows = act_rows[:3] + tuple(tie(x, spread) for x in act_rows[3:])
     act_all = gather_end(*act_rows)
-    w_conv = both_halves(conv_half).reshape(WIDTH, chans, outputs)
-    mixer_near = first_step(mixer_column, 0, mixer_column.shape[-1] // 2, act_all)
-    mixer_far = second_step(mixer_near)
+    w_conv = both_halves(tie(conv_half, *act_rows[1:3])).reshape(WIDTH, chans, outputs)
+    mixer_column = tie(mixer_column, w_conv)
+    mixer_near = first_step(mixer_column, 0, mixer_column.shape[-1] // 2)
     conv_slice = conv_forward(act_all, w_conv).reshape(4, bin_count, outputs)
+    spread = exchange_plane(spread, (conv_slice,))
+    track_grad = spread[:, head_rows:].reshape(crop_rows, 2 * BLOCK)
+    mixer_far = second_step(mixer_near, conv_slice)
     w_head = lax.all_gather(tie(spread[:, :head_rows], rest_column), "dp").reshape(-1, 2 * BLOCK)
     conv_slice = exchange_plane(conv_slice)
     conv_out = bias_conv + conv_slice.transpose(1, 0, 2).reshape(bin_count, chans).astype(wide)
@@ -738,9 +808,9 @@
     kv_rows = gather_begin(dense(normed_one, w_kv).astype(low))
     query_rows = (dense(normed_one, w_query).astype(low).astype(wide) * scale).astype(low)
     ffn_near = first_step(rest_column, 0, hidden, *kv_rows[1:3])
+    point_near = first_step(rest_column, 2 * hidden, point_weight.shape[1] // 2, *kv_rows[1:3])
     kv_all = gather_end(*kv_rows)
     ffn_far = second_step(ffn_near, kv_all)
-    point_near = first_step(rest_column, 2 * hidden, point_weight.shape[1] // 2, kv_all)
     point_far = second_step(point_near, *ffn_far)
     bucket_window = lax.dynamic_slice_in_dim(
         jnp.pad(rel_bucket, (1, 0), constant_values=-1),
@@ -754,6 +824,7 @@
     ).reshape(pairs, 2, full_len + bin_count)
     mixed = attn_fwd(query_rows, kv_all, distance_bias)
     second_sum = first_sum + dense(mixed, w_out)
+    ffn_far = [tie(x, second_sum) for x in ffn_far]
     (w_up, w_down) = sorted_rows(
         parts(ffn_near, ffn_far),
         [
@@ -766,6 +837,7 @@
     up_act, up_slope = gelu_and_slope(up_pre)
     third_sum = second_sum + dense(up_act, w_down) + bias_down
     third_rows = gather_begin(tie(third_sum.astype(low), w_head))
+    point_far = [tie(x, third_rows[0]) for x in point_far]
     third_all = gather_end(*third_rows)
     (w_point,) = sorted_rows(
         parts(point_near, point_far),
@@ -817,16 +889,14 @@
     preds = exchange_plane(
         tie(jnp.concatenate(preds, axis=1), third_grad).reshape(4, crop_rows // 4, 2 * BLOCK)
     )
-    point_once = fold_both(point_half, 0)
     down_grad = third_grad.astype(low)
     down_other = swap_cores(outer_half(up_act, down_grad, 1))
     grad_down_b = row_sum(down_grad)
     up_grad = (up_slope.astype(wide) * dense_back(down_grad, w_down)).astype(low)
+    point_once = fold_both(point_half, 0, (up_grad,))
     down_half = by_device(outer_half(up_act, down_grad, 0, down_other))
-    up_grad = tie(up_grad, down_half, *point_once)
-
-    point_twice = fold_both(point_once, 1)
-    down_once = fold_both(down_half, 0)
+    up_grad = tie(up_grad, down_half)
+
     up_other = swap_cores(outer_half(normed_two, up_grad, 1))
     grad_up_b = row_sum(up_grad)
     _, norm_two_back = jax.vjp(layer_norm, second_sum, gain_ffn, shift_ffn)
@@ -835,24 +905,43 @@
     out_grad = second_grad.astype(low)
     mixed_grad = dense_back(out_grad, w_out).astype(low)
     up_half = by_device(outer_half(normed_two, up_grad, 0, up_other))
-    mixed_grad = tie(mixed_grad, up_half, *point_twice, *down_once)
-
-    down_twice = fold_both(down_once, 1)
-    up_once = fold_both(up_half, 0)
+    mixed_grad = tie(mixed_grad, up_half, preds, *point_once)
+
     out_other = swap_cores(outer_half(mixed, out_grad, 1))
     query_low, kv_part, distance_grad = attn_bwd(
         query_rows, kv_all, distance_bias, mixed_grad
     )
-    kv_part = tie(kv_part, out_other, *down_twice, *up_once)
-
-    up_twice = fold_both(up_once, 1)
+    point_twice = fold_both(point_once, 1, (kv_part,))
+    down_once = fold_both(down_half, 0, (kv_part,))
+    kv_part = tie(kv_part, out_other, *point_twice, *down_once)
+
     kv_mine, kv_onward = scatter_begin(*scatter_blocks(kv_part))
     grad_table = jnp.dot(
         distance_grad.reshape(HEADS, -1), window_onehot, precision=lax.Precision.HIGHEST,
         preferred_element_type=wide,
     ).reshape(HEADS * NB)
     out_half = by_device(outer_half(mixed, out_grad, 0, out_other))
-    kv_onward = [tie(x, out_half, head_sum, *up_twice) for x in kv_onward]
+    kv_onward = [tie(x, out_half, head_sum) for x in kv_onward]
+    kv_low = scatter_end(kv_mine, kv_onward).astype(low)
+
+    mixer_grads = jnp.concatenate([kv_low, query_low], axis=1)
+    mixer_sent = outer_half(normed_one, mixer_grads, 1)
+    mixer_other = swap_cores(mixer_sent)
+    down_twice = fold_both([tie(x, *kv_onward) for x in down_once], 1, (kv_low,))
+    up_once = fold_both(tie(up_half, *kv_onward), 0, (mixer_sent,))
+    normed_one_grad = dense_back(kv_low, w_kv) + dense_back(tie(query_low, mixer_sent), w_query)
+    _, norm_one_back = jax.vjp(layer_norm, first_sum, gain_attn, shift_attn)
+    first_part, grad_attn_gain, grad_attn_shift = norm_one_back(normed_one_grad)
+    first_grad = second_grad + first_part
+    conv_grad = first_grad.astype(low)
+    grad_conv_b = row_sum(conv_grad)
+    conv_part = exchange_plane(
+        conv_grad.reshape(bin_count, 4, outputs).transpose(1, 0, 2)
+    ).reshape(full_len, outputs)
+    mixer_half = jnp.concatenate(
+        [by_device(outer_half(normed_one, mixer_grads, 0, mixer_other)), out_half], axis=-1
+    )
+    up_twice = fold_both(up_once, 1, (conv_grad,))
     rest_sum = lax.psum_scatter(
         jnp.concatenate(
             [*point_twice, *up_twice]
@@ -861,22 +950,7 @@
         ),
         "dp", scatter_dimension=0, tiled=False,
     ).astype(wide)
-    kv_low = scatter_end(kv_mine, kv_onward).astype(low)
-
-    mixer_grads = jnp.concatenate([kv_low, query_low], axis=1)
-    mixer_other = swap_cores(outer_half(normed_one, mixer_grads, 1))
-    normed_one_grad = dense_back(kv_low, w_kv) + dense_back(query_low, w_query)
-    _, norm_one_back = jax.vjp(layer_norm, first_sum, gain_attn, shift_attn)
-    first_part, grad_attn_gain, grad_attn_shift = norm_one_back(normed_one_grad)
-    first_grad = second_grad + first_part
-    mixer_half = jnp.concatenate(
-        [by_device(outer_half(normed_one, mixer_grads, 0, mixer_other)), out_half], axis=-1
-    )
-    conv_grad = tie(first_grad.astype(low), mixer_half)
-    grad_conv_b = row_sum(conv_grad)
-    conv_part = exchange_plane(
-        conv_grad.reshape(bin_count, 4, outputs).transpose(1, 0, 2)
-    ).reshape(full_len, outputs)
+    conv_part = tie(conv_part, mixer_half, *up_twice)
 
     mixer_once = fold_both(mixer_half, 0)
     padded = jnp.pad(conv_part, ((half_width, half_width), (0, 0)))
@@ -892,7 +966,7 @@
     act_mine, act_onward = scatter_begin(*scatter_blocks(act_part))
     act_onward = [tie(x, *mixer_twice) for x in act_onward]
     act_grad = scatter_end(act_mine, act_onward)
-    predictions = collect_tracks(tie(preds, *act_onward), tracks)
+    predictions = collect_tracks(tie(preds, *act_onward), tracks, low)
     grad_mixer = lax.psum_scatter(
         jnp.concatenate(mixer_twice, axis=-1), "dp", scatter_dimension=0, tiled=False
     ).astype(wide)
@@ -902,8 +976,8 @@
     grad_conv_w = exchange_plane(conv_sum.reshape(4, -1, outputs))
     grad_conv_w = grad_conv_w.transpose(1, 0, 2).reshape(-1, chans).astype(wide)
     head_grad = collect_tracks(
-        exchange_plane(tie(head_sum, *act_onward).reshape(4, head_rows, 2 * BLOCK)), tracks
-    ).astype(wide)
+        exchange_plane(tie(head_sum, *act_onward).reshape(4, head_rows, 2 * BLOCK)), tracks, wide
+    )
     grad_point_w = rest_sum[:, : point_weight.shape[1]]
     at = point_weight.shape[1]
     grad_up_w = rest_sum[:, at : at + hidden]

time: 1280 us -> 1240 us (0.969)
  waiting for transfers between devices: 458 us -> 408 us
  local copies, waits for them, and re-layouts: 226 us -> 200 us
  other arithmetic: 143 us -> 164 us
  Pallas kernels: 192 us -> 206 us
    ppermute x77, waiting for transfers between devices: 448 us -> 361 us  [flip(): return lax.ppermute(x, 'seq', [(i, i ^ bit) for i in range(peers)])]
    ppermute x4, waiting for transfers between devices: 4.49 us -> 31.7 us  [sum_column(): x = x + lax.ppermute(x, 'dp', [(i, i ^ step) for i in range(peers)])]
    pallas_call x0 -> x3, Pallas kernels: none -> 18.4 us  [the longest x2 9.85 us: collect_tracks(): pl.pallas_call(join_tracks_kernel, grid=(rows // step,), in_specs=[pl.Blo...]
    reshape x4 -> x0, local copies, waits for them, and re-layouts: 15.6 us -> none  [the longest x1 8.3 us: spread_tracks(): jnp.pad(x, ((0, 0), (0, 12 * BLOCK - x.shape[1])))]
    squeeze x8 -> x14, local copies, waits for them, and re-layouts: 2.17 us -> 17.4 us  [pick(): return lax.dynamic_index_in_dim(x, index, axis, keepdims=False)]
    unnamed x468 -> x495, local copies, waits for them, and re-layouts: 110 us -> 114 us
  transfers between devices with their start and end apart: 115 -> 115, of which waited for: 55 -> 56; matrix products, arithmetic and copies ran while one was open for 27% -> 27% of each run, Pallas kernels for 13% -> 15%
where the time goes in v2:
time: 1240 us; the launch traced here: 1230 us
  waiting for transfers between devices  408 us (33%)
  Pallas kernels  206 us (17%)
  local copies, waits for them, and re-layouts  200 us (16%)
  other arithmetic  164 us (13%)
  matrix products  123 us (10%)
  starting transfers between devices  107 us (9%)
  between operations  18 us (1%)
    ppermute x77, waiting for transfers between devices, flip(): return lax.ppermute(x, 'seq', [(i, i ^ bit) for i in range(peers)])  361 us
    unnamed x495, local copies, waits for them, and re-layouts  114 us
    ppermute x77, starting transfers between devices, flip(): return lax.ppermute(x, 'seq', [(i, i ^ bit) for i in range(peers)])  86.4 us
    pallas_call x12, Pallas kernels, outer_half(): pl.pallas_call(outer_kernel, grid_spec=pltpu.PrefetchScalarGridSpec(num_s...  74.1 us
    dot_general x8, matrix products, dense_back(): lax.dot_general(left, right, (((1,), (1,)), ((), ())), preferred_element_...  66 us
    dot_general x8, matrix products, dense(): return jnp.dot(left, right, preferred_element_type=jnp.float32)  56.3 us
    ppermute x4, waiting for transfers between devices, sum_column(): x = x + lax.ppermute(x, 'dp', [(i, i ^ step) for i in range(peers)])  31.7 us
    pallas_call x1, Pallas kernels, attn_bwd(): pl.pallas_call(attn_bwd_kernel, grid=(pairs,), in_specs=specs + [pl.Block...  29.2 us
  transfers between devices with their start and end apart: 115, of which 56 were waited for; matrix products, arithmetic and copies ran while one was open for 27% of the time, Pallas kernels for 15%

profile of v2, /device:TPU:0, one launch (start us, length us, event | category | flops | bytes accessed | tf_op | source)
XLA Modules:
  0.0 1225.4 jit_solution(3490900869996462406)
XLA Ops:
  37.6 10.6 collective-permute-done.3
  48.3 12.7 %collective-permute-done.4 = f32[170,128]{1,0:T(8,128)S(1)} collective-permute-done((f32[170,128]{1,0:T(8,128)S(1)}, f32[170,128]{1,0:T(8,128)S(1)}, u32[]{:S(2)}, u32[]{:S(2)}) %collective-permute-start.4) | collective-permute-done | bytes 87072 | tf_op jit(solution)/shard_map/ppermute | solution.py:539
  73.2 14.5 %collective-permute-done.5.refs_1_ = bf16[384,1536]{1,0:T(8,128)(2,1)S(1)} collective-permute-done((bf16[384,1536]{1,0:T(8,128)(2,1)S(1)}, bf16[384,1536]{1,0:T(8,128)(2,1)S(1)}, u32[]{:S(2)}, u32[]{:S(2)}) %collective-permute-start.5) | collective-permute-done | bytes 1179680 | tf_op jit(solution)/shard_map/ppermute | solution.py:155
  97.5 8.6 cut_tracks.1
  114.8 9.7 collective-permute-done.7.refs_3_
  129.7 5.3 all-gather.11.cloned.1.call-done
  150.0 12.8 %conv_forward.1 = bf16[1536,384]{1,0:T(8,128)(2,1)S(1)} custom-call(bf16[1536,1536]{1,0:T(8,128)(2,1)S(1)} %bitcast.595, bf16[5,1536,384]{2,1,0:T(8,128)(2,1)S(1)} %bitcast.585), custom_call_target="tpu_custom_call" | custom-call | flops 13589544960 | tf_op jit(solution)/shard_map/conv_forward/pallas_call | solution.py:365
  177.8 33.9 %collective-permute-done.15 = bf16[384,384]{1,0:T(8,128)(2,1)S(1)} collective-permute-done((bf16[384,384]{1,0:T(8,128)(2,1)S(1)}, bf16[384,384]{1,0:T(8,128)(2,1)S(1)}, u32[]{:S(2)}, u32[]{:S(2)}) %collective-permute-start.15) | collective-permute-done | bytes 294944 | tf_op jit(solution)/shard_map/ppermute | solution.py:155
  247.5 7.6 collective-permute-done.38.refs_0_
  263.7 25.6 %collective-permute-done.24.refs_1_ = bf16[384,2048]{1,0:T(8,128)(2,1)S(1)} collective-permute-done((bf16[384,2048]{1,0:T(8,128)(2,1)}, bf16[384,2048]{1,0:T(8,128)(2,1)S(1)}, u32[]{:S(2)}, u32[]{:S(2)}) %collective-permute-start.24) | collective-permute-done | bytes 1572896 | tf_op jit(solution)/shard_map/ppermute | solution.py:155
  306.2 11.2 collective-permute-done.26.refs_3_
  318.8 18.3 %collective-permute-done.27.refs_4_ = bf16[192,2048]{1,0:T(8,128)(2,1)} collective-permute-done((bf16[192,2048]{1,0:T(8,128)(2,1)}, bf16[192,2048]{1,0:T(8,128)(2,1)}, u32[]{:S(2)}, u32[]{:S(2)}) %collective-permute-start.27) | collective-permute-done | bytes 786464 | tf_op jit(solution)/shard_map/ppermute | solution.py:155
  350.0 5.4 collective-permute-done.48
  360.1 12.3 attention_forward.1.left_ref
  376.4 27.4 %collective-permute-done.29.refs_0_.refs_1_ = bf16[2,4,48,3072]{3,2,1,0:T(8,128)(2,1)S(1)} collective-permute-done((bf16[2,4,48,3072]{3,2,1,0:T(8,128)(2,1)}, bf16[2,4,48,3072]{3,2,1,0:T(8,128)(2,1)S(1)}, u32[]{:S(2)}, u32[]{:S(2)}) %collective-permute-start.29) | collective-permute-done | bytes 2359328 | tf_op jit(solution)/shard_map/ppermute | solution.py:155
  414.8 12.8 %sort_copies.11 = (bf16[2,4,4,1,48,3072]{5,4,3,2,1,0:T(8,128)(2,1)}, bf16[2,4,4,2,48,1536]{5,4,3,2,1,0:T(8,128)(2,1)}) custom-call(bf16[2,4,48,3072]{3,2,1,0:T(8,128)(2,1)} %tie.68.refs_0_, bf16[2,4,48,3072]{3,2,1,0:T(8,128)(2,1)S(1)} %copy-done.20, bf16[2,4,48,3072]{3,2,1,0:T(8,128)(2,1)} %collective-permute-done.30.refs_2_, ...), custom_call_target="tpu_custom_call" | custom-call | bytes 75497472 | tf_op jit(solution)/shard_map/sort_copies/pallas_call | solution.py:197
  427.6 10.7 multiply_convert_fusion.3
  448.7 24.2 %collective-permute-done.40.refs_1_ = bf16[384,1536]{1,0:T(8,128)(2,1)} collective-permute-done((bf16[384,1536]{1,0:T(8,128)(2,1)}, bf16[384,1536]{1,0:T(8,128)(2,1)}, u32[]{:S(2)}, u32[]{:S(2)}) %collective-permute-start.40) | collective-permute-done | bytes 1179680 | tf_op jit(solution)/shard_map/ppermute | solution.py:155
  483.3 7.6 collective-permute-done.42.refs_3_
  497.1 13.9 %multiply_convert_fusion.1 = (bf16[896,3072]{1,0:T(8,128)(2,1)}, f32[896,3072]{1,0:T(8,128)}) fusion(f32[3072]{0:T(1024)S(1)} %get-tuple-element.194, bf16[896,1536]{1,0:T(8,128)(2,1)S(1)} %constant_dynamic-slice_fusion.31.left_ref, bf16[1536,3072]{1,0:T(8,128)(2,1)S(1)} %bitcast.593), kind=kOutput, calls=%fused_computation.11 | convolution fusion | flops 8483241984 | bytes 28717056 | tf_op jit(solution)/shard_map/dot_general | solution.py:649
  524.6 8.7 fusion.63
  541.2 8.9 multiply_convert_fusion.4
  551.1 19.1 %multiply_convert_fusion.refs_0_ = bf16[896,3072]{1,0:T(8,128)(2,1)S(1)} fusion(bf16[896,3072]{1,0:T(8,128)(2,1)} %collective-permute-done.53, f32[896,3072]{1,0:T(8,128)} %get-tuple-element.222, f32[3072]{0:T(1024)S(1)} %get-tuple-element.194, pred[]{:T(512)S(6)} %eq.8, bf16[3072,1024]{1,0:T(8,128)(2,1)} %bitcast.632, ...), kind=kOutput, calls=%fused_computation.10 | convolution fusion | flops 5709627392 | bytes 30158848 | tf_op jit(solution)/shard_map/dot_general | solution.py:653
  570.2 13.3 %convolution_convert_fusion.1.x_ref = bf16[896,1536]{1,0:T(8,128)(2,1)S(1)} fusion(bf16[896,3072]{1,0:T(8,128)(2,1)S(1)} %multiply_convert_fusion.refs_0_, bf16[1536,3072]{1,0:T(8,128)(2,1)} %bitcast.594), kind=kOutput, calls=%fused_computation.32 | convolution fusion | flops 8457093120 | bytes 17694720 | tf_op jit(solution)/shard_map/dot_general | solution.py:653
  595.0 6.8 outer_half.12.refs_2_
  611.9 12.1 tracks_grad.1
  624.1 8.4 collective-permute-done.54
  642.1 12.5 %collective-permute-done.55.refs_0_ = bf16[192,1536]{1,0:T(8,128)(2,1)S(1)} collective-permute-done((bf16[192,1536]{1,0:T(8,128)(2,1)}, bf16[192,1536]{1,0:T(8,128)(2,1)S(1)}, u32[]{:S(2)}, u32[]{:S(2)}) %collective-permute-start.55) | collective-permute-done | bytes 589856 | tf_op jit(solution)/shard_map/ppermute | solution.py:155
  659.9 8.7 outer_half.13
  673.4 5.3 outer_half.14
  698.9 7.0 multiply_convert_fusion.2.refs_0_.refs_1_
  708.9 23.5 %collective-permute-done.65.refs_0_ = bf16[4,2,48,1536]{3,2,1,0:T(8,128)(2,1)} collective-permute-done((bf16[4,2,48,1536]{3,2,1,0:T(8,128)(2,1)S(1)}, bf16[4,2,48,1536]{3,2,1,0:T(8,128)(2,1)}, u32[]{:S(2)}, u32[]{:S(2)}) %collective-permute-start.65) | collective-permute-done | bytes 1179680 | tf_op jit(solution)/shard_map/ppermute | solution.py:155
  735.3 6.2 outer_half.15
  759.1 7.7 multiply_reduce_fusion
  777.7 5.4 convolution_convert_fusion.2.refs_0_
  789.5 29.2 %attention_backward.1 = (bf16[384,512]{1,0:T(8,128)(2,1)}, bf16[1536,2048]{1,0:T(8,128)(2,1)}, f32[4,2,1920]{2,1,0:T(2,128)}) custom-call(bf16[384,512]{1,0:T(8,128)(2,1)} %fusion.81.q_ref, bf16[1536,2048]{1,0:T(8,128)(2,1)} %bitcast.567, f32[4,2,1920]{2,1,0:T(2,128)} %copy-done.74, bf16[384,1536]{1,0:T(8,128)(2,1)} %tie.94.g_ref), custom_call_target="tpu_custom_call" | custom-call | flops 32000000000 | tf_op jit(solution)/shard_map/attention_backward/pallas_call | solution.py:130
  845.5 26.2 %collective-permute-done.71 = bf16[2,192,2048]{2,1,0:T(8,128)(2,1)} collective-permute-done((bf16[2,192,2048]{2,1,0:T(8,128)(2,1)}, bf16[2,192,2048]{2,1,0:T(8,128)(2,1)}, u32[]{:S(2)}, u32[]{:S(2)}) %collective-permute-start.71) | collective-permute-done | bytes 1572896 | tf_op jit(solution)/shard_map/ppermute | solution.py:155
  882.3 5.2 fusion.134
  916.8 6.6 multiply_reduce_fusion.1
  956.2 8.8 collective-permute-done.80.refs_0_
  990.7 11.5 outer_half.22.refs_1_
  1010.2 16.1 %conv_back.1.refs_0_.refs_1_ = bf16[1536,1536]{1,0:T(8,128)(2,1)S(1)} custom-call(bf16[1536,1920]{1,0:T(8,128)(2,1)S(1)} %bitcast.582, bf16[5,1536,384]{2,1,0:T(8,128)(2,1)} %bitcast.584), custom_call_target="tpu_custom_call" | custom-call | flops 13589544960 | tf_op jit(solution)/shard_map/conv_back/pallas_call | solution.py:393
  1028.5 13.8 %collective-permute-done.83 = bf16[4,2,48,2048]{3,2,0,1:T(8,128)(2,1)} collective-permute-done((bf16[4,2,48,2048]{3,2,0,1:T(8,128)(2,1)S(1)}, bf16[4,2,48,2048]{3,2,0,1:T(8,128)(2,1)}, u32[]{:S(2)}, u32[]{:S(2)}) %collective-permute-start.83) | collective-permute-done | bytes 1572896 | tf_op jit(solution)/shard_map/ppermute | solution.py:155
  1059.7 15.1 %outer_half.23 = bf16[3840,384]{1,0:T(8,128)(2,1)} custom-call(s32[1]{0:T(128)} %bitcast.168.base_ref, bf16[1536,1536]{1,0:T(8,128)(2,1)S(1)} %bitcast.601, bf16[1536,1920]{1,0:T(8,128)(2,1)} %tie.116.right_ref, bf16[3840,384]{1,0:T(8,128)(2,1)} %collective-permute-done.97.refs_0_), custom_call_target="tpu_custom_call" | custom-call | flops 6794772480 | tf_op jit(solution)/shard_map/outer_half/pallas_call | solution.py:424
  1075.1 22.0 %collective-permute-done.86 = bf16[4,48,2048]{2,1,0:T(8,128)(2,1)} collective-permute-done((bf16[4,48,2048]{2,1,0:T(8,128)(2,1)}, bf16[4,48,2048]{2,1,0:T(8,128)(2,1)}, u32[]{:S(2)}, u32[]{:S(2)}) %collective-permute-start.86) | collective-permute-done | bytes 786464 | tf_op jit(solution)/shard_map/ppermute | solution.py:155
  1155.1 14.4 %collective-permute-done.93 = f32[146,128]{1,0:T(8,128)} collective-permute-done((f32[146,128]{1,0:T(8,128)}, f32[146,128]{1,0:T(8,128)}, u32[]{:S(2)}, u32[]{:S(2)}) %collective-permute-start.93) | collective-permute-done | bytes 74784 | tf_op jit(solution)/shard_map/ppermute | solution.py:155
  1175.9 7.7 collective-permute-done.95
  1185.5 5.0 join_tracks.2
  (1017 shorter events, 587.3 us)
Async XLA Ops:
  7.2 82.4 %all-gather.9.cloned.1.call-start = ((), (), s32[]{:S(2)}) async-start(), calls=%async_computation.8 | async-start | bytes 3686400 | tf_op jit(solution)/shard_map/all_gather | solution.py:713
  24.8 110.2 %all-gather.11.cloned.1.call-start = ((), (), s32[]{:S(2)}) async-start(), calls=%async_computation.9 | async-start | bytes 1966080 | tf_op jit(solution)/shard_map/all_gather | solution.py:755
  89.9 45.1 %collective-permute-start.12 = (bf16[4,4,240,384]{3,2,1,0:T(8,128)(2,1)}, bf16[4,4,240,384]{3,2,1,0:T(8,128)(2,1)}, u32[]{:S(2)}, u32[]{:S(2)}) collective-permute-start(bf16[4,4,240,384]{3,2,1,0:T(8,128)(2,1)} %tie.61.refs_0_), channel_id=1, source_target_pairs={{0,16},{16,0},{1,17},{17,1},{2,18},{18,2},{3,19},{19,3},{4,20},{20... | collective-permute-start | bytes 8847368 | tf_op jit(solution)/shard_map/ppermute | solution.py:159
  95.8 164.7 %all-gather.13.cloned.1.call-start = ((), (), s32[]{:S(2)}) async-start(), calls=%async_computation.10 | async-start | bytes 4423680 | tf_op jit(solution)/shard_map/all_gather | solution.py:760
  107.3 63.6 %collective-permute-start.36 = (bf16[4,416,512]{2,1,0:T(8,128)(2,1)}, bf16[4,416,512]{2,1,0:T(8,128)(2,1)}, u32[]{:S(2)}, u32[]{:S(2)}) collective-permute-start(bf16[4,416,512]{2,1,0:T(8,128)(2,1)} %get-tuple-element.39), channel_id=1, source_target_pairs={{0,16},{1,17},{2,18},{3,19},{4,20},{5,21},{6,22},{7,23},{8,24},{9,... | collective-permute-start | bytes 5111816 | tf_op jit(solution)/shard_map/ppermute | solution.py:163
  135.0 309.7 %all-gather.15.cloned.1.call-start = ((), (), s32[]{:S(2)}) async-start(), calls=%async_computation.11 | async-start | bytes 7864320 | tf_op jit(solution)/shard_map/all_gather | solution.py:794
  165.1 61.9 %collective-permute-start.17 = (bf16[2,4,48,2048]{3,2,1,0:T(8,128)(2,1)}, bf16[2,4,48,2048]{3,2,1,0:T(8,128)(2,1)}, u32[]{:S(2)}, u32[]{:S(2)}) collective-permute-start(bf16[2,4,48,2048]{3,2,1,0:T(8,128)(2,1)} %tie.64.refs_0_), channel_id=1, source_target_pairs={{0,2},{1,3},{2,0},{3,1},{4,6},{5,7},{6,4},{7,5},{8,10},{9,11},{10,... | collective-permute-start | bytes 4718600 | tf_op jit(solution)/shard_map/ppermute | solution.py:155
  167.2 59.9 %collective-permute-start.21 = (bf16[2,4,48,2048]{3,2,1,0:T(8,128)(2,1)}, bf16[2,4,48,2048]{3,2,1,0:T(8,128)(2,1)}, u32[]{:S(2)}, u32[]{:S(2)}) collective-permute-start(bf16[2,4,48,2048]{3,2,1,0:T(8,128)(2,1)} %tie.65.refs_4_), channel_id=1, source_target_pairs={{0,1},{1,0},{2,3},{3,2},{4,5},{5,4},{6,7},{7,6},{8,9},{9,8},{10,11... | collective-permute-start | bytes 4718600 | tf_op jit(solution)/shard_map/ppermute | solution.py:155
  168.6 43.2 %collective-permute-start.15 = (bf16[384,384]{1,0:T(8,128)(2,1)S(1)}, bf16[384,384]{1,0:T(8,128)(2,1)S(1)}, u32[]{:S(2)}, u32[]{:S(2)}) collective-permute-start(bf16[384,384]{1,0:T(8,128)(2,1)S(1)} %get-tuple-element.171), channel_id=1, source_target_pairs={{0,3},{1,2},{2,1},{3,0},{4,7},{5,6},{6,5},{7,4},{8,11},{9,10},{10,... | collective-permute-start | bytes 884744 | tf_op jit(solution)/shard_map/ppermute | solution.py:155
  170.1 43.5 %collective-permute-start.14 = (bf16[384,384]{1,0:T(8,128)(2,1)S(1)}, bf16[384,384]{1,0:T(8,128)(2,1)S(1)}, u32[]{:S(2)}, u32[]{:S(2)}) collective-permute-start(bf16[384,384]{1,0:T(8,128)(2,1)S(1)} %get-tuple-element.172), channel_id=1, source_target_pairs={{0,2},{1,3},{2,0},{3,1},{4,6},{5,7},{6,4},{7,5},{8,10},{9,11},{10,... | collective-permute-start | bytes 884744 | tf_op jit(solution)/shard_map/ppermute | solution.py:155
  170.9 46.5 %collective-permute-start.13 = (bf16[384,384]{1,0:T(8,128)(2,1)S(1)}, bf16[384,384]{1,0:T(8,128)(2,1)S(1)}, u32[]{:S(2)}, u32[]{:S(2)}) collective-permute-start(bf16[384,384]{1,0:T(8,128)(2,1)S(1)} %get-tuple-element.173), channel_id=1, source_target_pairs={{0,1},{1,0},{2,3},{3,2},{4,5},{5,4},{6,7},{7,6},{8,9},{9,8},{10,11... | collective-permute-start | bytes 884744 | tf_op jit(solution)/shard_map/ppermute | solution.py:155
  245.3 44.0 %collective-permute-start.24 = (bf16[384,2048]{1,0:T(8,128)(2,1)}, bf16[384,2048]{1,0:T(8,128)(2,1)S(1)}, u32[]{:S(2)}, u32[]{:S(2)}) collective-permute-start(bf16[384,2048]{1,0:T(8,128)(2,1)} %convolution_convert_fusion.3.refs_0_), channel_id=1, source_target_pairs={{0,1},{1,0},{2,3},{3,2},{4,5},{5,4},{6,7},{7,6},{8,9},{9,8},{10,11... | collective-permute-start | bytes 4718600 | tf_op jit(solution)/shard_map/ppermute | solution.py:155
  246.0 43.3 %collective-permute-start.25 = (bf16[384,2048]{1,0:T(8,128)(2,1)}, bf16[384,2048]{1,0:T(8,128)(2,1)S(1)}, u32[]{:S(2)}, u32[]{:S(2)}) collective-permute-start(bf16[384,2048]{1,0:T(8,128)(2,1)} %convolution_convert_fusion.3.refs_0_), channel_id=1, source_target_pairs={{0,2},{1,3},{2,0},{3,1},{4,6},{5,7},{6,4},{7,5},{8,10},{9,11},{10,... | collective-permute-start | bytes 4718600 | tf_op jit(solution)/shard_map/ppermute | solution.py:155
  291.0 50.7 %collective-permute-start.28 = (bf16[4,48,3072]{2,1,0:T(8,128)(2,1)}, bf16[4,48,3072]{2,1,0:T(8,128)(2,1)}, u32[]{:S(2)}, u32[]{:S(2)}) collective-permute-start(bf16[4,48,3072]{2,1,0:T(8,128)(2,1)} %tie.67), channel_id=1, source_target_pairs={{0,1},{1,0},{2,3},{3,2},{4,5},{5,4},{6,7},{7,6},{8,9},{9,8},{10,11... | collective-permute-start | bytes 3538952 | tf_op jit(solution)/shard_map/ppermute | solution.py:155
  294.3 586.2 %reduce-scatter.5.cloned.1.call-start = ((), (), s32[]{:S(2)}) async-start(), calls=%async_computation.4 | async-start | bytes 7864320 | tf_op jit(solution)/shard_map/reduce_scatter | solution.py:884
  298.9 38.1 %collective-permute-start.27 = (bf16[192,2048]{1,0:T(8,128)(2,1)}, bf16[192,2048]{1,0:T(8,128)(2,1)}, u32[]{:S(2)}, u32[]{:S(2)}) collective-permute-start(bf16[192,2048]{1,0:T(8,128)(2,1)} %slice.357), channel_id=1, source_target_pairs={{0,1},{1,0},{2,3},{3,2},{4,5},{5,4},{6,7},{7,6},{8,9},{9,8},{10,11... | collective-permute-start | bytes 2359304 | tf_op jit(solution)/shard_map/ppermute | solution.py:155
  300.1 45.7 %collective-permute-start.32 = (bf16[4,48,3072]{2,1,0:T(8,128)(2,1)}, bf16[4,48,3072]{2,1,0:T(8,128)(2,1)}, u32[]{:S(2)}, u32[]{:S(2)}) collective-permute-start(bf16[4,48,3072]{2,1,0:T(8,128)(2,1)} %tie.70), channel_id=1, source_target_pairs={{0,2},{1,3},{2,0},{3,1},{4,6},{5,7},{6,4},{7,5},{8,10},{9,11},{10,... | collective-permute-start | bytes 3538952 | tf_op jit(solution)/shard_map/ppermute | solution.py:155
  305.4 50.0 %collective-permute-start.48 = (bf16[4,48,1536]{2,1,0:T(8,128)(2,1)}, bf16[4,48,1536]{2,1,0:T(8,128)(2,1)}, u32[]{:S(2)}, u32[]{:S(2)}) collective-permute-start(bf16[4,48,1536]{2,1,0:T(8,128)(2,1)} %tie.81), channel_id=1, source_target_pairs={{0,2},{1,3},{2,0},{3,1},{4,6},{5,7},{6,4},{7,5},{8,10},{9,11},{10,... | collective-permute-start | bytes 1769480 | tf_op jit(solution)/shard_map/ppermute | solution.py:155
  317.4 40.4 %collective-permute-start.44 = (bf16[4,48,1536]{2,1,0:T(8,128)(2,1)}, bf16[4,48,1536]{2,1,0:T(8,128)(2,1)}, u32[]{:S(2)}, u32[]{:S(2)}) collective-permute-start(bf16[4,48,1536]{2,1,0:T(8,128)(2,1)} %tie.78), channel_id=1, source_target_pairs={{0,1},{1,0},{2,3},{3,2},{4,5},{5,4},{6,7},{7,6},{8,9},{9,8},{10,11... | collective-permute-start | bytes 1769480 | tf_op jit(solution)/shard_map/ppermute | solution.py:155
  344.6 59.2 %collective-permute-start.29 = (bf16[2,4,48,3072]{3,2,1,0:T(8,128)(2,1)}, bf16[2,4,48,3072]{3,2,1,0:T(8,128)(2,1)S(1)}, u32[]{:S(2)}, u32[]{:S(2)}) collective-permute-start(bf16[2,4,48,3072]{3,2,1,0:T(8,128)(2,1)} %tie.68.refs_0_), channel_id=1, source_target_pairs={{0,2},{1,3},{2,0},{3,1},{4,6},{5,7},{6,4},{7,5},{8,10},{9,11},{10,... | collective-permute-start | bytes 7077896 | tf_op jit(solution)/shard_map/ppermute | solution.py:155
  349.1 54.6 %collective-permute-start.33 = (bf16[2,4,48,3072]{3,2,1,0:T(8,128)(2,1)}, bf16[2,4,48,3072]{3,2,1,0:T(8,128)(2,1)}, u32[]{:S(2)}, u32[]{:S(2)}) collective-permute-start(bf16[2,4,48,3072]{3,2,1,0:T(8,128)(2,1)} %tie.71.refs_4_), channel_id=1, source_target_pairs={{0,1},{1,0},{2,3},{3,2},{4,5},{5,4},{6,7},{7,6},{8,9},{9,8},{10,11... | collective-permute-start | bytes 7077896 | tf_op jit(solution)/shard_map/ppermute | solution.py:155
  375.9 37.5 %collective-permute-start.34 = (bf16[2,4,48,3072]{3,2,1,0:T(8,128)(2,1)}, bf16[2,4,48,3072]{3,2,1,0:T(8,128)(2,1)}, u32[]{:S(2)}, u32[]{:S(2)}) collective-permute-start(bf16[2,4,48,3072]{3,2,1,0:T(8,128)(2,1)} %tie.71.refs_4_), channel_id=1, source_target_pairs={{0,16},{16,0},{1,17},{17,1},{2,18},{18,2},{3,19},{19,3},{4,20},{20... | collective-permute-start | bytes 7077896 | tf_op jit(solution)/shard_map/ppermute | solution.py:159
  410.7 36.5 %collective-permute-start.45 = (bf16[2,4,48,1536]{3,2,1,0:T(8,128)(2,1)S(1)}, bf16[2,4,48,1536]{3,2,1,0:T(8,128)(2,1)}, u32[]{:S(2)}, u32[]{:S(2)}) collective-permute-start(bf16[2,4,48,1536]{3,2,1,0:T(8,128)(2,1)S(1)} %copy-done.35), channel_id=1, source_target_pairs={{0,2},{1,3},{2,0},{3,1},{4,6},{5,7},{6,4},{7,5},{8,10},{9,11},{10,... | collective-permute-start | bytes 3538952 | tf_op jit(solution)/shard_map/ppermute | solution.py:155
  601.8 58.0 %collective-permute-start.58 = (bf16[768,3072]{1,0:T(8,128)(2,1)}, bf16[768,3072]{1,0:T(8,128)(2,1)}, u32[]{:S(2)}, u32[]{:S(2)}) collective-permute-start(bf16[768,3072]{1,0:T(8,128)(2,1)} %outer_half.12.refs_2_), channel_id=1, source_target_pairs={{0,16},{16,0},{1,17},{17,1},{2,18},{18,2},{3,19},{19,3},{4,20},{20... | collective-permute-start | bytes 14155784 | tf_op jit(solution)/shard_map/ppermute | solution.py:159
  678.7 56.7 %collective-permute-start.62 = (bf16[1536,1536]{1,0:T(8,128)(2,1)}, bf16[1536,1536]{1,0:T(8,128)(2,1)}, u32[]{:S(2)}, u32[]{:S(2)}) collective-permute-start(bf16[1536,1536]{1,0:T(8,128)(2,1)} %outer_half.14), channel_id=1, source_target_pairs={{0,16},{16,0},{1,17},{17,1},{2,18},{18,2},{3,19},{19,3},{4,20},{20... | collective-permute-start | bytes 14155784 | tf_op jit(solution)/shard_map/ppermute | solution.py:159
  681.6 518.4 %reduce-scatter.11.cloned.1.call-start = ((), (), s32[]{:S(2)}) async-start(), calls=%async_computation.7 | async-start | bytes 4423680 | tf_op jit(solution)/shard_map/reduce_scatter | solution.py:945
  691.5 40.9 %collective-permute-start.65 = (bf16[4,2,48,1536]{3,2,1,0:T(8,128)(2,1)S(1)}, bf16[4,2,48,1536]{3,2,1,0:T(8,128)(2,1)}, u32[]{:S(2)}, u32[]{:S(2)}) collective-permute-start(bf16[4,2,48,1536]{3,2,1,0:T(8,128)(2,1)S(1)} %get-tuple-element.126), channel_id=1, source_target_pairs={{0,2},{1,3},{2,0},{3,1},{4,6},{5,7},{6,4},{7,5},{8,10},{9,11},{10,... | collective-permute-start | bytes 3538952 | tf_op jit(solution)/shard_map/ppermute | solution.py:155
  755.9 62.7 %collective-permute-start.67 = (bf16[4,48,1536]{2,1,0:T(8,128)(2,1)}, bf16[4,48,1536]{2,1,0:T(8,128)(2,1)}, u32[]{:S(2)}, u32[]{:S(2)}) collective-permute-start(bf16[4,48,1536]{2,1,0:T(8,128)(2,1)} %dynamic-slice_bitcast_fusion.24), channel_id=1, source_target_pairs={{0,2},{1,3},{2,0},{3,1},{4,6},{5,7},{6,4},{7,5},{8,10},{9,11},{10,... | collective-permute-start | bytes 1769480 | tf_op jit(solution)/shard_map/ppermute | solution.py:155
  757.8 60.8 %collective-permute-start.68 = (bf16[4,48,1536]{2,1,0:T(8,128)(2,1)}, bf16[4,48,1536]{2,1,0:T(8,128)(2,1)}, u32[]{:S(2)}, u32[]{:S(2)}) collective-permute-start(bf16[4,48,1536]{2,1,0:T(8,128)(2,1)} %dynamic-slice_bitcast_fusion.23), channel_id=1, source_target_pairs={{0,1},{1,0},{2,3},{3,2},{4,5},{5,4},{6,7},{7,6},{8,9},{9,8},{10,11... | collective-permute-start | bytes 1769480 | tf_op jit(solution)/shard_map/ppermute | solution.py:155
  773.8 54.8 %collective-permute-start.66 = (bf16[768,1536]{1,0:T(8,128)(2,1)}, bf16[768,1536]{1,0:T(8,128)(2,1)S(1)}, u32[]{:S(2)}, u32[]{:S(2)}) collective-permute-start(bf16[768,1536]{1,0:T(8,128)(2,1)} %outer_half.18), channel_id=1, source_target_pairs={{0,16},{16,0},{1,17},{17,1},{2,18},{18,2},{3,19},{19,3},{4,20},{20... | collective-permute-start | bytes 7077896 | tf_op jit(solution)/shard_map/ppermute | solution.py:159
  775.8 42.9 %collective-permute-start.69 = (bf16[4,2,96,768]{3,2,1,0:T(8,128)(2,1)}, bf16[4,2,96,768]{3,2,1,0:T(8,128)(2,1)}, u32[]{:S(2)}, u32[]{:S(2)}) collective-permute-start(bf16[4,2,96,768]{3,2,1,0:T(8,128)(2,1)} %dynamic-slice_bitcast_fusion.3), channel_id=1, source_target_pairs={{0,1},{1,0},{2,3},{3,2},{4,5},{5,4},{6,7},{7,6},{8,9},{9,8},{10,11... | collective-permute-start | bytes 3538952 | tf_op jit(solution)/shard_map/ppermute | solution.py:155
  835.2 36.6 %collective-permute-start.71 = (bf16[2,192,2048]{2,1,0:T(8,128)(2,1)}, bf16[2,192,2048]{2,1,0:T(8,128)(2,1)}, u32[]{:S(2)}, u32[]{:S(2)}) collective-permute-start(bf16[2,192,2048]{2,1,0:T(8,128)(2,1)} %pad_maximum_fusion.20), channel_id=1, source_target_pairs={{0,1},{1,0},{2,3},{3,2},{4,5},{5,4},{6,7},{7,6},{8,9},{9,8},{10,11... | collective-permute-start | bytes 4718600 | tf_op jit(solution)/shard_map/ppermute | solution.py:155
  837.7 36.3 %collective-permute-start.73 = (bf16[2,192,2048]{2,1,0:T(8,128)(2,1)}, bf16[2,192,2048]{2,1,0:T(8,128)(2,1)}, u32[]{:S(2)}, u32[]{:S(2)}) collective-permute-start(bf16[2,192,2048]{2,1,0:T(8,128)(2,1)} %pad_maximum_fusion.21), channel_id=1, source_target_pairs={{0,2},{1,3},{2,0},{3,1},{4,6},{5,7},{6,4},{7,5},{8,10},{9,11},{10,... | collective-permute-start | bytes 4718600 | tf_op jit(solution)/shard_map/ppermute | solution.py:155
  890.9 50.5 %collective-permute-start.79 = (bf16[4,2,48,1536]{3,2,1,0:T(8,128)(2,1)}, bf16[4,2,48,1536]{3,2,1,0:T(8,128)(2,1)}, u32[]{:S(2)}, u32[]{:S(2)}) collective-permute-start(bf16[4,2,48,1536]{3,2,1,0:T(8,128)(2,1)} %get-tuple-element.124), channel_id=1, source_target_pairs={{0,1},{1,0},{2,3},{3,2},{4,5},{5,4},{6,7},{7,6},{8,9},{9,8},{10,11... | collective-permute-start | bytes 3538952 | tf_op jit(solution)/shard_map/ppermute | solution.py:155
  893.8 51.4 %collective-permute-start.81 = (bf16[4,2,48,1536]{3,2,1,0:T(8,128)(2,1)}, bf16[4,2,48,1536]{3,2,1,0:T(8,128)(2,1)}, u32[]{:S(2)}, u32[]{:S(2)}) collective-permute-start(bf16[4,2,48,1536]{3,2,1,0:T(8,128)(2,1)} %get-tuple-element.122), channel_id=1, source_target_pairs={{0,2},{1,3},{2,0},{3,1},{4,6},{5,7},{6,4},{7,5},{8,10},{9,11},{10,... | collective-permute-start | bytes 3538952 | tf_op jit(solution)/shard_map/ppermute | solution.py:155
  895.6 41.3 %collective-permute-start.101 = (bf16[4,96,768]{2,1,0:T(8,128)(2,1)}, bf16[4,96,768]{2,1,0:T(8,128)(2,1)}, u32[]{:S(2)}, u32[]{:S(2)}) collective-permute-start(bf16[4,96,768]{2,1,0:T(8,128)(2,1)} %dynamic-slice_bitcast_fusion.16), channel_id=1, source_target_pairs={{0,2},{1,3},{2,0},{3,1},{4,6},{5,7},{6,4},{7,5},{8,10},{9,11},{10,... | collective-permute-start | bytes 1769480 | tf_op jit(solution)/shard_map/ppermute | solution.py:155
  901.3 37.2 %collective-permute-start.102 = (bf16[4,96,768]{2,1,0:T(8,128)(2,1)}, bf16[4,96,768]{2,1,0:T(8,128)(2,1)}, u32[]{:S(2)}, u32[]{:S(2)}) collective-permute-start(bf16[4,96,768]{2,1,0:T(8,128)(2,1)} %dynamic-slice_bitcast_fusion.15), channel_id=1, source_target_pairs={{0,1},{1,0},{2,3},{3,2},{4,5},{5,4},{6,7},{7,6},{8,9},{9,8},{10,11... | collective-permute-start | bytes 1769480 | tf_op jit(solution)/shard_map/ppermute | solution.py:155
  913.3 59.5 %collective-permute-start.78 = (bf16[768,2560]{1,0:T(8,128)(2,1)}, bf16[768,2560]{1,0:T(8,128)(2,1)}, u32[]{:S(2)}, u32[]{:S(2)}) collective-permute-start(bf16[768,2560]{1,0:T(8,128)(2,1)} %copy-done.22), channel_id=1, source_target_pairs={{0,16},{16,0},{1,17},{17,1},{2,18},{18,2},{3,19},{19,3},{4,20},{20... | collective-permute-start | bytes 11796488 | tf_op jit(solution)/shard_map/ppermute | solution.py:159
  972.7 230.6 %reduce-scatter.7.cloned.1.call-start = ((), (), s32[]{:S(2)}) async-start(), calls=%async_computation.5 | async-start | bytes 3686400 | tf_op jit(solution)/shard_map/reduce_scatter | solution.py:973
  1002.2 57.4 %collective-permute-start.97 = (bf16[3840,384]{1,0:T(8,128)(2,1)}, bf16[3840,384]{1,0:T(8,128)(2,1)}, u32[]{:S(2)}, u32[]{:S(2)}) collective-permute-start(bf16[3840,384]{1,0:T(8,128)(2,1)} %outer_half.22.refs_1_), channel_id=1, source_target_pairs={{0,16},{16,0},{1,17},{17,1},{2,18},{18,2},{3,19},{19,3},{4,20},{20... | collective-permute-start | bytes 8847368 | tf_op jit(solution)/shard_map/ppermute | solution.py:159
  1005.4 36.8 %collective-permute-start.83 = (bf16[4,2,48,2048]{3,2,0,1:T(8,128)(2,1)S(1)}, bf16[4,2,48,2048]{3,2,0,1:T(8,128)(2,1)}, u32[]{:S(2)}, u32[]{:S(2)}) collective-permute-start(bf16[4,2,48,2048]{3,2,0,1:T(8,128)(2,1)S(1)} %bitcast.642), channel_id=1, source_target_pairs={{0,1},{1,0},{2,3},{3,2},{4,5},{5,4},{6,7},{7,6},{8,9},{9,8},{10,11... | collective-permute-start | bytes 4718600 | tf_op jit(solution)/shard_map/ppermute | solution.py:155
  1009.4 36.8 %collective-permute-start.84 = (bf16[4,2,48,2048]{3,2,0,1:T(8,128)(2,1)}, bf16[4,2,48,2048]{3,2,0,1:T(8,128)(2,1)}, u32[]{:S(2)}, u32[]{:S(2)}) collective-permute-start(bf16[4,2,48,2048]{3,2,0,1:T(8,128)(2,1)} %bitcast.538), channel_id=1, source_target_pairs={{0,2},{1,3},{2,0},{3,1},{4,6},{5,7},{6,4},{7,5},{8,10},{9,11},{10,... | collective-permute-start | bytes 4718600 | tf_op jit(solution)/shard_map/ppermute | solution.py:155
  1052.5 49.2 %collective-permute-start.88 = (bf16[2,192,1536]{2,1,0:T(8,128)(2,1)}, bf16[2,192,1536]{2,1,0:T(8,128)(2,1)}, u32[]{:S(2)}, u32[]{:S(2)}) collective-permute-start(bf16[2,192,1536]{2,1,0:T(8,128)(2,1)} %pad_maximum_fusion.35), channel_id=1, source_target_pairs={{0,2},{1,3},{2,0},{3,1},{4,6},{5,7},{6,4},{7,5},{8,10},{9,11},{10,... | collective-permute-start | bytes 3538952 | tf_op jit(solution)/shard_map/ppermute | solution.py:155
  1054.8 48.5 %collective-permute-start.85 = (bf16[2,192,1536]{2,1,0:T(8,128)(2,1)}, bf16[2,192,1536]{2,1,0:T(8,128)(2,1)}, u32[]{:S(2)}, u32[]{:S(2)}) collective-permute-start(bf16[2,192,1536]{2,1,0:T(8,128)(2,1)} %pad_maximum_fusion.34), channel_id=1, source_target_pairs={{0,1},{1,0},{2,3},{3,2},{4,5},{5,4},{6,7},{7,6},{8,9},{9,8},{10,11... | collective-permute-start | bytes 3538952 | tf_op jit(solution)/shard_map/ppermute | solution.py:155
  1056.6 40.5 %collective-permute-start.86 = (bf16[4,48,2048]{2,1,0:T(8,128)(2,1)}, bf16[4,48,2048]{2,1,0:T(8,128)(2,1)}, u32[]{:S(2)}, u32[]{:S(2)}) collective-permute-start(bf16[4,48,2048]{2,1,0:T(8,128)(2,1)} %dynamic-slice_bitcast_fusion.10), channel_id=1, source_target_pairs={{0,2},{1,3},{2,0},{3,1},{4,6},{5,7},{6,4},{7,5},{8,10},{9,11},{10,... | collective-permute-start | bytes 2359304 | tf_op jit(solution)/shard_map/ppermute | solution.py:155
  1058.8 40.7 %collective-permute-start.87 = (bf16[4,48,2048]{2,1,0:T(8,128)(2,1)}, bf16[4,48,2048]{2,1,0:T(8,128)(2,1)}, u32[]{:S(2)}, u32[]{:S(2)}) collective-permute-start(bf16[4,48,2048]{2,1,0:T(8,128)(2,1)} %dynamic-slice_bitcast_fusion.9), channel_id=1, source_target_pairs={{0,1},{1,0},{2,3},{3,2},{4,5},{5,4},{6,7},{7,6},{8,9},{9,8},{10,11... | collective-permute-start | bytes 2359304 | tf_op jit(solution)/shard_map/ppermute | solution.py:155
  1074.8 133.4 %reduce-scatter.9.cloned.1.call-start = ((), (), s32[]{:S(2)}) async-start(), calls=%async_computation.6 | async-start | bytes 1966080 | tf_op jit(solution)/shard_map/reduce_scatter | solution.py:970
  1119.5 66.0 %collective-permute-start.89 = (bf16[4,224,512]{2,1,0:T(8,128)(2,1)}, bf16[4,224,512]{2,1,0:T(8,128)(2,1)S(1)}, u32[]{:S(2)}, u32[]{:S(2)}) collective-permute-start(bf16[4,224,512]{2,1,0:T(8,128)(2,1)} %slice.393), channel_id=1, source_target_pairs={{16,0},{17,1},{18,2},{19,3},{20,4},{21,5},{22,6},{23,7},{24,8},{25... | collective-permute-start | bytes 2752520 | tf_op jit(solution)/shard_map/ppermute | solution.py:167
  (290 other events, 2952.0 us)
Sparse Core Ops, SparseCore 0:
  24.9 64.6 all-gather.8
  95.9 39.0 all-gather.10
  136.5 68.8 all-gather.12
  294.4 114.2 all-gather.14
  681.7 109.4 reduce-scatter.4
  972.8 64.5 reduce-scatter.10
  1074.9 55.2 reduce-scatter.6
  1155.3 37.1 reduce-scatter.8

commit v3 on v2

--- a/solution.py
+++ b/solution.py
@@ -893,7 +893,7 @@
     down_other = swap_cores(outer_half(up_act, down_grad, 1))
     grad_down_b = row_sum(down_grad)
     up_grad = (up_slope.astype(wide) * dense_back(down_grad, w_down)).astype(low)
-    point_once = fold_both(point_half, 0, (up_grad,))
+    point_once = fold_both(point_half, 0, (down_other,))
     down_half = by_device(outer_half(up_act, down_grad, 0, down_other))
     up_grad = tie(up_grad, down_half)
 

time: 1240 us -> 1220 us (0.984)
  waiting for transfers between devices: 408 us -> 388 us
    ppermute x77, waiting for transfers between devices: 361 us -> 342 us  [flip(): return lax.ppermute(x, 'seq', [(i, i ^ bit) for i in range(peers)])]
    unnamed x495 -> x497, local copies, waits for them, and re-layouts: 114 us -> 117 us
  transfers between devices with their start and end apart: 115 -> 115, of which waited for: 56 -> 54; matrix products, arithmetic and copies ran while one was open for 27% -> 28% of each run, Pallas kernels for 15% -> 15%
where the time goes in v3:
time: 1220 us; the launch traced here: 1210 us
  waiting for transfers between devices  388 us (32%)
  Pallas kernels  208 us (17%)
  local copies, waits for them, and re-layouts  204 us (17%)
  other arithmetic  162 us (13%)
  matrix products  122 us (10%)
  starting transfers between devices  107 us (9%)
  between operations  18 us (1%)
    ppermute x77, waiting for transfers between devices, flip(): return lax.ppermute(x, 'seq', [(i, i ^ bit) for i in range(peers)])  342 us
    unnamed x497, local copies, waits for them, and re-layouts  117 us
    ppermute x77, starting transfers between devices, flip(): return lax.ppermute(x, 'seq', [(i, i ^ bit) for i in range(peers)])  85.9 us
    pallas_call x12, Pallas kernels, outer_half(): pl.pallas_call(outer_kernel, grid_spec=pltpu.PrefetchScalarGridSpec(num_s...  76 us
    dot_general x8, matrix products, dense_back(): lax.dot_general(left, right, (((1,), (1,)), ((), ())), preferred_element_...  65.6 us
    dot_general x8, matrix products, dense(): return jnp.dot(left, right, preferred_element_type=jnp.float32)  56.4 us
    ppermute x4, waiting for transfers between devices, sum_column(): x = x + lax.ppermute(x, 'dp', [(i, i ^ step) for i in range(peers)])  31.7 us
    pallas_call x1, Pallas kernels, attn_bwd(): pl.pallas_call(attn_bwd_kernel, grid=(pairs,), in_specs=specs + [pl.Block...  29 us
  transfers between devices with their start and end apart: 115, of which 54 were waited for; matrix products, arithmetic and copies ran while one was open for 28% of the time, Pallas kernels for 15%

profile of v3, /device:TPU:0, one launch (start us, length us, event | category | flops | bytes accessed | tf_op | source)
XLA Modules:
  0.0 1209.9 jit_solution(2423588701154456852)
XLA Ops:
  37.6 10.6 collective-permute-done.3
  48.3 12.7 %collective-permute-done.4 = f32[170,128]{1,0:T(8,128)S(1)} collective-permute-done((f32[170,128]{1,0:T(8,128)S(1)}, f32[170,128]{1,0:T(8,128)S(1)}, u32[]{:S(2)}, u32[]{:S(2)}) %collective-permute-start.4) | collective-permute-done | bytes 87072 | tf_op jit(solution)/shard_map/ppermute | solution.py:539
  73.2 14.5 %collective-permute-done.5.refs_1_ = bf16[384,1536]{1,0:T(8,128)(2,1)S(1)} collective-permute-done((bf16[384,1536]{1,0:T(8,128)(2,1)S(1)}, bf16[384,1536]{1,0:T(8,128)(2,1)S(1)}, u32[]{:S(2)}, u32[]{:S(2)}) %collective-permute-start.5) | collective-permute-done | bytes 1179680 | tf_op jit(solution)/shard_map/ppermute | solution.py:155
  97.5 8.6 cut_tracks.1
  114.8 9.7 collective-permute-done.7.refs_3_
  129.7 5.3 all-gather.11.cloned.1.call-done
  150.0 13.0 %conv_forward.1 = bf16[1536,384]{1,0:T(8,128)(2,1)S(1)} custom-call(bf16[1536,1536]{1,0:T(8,128)(2,1)S(1)} %bitcast.595, bf16[5,1536,384]{2,1,0:T(8,128)(2,1)S(1)} %bitcast.585), custom_call_target="tpu_custom_call" | custom-call | flops 13589544960 | tf_op jit(solution)/shard_map/conv_forward/pallas_call | solution.py:365
  178.1 33.9 %collective-permute-done.15 = bf16[384,384]{1,0:T(8,128)(2,1)S(1)} collective-permute-done((bf16[384,384]{1,0:T(8,128)(2,1)S(1)}, bf16[384,384]{1,0:T(8,128)(2,1)S(1)}, u32[]{:S(2)}, u32[]{:S(2)}) %collective-permute-start.15) | collective-permute-done | bytes 294944 | tf_op jit(solution)/shard_map/ppermute | solution.py:155
  247.8 7.6 collective-permute-done.38.refs_0_
  263.9 25.6 %collective-permute-done.24.refs_1_ = bf16[384,2048]{1,0:T(8,128)(2,1)S(1)} collective-permute-done((bf16[384,2048]{1,0:T(8,128)(2,1)}, bf16[384,2048]{1,0:T(8,128)(2,1)S(1)}, u32[]{:S(2)}, u32[]{:S(2)}) %collective-permute-start.24) | collective-permute-done | bytes 1572896 | tf_op jit(solution)/shard_map/ppermute | solution.py:155
  306.4 11.2 collective-permute-done.26.refs_3_
  319.0 18.3 %collective-permute-done.27.refs_4_ = bf16[192,2048]{1,0:T(8,128)(2,1)} collective-permute-done((bf16[192,2048]{1,0:T(8,128)(2,1)}, bf16[192,2048]{1,0:T(8,128)(2,1)}, u32[]{:S(2)}, u32[]{:S(2)}) %collective-permute-start.27) | collective-permute-done | bytes 786464 | tf_op jit(solution)/shard_map/ppermute | solution.py:155
  350.2 5.4 collective-permute-done.48
  360.4 12.3 %attention_forward.1.left_ref = bf16[384,1536]{1,0:T(8,128)(2,1)S(1)} custom-call(bf16[384,512]{1,0:T(8,128)(2,1)S(1)} %copy-done.75, bf16[1536,2048]{1,0:T(8,128)(2,1)} %bitcast.566, f32[4,2,1920]{2,1,0:T(2,128)S(1)} %fusion.108.u_ref), custom_call_target="tpu_custom_call" | custom-call | flops 14000000000 | tf_op jit(solution)/shard_map/attention_forward/pallas_call | solution.py:62
  376.6 27.4 %collective-permute-done.29.refs_0_.refs_1_ = bf16[2,4,48,3072]{3,2,1,0:T(8,128)(2,1)S(1)} collective-permute-done((bf16[2,4,48,3072]{3,2,1,0:T(8,128)(2,1)}, bf16[2,4,48,3072]{3,2,1,0:T(8,128)(2,1)S(1)}, u32[]{:S(2)}, u32[]{:S(2)}) %collective-permute-start.29) | collective-permute-done | bytes 2359328 | tf_op jit(solution)/shard_map/ppermute | solution.py:155
  415.0 12.8 %sort_copies.11 = (bf16[2,4,4,1,48,3072]{5,4,3,2,1,0:T(8,128)(2,1)}, bf16[2,4,4,2,48,1536]{5,4,3,2,1,0:T(8,128)(2,1)}) custom-call(bf16[2,4,48,3072]{3,2,1,0:T(8,128)(2,1)} %tie.68.refs_0_, bf16[2,4,48,3072]{3,2,1,0:T(8,128)(2,1)S(1)} %copy-done.17, bf16[2,4,48,3072]{3,2,1,0:T(8,128)(2,1)} %collective-permute-done.30.refs_2_, ...), custom_call_target="tpu_custom_call" | custom-call | bytes 75497472 | tf_op jit(solution)/shard_map/sort_copies/pallas_call | solution.py:197
  427.9 10.7 multiply_convert_fusion.3
  449.0 24.3 %collective-permute-done.40.refs_1_ = bf16[384,1536]{1,0:T(8,128)(2,1)} collective-permute-done((bf16[384,1536]{1,0:T(8,128)(2,1)}, bf16[384,1536]{1,0:T(8,128)(2,1)}, u32[]{:S(2)}, u32[]{:S(2)}) %collective-permute-start.40) | collective-permute-done | bytes 1179680 | tf_op jit(solution)/shard_map/ppermute | solution.py:155
  483.6 7.6 collective-permute-done.42.refs_3_
  497.4 13.9 %multiply_convert_fusion.1 = (bf16[896,3072]{1,0:T(8,128)(2,1)}, f32[896,3072]{1,0:T(8,128)}) fusion(f32[3072]{0:T(1024)S(1)} %get-tuple-element.194, bf16[896,1536]{1,0:T(8,128)(2,1)S(1)} %constant_dynamic-slice_fusion.31.left_ref, bf16[1536,3072]{1,0:T(8,128)(2,1)S(1)} %bitcast.593), kind=kOutput, calls=%fused_computation.11 | convolution fusion | flops 8483241984 | bytes 28717056 | tf_op jit(solution)/shard_map/dot_general | solution.py:649
  524.9 8.7 fusion.63
  541.5 8.9 multiply_convert_fusion.4
  551.4 18.8 %multiply_convert_fusion.refs_0_ = bf16[896,3072]{1,0:T(8,128)(2,1)S(1)} fusion(bf16[896,3072]{1,0:T(8,128)(2,1)} %collective-permute-done.53, f32[896,3072]{1,0:T(8,128)} %get-tuple-element.222, f32[3072]{0:T(1024)S(1)} %get-tuple-element.194, pred[]{:T(512)S(6)} %eq.8, bf16[3072,1024]{1,0:T(8,128)(2,1)} %bitcast.634, ...), kind=kOutput, calls=%fused_computation.10 | convolution fusion | flops 5709627392 | bytes 30158848 | tf_op jit(solution)/shard_map/dot_general | solution.py:653
  570.2 13.3 %convolution_convert_fusion.1.x_ref = bf16[896,1536]{1,0:T(8,128)(2,1)S(1)} fusion(bf16[896,3072]{1,0:T(8,128)(2,1)S(1)} %multiply_convert_fusion.refs_0_, bf16[1536,3072]{1,0:T(8,128)(2,1)} %bitcast.594), kind=kOutput, calls=%fused_computation.32 | convolution fusion | flops 8457093120 | bytes 17694720 | tf_op jit(solution)/shard_map/dot_general | solution.py:653
  595.0 6.8 outer_half.12.refs_2_
  612.0 12.4 %tracks_grad.1 = bf16[3072,1024]{1,0:T(8,128)(2,1)S(1)} custom-call(bf16[896,3072]{1,0:T(8,128)(2,1)S(1)} %copy-done.47, bf16[896,3072]{1,0:T(8,128)(2,1)} %get-tuple-element.221.second_ref, bf16[896,1024]{1,0:T(8,128)(2,1)S(1)} %copy-done.45), custom_call_target="tpu_custom_call" | custom-call | flops 11274289152 | tf_op jit(solution)/shard_map/tracks_grad/pallas_call | solution.py:333
  624.4 8.2 collective-permute-done.54
  642.2 12.5 %collective-permute-done.55.refs_0_ = bf16[192,1536]{1,0:T(8,128)(2,1)S(1)} collective-permute-done((bf16[192,1536]{1,0:T(8,128)(2,1)}, bf16[192,1536]{1,0:T(8,128)(2,1)S(1)}, u32[]{:S(2)}, u32[]{:S(2)}) %collective-permute-start.55) | collective-permute-done | bytes 589856 | tf_op jit(solution)/shard_map/ppermute | solution.py:155
  660.0 8.7 outer_half.13
  673.5 5.3 outer_half.14
  691.0 9.3 multiply_convert_fusion.2.refs_0_
  709.0 6.1 outer_half.15
  724.8 7.4 collective-permute-done.64.refs_0_
  740.7 7.5 multiply_reduce_fusion
  767.0 5.1 outer_half.17
  774.3 29.0 %attention_backward.1 = (bf16[384,512]{1,0:T(8,128)(2,1)}, bf16[1536,2048]{1,0:T(8,128)(2,1)}, f32[4,2,1920]{2,1,0:T(2,128)}) custom-call(bf16[384,512]{1,0:T(8,128)(2,1)} %fusion.81.q_ref, bf16[1536,2048]{1,0:T(8,128)(2,1)} %bitcast.567, f32[4,2,1920]{2,1,0:T(2,128)} %copy-done.74, bf16[384,1536]{1,0:T(8,128)(2,1)} %tie.94.g_ref), custom_call_target="tpu_custom_call" | custom-call | flops 32000000000 | tf_op jit(solution)/shard_map/attention_backward/pallas_call | solution.py:130
  830.2 25.8 %collective-permute-done.71 = bf16[2,192,2048]{2,1,0:T(8,128)(2,1)} collective-permute-done((bf16[2,192,2048]{2,1,0:T(8,128)(2,1)}, bf16[2,192,2048]{2,1,0:T(8,128)(2,1)}, u32[]{:S(2)}, u32[]{:S(2)}) %collective-permute-start.71) | collective-permute-done | bytes 1572896 | tf_op jit(solution)/shard_map/ppermute | solution.py:155
  866.7 5.2 fusion.134
  901.1 6.6 multiply_reduce_fusion.1
  940.5 8.8 collective-permute-done.80.refs_0_
  958.7 5.1 outer_half.21
  975.2 11.5 outer_half.22.refs_1_
  994.6 16.1 %conv_back.1.refs_0_.refs_1_ = bf16[1536,1536]{1,0:T(8,128)(2,1)S(1)} custom-call(bf16[1536,1920]{1,0:T(8,128)(2,1)S(1)} %bitcast.582, bf16[5,1536,384]{2,1,0:T(8,128)(2,1)} %bitcast.584), custom_call_target="tpu_custom_call" | custom-call | flops 13589544960 | tf_op jit(solution)/shard_map/conv_back/pallas_call | solution.py:393
  1012.9 13.8 %collective-permute-done.83 = bf16[4,2,48,2048]{3,2,0,1:T(8,128)(2,1)} collective-permute-done((bf16[4,2,48,2048]{3,2,0,1:T(8,128)(2,1)S(1)}, bf16[4,2,48,2048]{3,2,0,1:T(8,128)(2,1)}, u32[]{:S(2)}, u32[]{:S(2)}) %collective-permute-start.83) | collective-permute-done | bytes 1572896 | tf_op jit(solution)/shard_map/ppermute | solution.py:155
  1044.1 15.1 %outer_half.23 = bf16[3840,384]{1,0:T(8,128)(2,1)} custom-call(s32[1]{0:T(128)} %bitcast.168.base_ref, bf16[1536,1536]{1,0:T(8,128)(2,1)S(1)} %bitcast.601, bf16[1536,1920]{1,0:T(8,128)(2,1)} %tie.116.right_ref, bf16[3840,384]{1,0:T(8,128)(2,1)} %collective-permute-done.97.refs_0_), custom_call_target="tpu_custom_call" | custom-call | flops 6794772480 | tf_op jit(solution)/shard_map/outer_half/pallas_call | solution.py:424
  1059.5 22.1 %collective-permute-done.86 = bf16[4,48,2048]{2,1,0:T(8,128)(2,1)} collective-permute-done((bf16[4,48,2048]{2,1,0:T(8,128)(2,1)}, bf16[4,48,2048]{2,1,0:T(8,128)(2,1)}, u32[]{:S(2)}, u32[]{:S(2)}) %collective-permute-start.86) | collective-permute-done | bytes 786464 | tf_op jit(solution)/shard_map/ppermute | solution.py:155
  1139.5 14.5 %collective-permute-done.93 = f32[146,128]{1,0:T(8,128)} collective-permute-done((f32[146,128]{1,0:T(8,128)}, f32[146,128]{1,0:T(8,128)}, u32[]{:S(2)}, u32[]{:S(2)}) %collective-permute-start.93) | collective-permute-done | bytes 74784 | tf_op jit(solution)/shard_map/ppermute | solution.py:155
  1160.7 7.6 collective-permute-done.95
  (1019 shorter events, 586.5 us)
Async XLA Ops:
  7.2 82.4 %all-gather.9.cloned.1.call-start = ((), (), s32[]{:S(2)}) async-start(), calls=%async_computation.8 | async-start | bytes 3686400 | tf_op jit(solution)/shard_map/all_gather | solution.py:713
  24.8 110.2 %all-gather.11.cloned.1.call-start = ((), (), s32[]{:S(2)}) async-start(), calls=%async_computation.9 | async-start | bytes 1966080 | tf_op jit(solution)/shard_map/all_gather | solution.py:755
  89.9 45.1 %collective-permute-start.12 = (bf16[4,4,240,384]{3,2,1,0:T(8,128)(2,1)}, bf16[4,4,240,384]{3,2,1,0:T(8,128)(2,1)}, u32[]{:S(2)}, u32[]{:S(2)}) collective-permute-start(bf16[4,4,240,384]{3,2,1,0:T(8,128)(2,1)} %tie.61.refs_0_), channel_id=1, source_target_pairs={{0,16},{16,0},{1,17},{17,1},{2,18},{18,2},{3,19},{19,3},{4,20},{20... | collective-permute-start | bytes 8847368 | tf_op jit(solution)/shard_map/ppermute | solution.py:159
  95.8 164.9 %all-gather.13.cloned.1.call-start = ((), (), s32[]{:S(2)}) async-start(), calls=%async_computation.10 | async-start | bytes 4423680 | tf_op jit(solution)/shard_map/all_gather | solution.py:760
  107.3 63.8 %collective-permute-start.36 = (bf16[4,416,512]{2,1,0:T(8,128)(2,1)}, bf16[4,416,512]{2,1,0:T(8,128)(2,1)}, u32[]{:S(2)}, u32[]{:S(2)}) collective-permute-start(bf16[4,416,512]{2,1,0:T(8,128)(2,1)} %get-tuple-element.39), channel_id=1, source_target_pairs={{0,16},{1,17},{2,18},{3,19},{4,20},{5,21},{6,22},{7,23},{8,24},{9,... | collective-permute-start | bytes 5111816 | tf_op jit(solution)/shard_map/ppermute | solution.py:163
  135.0 309.9 %all-gather.15.cloned.1.call-start = ((), (), s32[]{:S(2)}) async-start(), calls=%async_computation.11 | async-start | bytes 7864320 | tf_op jit(solution)/shard_map/all_gather | solution.py:794
  165.3 61.9 %collective-permute-start.17 = (bf16[2,4,48,2048]{3,2,1,0:T(8,128)(2,1)}, bf16[2,4,48,2048]{3,2,1,0:T(8,128)(2,1)}, u32[]{:S(2)}, u32[]{:S(2)}) collective-permute-start(bf16[2,4,48,2048]{3,2,1,0:T(8,128)(2,1)} %tie.64.refs_0_), channel_id=1, source_target_pairs={{0,2},{1,3},{2,0},{3,1},{4,6},{5,7},{6,4},{7,5},{8,10},{9,11},{10,... | collective-permute-start | bytes 4718600 | tf_op jit(solution)/shard_map/ppermute | solution.py:155
  167.4 59.9 %collective-permute-start.21 = (bf16[2,4,48,2048]{3,2,1,0:T(8,128)(2,1)}, bf16[2,4,48,2048]{3,2,1,0:T(8,128)(2,1)}, u32[]{:S(2)}, u32[]{:S(2)}) collective-permute-start(bf16[2,4,48,2048]{3,2,1,0:T(8,128)(2,1)} %tie.65.refs_4_), channel_id=1, source_target_pairs={{0,1},{1,0},{2,3},{3,2},{4,5},{5,4},{6,7},{7,6},{8,9},{9,8},{10,11... | collective-permute-start | bytes 4718600 | tf_op jit(solution)/shard_map/ppermute | solution.py:155
  168.8 43.2 %collective-permute-start.15 = (bf16[384,384]{1,0:T(8,128)(2,1)S(1)}, bf16[384,384]{1,0:T(8,128)(2,1)S(1)}, u32[]{:S(2)}, u32[]{:S(2)}) collective-permute-start(bf16[384,384]{1,0:T(8,128)(2,1)S(1)} %get-tuple-element.171), channel_id=1, source_target_pairs={{0,3},{1,2},{2,1},{3,0},{4,7},{5,6},{6,5},{7,4},{8,11},{9,10},{10,... | collective-permute-start | bytes 884744 | tf_op jit(solution)/shard_map/ppermute | solution.py:155
  170.3 43.5 %collective-permute-start.14 = (bf16[384,384]{1,0:T(8,128)(2,1)S(1)}, bf16[384,384]{1,0:T(8,128)(2,1)S(1)}, u32[]{:S(2)}, u32[]{:S(2)}) collective-permute-start(bf16[384,384]{1,0:T(8,128)(2,1)S(1)} %get-tuple-element.172), channel_id=1, source_target_pairs={{0,2},{1,3},{2,0},{3,1},{4,6},{5,7},{6,4},{7,5},{8,10},{9,11},{10,... | collective-permute-start | bytes 884744 | tf_op jit(solution)/shard_map/ppermute | solution.py:155
  171.1 46.5 %collective-permute-start.13 = (bf16[384,384]{1,0:T(8,128)(2,1)S(1)}, bf16[384,384]{1,0:T(8,128)(2,1)S(1)}, u32[]{:S(2)}, u32[]{:S(2)}) collective-permute-start(bf16[384,384]{1,0:T(8,128)(2,1)S(1)} %get-tuple-element.173), channel_id=1, source_target_pairs={{0,1},{1,0},{2,3},{3,2},{4,5},{5,4},{6,7},{7,6},{8,9},{9,8},{10,11... | collective-permute-start | bytes 884744 | tf_op jit(solution)/shard_map/ppermute | solution.py:155
  245.6 44.0 %collective-permute-start.24 = (bf16[384,2048]{1,0:T(8,128)(2,1)}, bf16[384,2048]{1,0:T(8,128)(2,1)S(1)}, u32[]{:S(2)}, u32[]{:S(2)}) collective-permute-start(bf16[384,2048]{1,0:T(8,128)(2,1)} %convolution_convert_fusion.3.refs_0_), channel_id=1, source_target_pairs={{0,1},{1,0},{2,3},{3,2},{4,5},{5,4},{6,7},{7,6},{8,9},{9,8},{10,11... | collective-permute-start | bytes 4718600 | tf_op jit(solution)/shard_map/ppermute | solution.py:155
  246.2 43.3 %collective-permute-start.25 = (bf16[384,2048]{1,0:T(8,128)(2,1)}, bf16[384,2048]{1,0:T(8,128)(2,1)S(1)}, u32[]{:S(2)}, u32[]{:S(2)}) collective-permute-start(bf16[384,2048]{1,0:T(8,128)(2,1)} %convolution_convert_fusion.3.refs_0_), channel_id=1, source_target_pairs={{0,2},{1,3},{2,0},{3,1},{4,6},{5,7},{6,4},{7,5},{8,10},{9,11},{10,... | collective-permute-start | bytes 4718600 | tf_op jit(solution)/shard_map/ppermute | solution.py:155
  291.2 50.7 %collective-permute-start.28 = (bf16[4,48,3072]{2,1,0:T(8,128)(2,1)}, bf16[4,48,3072]{2,1,0:T(8,128)(2,1)}, u32[]{:S(2)}, u32[]{:S(2)}) collective-permute-start(bf16[4,48,3072]{2,1,0:T(8,128)(2,1)} %tie.67), channel_id=1, source_target_pairs={{0,1},{1,0},{2,3},{3,2},{4,5},{5,4},{6,7},{7,6},{8,9},{9,8},{10,11... | collective-permute-start | bytes 3538952 | tf_op jit(solution)/shard_map/ppermute | solution.py:155
  294.5 570.3 %reduce-scatter.5.cloned.1.call-start = ((), (), s32[]{:S(2)}) async-start(), calls=%async_computation.4 | async-start | bytes 7864320 | tf_op jit(solution)/shard_map/reduce_scatter | solution.py:884
  299.1 38.1 %collective-permute-start.27 = (bf16[192,2048]{1,0:T(8,128)(2,1)}, bf16[192,2048]{1,0:T(8,128)(2,1)}, u32[]{:S(2)}, u32[]{:S(2)}) collective-permute-start(bf16[192,2048]{1,0:T(8,128)(2,1)} %slice.357), channel_id=1, source_target_pairs={{0,1},{1,0},{2,3},{3,2},{4,5},{5,4},{6,7},{7,6},{8,9},{9,8},{10,11... | collective-permute-start | bytes 2359304 | tf_op jit(solution)/shard_map/ppermute | solution.py:155
  300.4 45.7 %collective-permute-start.32 = (bf16[4,48,3072]{2,1,0:T(8,128)(2,1)}, bf16[4,48,3072]{2,1,0:T(8,128)(2,1)}, u32[]{:S(2)}, u32[]{:S(2)}) collective-permute-start(bf16[4,48,3072]{2,1,0:T(8,128)(2,1)} %tie.70), channel_id=1, source_target_pairs={{0,2},{1,3},{2,0},{3,1},{4,6},{5,7},{6,4},{7,5},{8,10},{9,11},{10,... | collective-permute-start | bytes 3538952 | tf_op jit(solution)/shard_map/ppermute | solution.py:155
  305.6 50.0 %collective-permute-start.48 = (bf16[4,48,1536]{2,1,0:T(8,128)(2,1)}, bf16[4,48,1536]{2,1,0:T(8,128)(2,1)}, u32[]{:S(2)}, u32[]{:S(2)}) collective-permute-start(bf16[4,48,1536]{2,1,0:T(8,128)(2,1)} %tie.81), channel_id=1, source_target_pairs={{0,2},{1,3},{2,0},{3,1},{4,6},{5,7},{6,4},{7,5},{8,10},{9,11},{10,... | collective-permute-start | bytes 1769480 | tf_op jit(solution)/shard_map/ppermute | solution.py:155
  317.6 40.4 %collective-permute-start.44 = (bf16[4,48,1536]{2,1,0:T(8,128)(2,1)}, bf16[4,48,1536]{2,1,0:T(8,128)(2,1)}, u32[]{:S(2)}, u32[]{:S(2)}) collective-permute-start(bf16[4,48,1536]{2,1,0:T(8,128)(2,1)} %tie.78), channel_id=1, source_target_pairs={{0,1},{1,0},{2,3},{3,2},{4,5},{5,4},{6,7},{7,6},{8,9},{9,8},{10,11... | collective-permute-start | bytes 1769480 | tf_op jit(solution)/shard_map/ppermute | solution.py:155
  344.8 59.2 %collective-permute-start.29 = (bf16[2,4,48,3072]{3,2,1,0:T(8,128)(2,1)}, bf16[2,4,48,3072]{3,2,1,0:T(8,128)(2,1)S(1)}, u32[]{:S(2)}, u32[]{:S(2)}) collective-permute-start(bf16[2,4,48,3072]{3,2,1,0:T(8,128)(2,1)} %tie.68.refs_0_), channel_id=1, source_target_pairs={{0,2},{1,3},{2,0},{3,1},{4,6},{5,7},{6,4},{7,5},{8,10},{9,11},{10,... | collective-permute-start | bytes 7077896 | tf_op jit(solution)/shard_map/ppermute | solution.py:155
  349.3 54.7 %collective-permute-start.33 = (bf16[2,4,48,3072]{3,2,1,0:T(8,128)(2,1)}, bf16[2,4,48,3072]{3,2,1,0:T(8,128)(2,1)}, u32[]{:S(2)}, u32[]{:S(2)}) collective-permute-start(bf16[2,4,48,3072]{3,2,1,0:T(8,128)(2,1)} %tie.71.refs_4_), channel_id=1, source_target_pairs={{0,1},{1,0},{2,3},{3,2},{4,5},{5,4},{6,7},{7,6},{8,9},{9,8},{10,11... | collective-permute-start | bytes 7077896 | tf_op jit(solution)/shard_map/ppermute | solution.py:155
  376.1 36.2 %collective-permute-start.30 = (bf16[2,4,48,3072]{3,2,1,0:T(8,128)(2,1)}, bf16[2,4,48,3072]{3,2,1,0:T(8,128)(2,1)}, u32[]{:S(2)}, u32[]{:S(2)}) collective-permute-start(bf16[2,4,48,3072]{3,2,1,0:T(8,128)(2,1)} %tie.68.refs_0_), channel_id=1, source_target_pairs={{0,16},{16,0},{1,17},{17,1},{2,18},{18,2},{3,19},{19,3},{4,20},{20... | collective-permute-start | bytes 7077896 | tf_op jit(solution)/shard_map/ppermute | solution.py:159
  376.1 37.5 %collective-permute-start.34 = (bf16[2,4,48,3072]{3,2,1,0:T(8,128)(2,1)}, bf16[2,4,48,3072]{3,2,1,0:T(8,128)(2,1)}, u32[]{:S(2)}, u32[]{:S(2)}) collective-permute-start(bf16[2,4,48,3072]{3,2,1,0:T(8,128)(2,1)} %tie.71.refs_4_), channel_id=1, source_target_pairs={{0,16},{16,0},{1,17},{17,1},{2,18},{18,2},{3,19},{19,3},{4,20},{20... | collective-permute-start | bytes 7077896 | tf_op jit(solution)/shard_map/ppermute | solution.py:159
  410.9 36.5 %collective-permute-start.45 = (bf16[2,4,48,1536]{3,2,1,0:T(8,128)(2,1)S(1)}, bf16[2,4,48,1536]{3,2,1,0:T(8,128)(2,1)}, u32[]{:S(2)}, u32[]{:S(2)}) collective-permute-start(bf16[2,4,48,1536]{3,2,1,0:T(8,128)(2,1)S(1)} %copy-done.35), channel_id=1, source_target_pairs={{0,2},{1,3},{2,0},{3,1},{4,6},{5,7},{6,4},{7,5},{8,10},{9,11},{10,... | collective-permute-start | bytes 3538952 | tf_op jit(solution)/shard_map/ppermute | solution.py:155
  601.8 58.2 %collective-permute-start.58 = (bf16[768,3072]{1,0:T(8,128)(2,1)}, bf16[768,3072]{1,0:T(8,128)(2,1)}, u32[]{:S(2)}, u32[]{:S(2)}) collective-permute-start(bf16[768,3072]{1,0:T(8,128)(2,1)} %outer_half.12.refs_2_), channel_id=1, source_target_pairs={{0,16},{16,0},{1,17},{17,1},{2,18},{18,2},{3,19},{19,3},{4,20},{20... | collective-permute-start | bytes 14155784 | tf_op jit(solution)/shard_map/ppermute | solution.py:159
  681.7 503.1 %reduce-scatter.11.cloned.1.call-start = ((), (), s32[]{:S(2)}) async-start(), calls=%async_computation.7 | async-start | bytes 4423680 | tf_op jit(solution)/shard_map/reduce_scatter | solution.py:945
  724.6 41.4 %collective-permute-start.63 = (bf16[768,3072]{1,0:T(8,128)(2,1)}, bf16[768,3072]{1,0:T(8,128)(2,1)}, u32[]{:S(2)}, u32[]{:S(2)}) collective-permute-start(bf16[768,3072]{1,0:T(8,128)(2,1)} %outer_half.16), channel_id=1, source_target_pairs={{0,16},{16,0},{1,17},{17,1},{2,18},{18,2},{3,19},{19,3},{4,20},{20... | collective-permute-start | bytes 14155784 | tf_op jit(solution)/shard_map/ppermute | solution.py:159
  755.3 58.1 %collective-permute-start.66 = (bf16[768,1536]{1,0:T(8,128)(2,1)}, bf16[768,1536]{1,0:T(8,128)(2,1)S(1)}, u32[]{:S(2)}, u32[]{:S(2)}) collective-permute-start(bf16[768,1536]{1,0:T(8,128)(2,1)} %outer_half.18), channel_id=1, source_target_pairs={{0,16},{16,0},{1,17},{17,1},{2,18},{18,2},{3,19},{19,3},{4,20},{20... | collective-permute-start | bytes 7077896 | tf_op jit(solution)/shard_map/ppermute | solution.py:159
  756.2 47.1 %collective-permute-start.67 = (bf16[4,48,1536]{2,1,0:T(8,128)(2,1)}, bf16[4,48,1536]{2,1,0:T(8,128)(2,1)}, u32[]{:S(2)}, u32[]{:S(2)}) collective-permute-start(bf16[4,48,1536]{2,1,0:T(8,128)(2,1)} %dynamic-slice_bitcast_fusion.24), channel_id=1, source_target_pairs={{0,2},{1,3},{2,0},{3,1},{4,6},{5,7},{6,4},{7,5},{8,10},{9,11},{10,... | collective-permute-start | bytes 1769480 | tf_op jit(solution)/shard_map/ppermute | solution.py:155
  758.0 45.2 %collective-permute-start.68 = (bf16[4,48,1536]{2,1,0:T(8,128)(2,1)}, bf16[4,48,1536]{2,1,0:T(8,128)(2,1)}, u32[]{:S(2)}, u32[]{:S(2)}) collective-permute-start(bf16[4,48,1536]{2,1,0:T(8,128)(2,1)} %dynamic-slice_bitcast_fusion.23), channel_id=1, source_target_pairs={{0,1},{1,0},{2,3},{3,2},{4,5},{5,4},{6,7},{7,6},{8,9},{9,8},{10,11... | collective-permute-start | bytes 1769480 | tf_op jit(solution)/shard_map/ppermute | solution.py:155
  761.0 42.3 %collective-permute-start.69 = (bf16[4,2,96,768]{3,2,1,0:T(8,128)(2,1)}, bf16[4,2,96,768]{3,2,1,0:T(8,128)(2,1)}, u32[]{:S(2)}, u32[]{:S(2)}) collective-permute-start(bf16[4,2,96,768]{3,2,1,0:T(8,128)(2,1)} %dynamic-slice_bitcast_fusion.3), channel_id=1, source_target_pairs={{0,1},{1,0},{2,3},{3,2},{4,5},{5,4},{6,7},{7,6},{8,9},{9,8},{10,11... | collective-permute-start | bytes 3538952 | tf_op jit(solution)/shard_map/ppermute | solution.py:155
  766.0 37.3 %collective-permute-start.70 = (bf16[4,2,96,768]{3,2,1,0:T(8,128)(2,1)}, bf16[4,2,96,768]{3,2,1,0:T(8,128)(2,1)}, u32[]{:S(2)}, u32[]{:S(2)}) collective-permute-start(bf16[4,2,96,768]{3,2,1,0:T(8,128)(2,1)} %dynamic-slice_bitcast_fusion.2), channel_id=1, source_target_pairs={{0,2},{1,3},{2,0},{3,1},{4,6},{5,7},{6,4},{7,5},{8,10},{9,11},{10,... | collective-permute-start | bytes 3538952 | tf_op jit(solution)/shard_map/ppermute | solution.py:155
  819.9 36.1 %collective-permute-start.71 = (bf16[2,192,2048]{2,1,0:T(8,128)(2,1)}, bf16[2,192,2048]{2,1,0:T(8,128)(2,1)}, u32[]{:S(2)}, u32[]{:S(2)}) collective-permute-start(bf16[2,192,2048]{2,1,0:T(8,128)(2,1)} %pad_maximum_fusion.20), channel_id=1, source_target_pairs={{0,1},{1,0},{2,3},{3,2},{4,5},{5,4},{6,7},{7,6},{8,9},{9,8},{10,11... | collective-permute-start | bytes 4718600 | tf_op jit(solution)/shard_map/ppermute | solution.py:155
  875.4 50.3 %collective-permute-start.79 = (bf16[4,2,48,1536]{3,2,1,0:T(8,128)(2,1)}, bf16[4,2,48,1536]{3,2,1,0:T(8,128)(2,1)}, u32[]{:S(2)}, u32[]{:S(2)}) collective-permute-start(bf16[4,2,48,1536]{3,2,1,0:T(8,128)(2,1)} %get-tuple-element.124), channel_id=1, source_target_pairs={{0,1},{1,0},{2,3},{3,2},{4,5},{5,4},{6,7},{7,6},{8,9},{9,8},{10,11... | collective-permute-start | bytes 3538952 | tf_op jit(solution)/shard_map/ppermute | solution.py:155
  878.1 51.3 %collective-permute-start.81 = (bf16[4,2,48,1536]{3,2,1,0:T(8,128)(2,1)}, bf16[4,2,48,1536]{3,2,1,0:T(8,128)(2,1)}, u32[]{:S(2)}, u32[]{:S(2)}) collective-permute-start(bf16[4,2,48,1536]{3,2,1,0:T(8,128)(2,1)} %get-tuple-element.122), channel_id=1, source_target_pairs={{0,2},{1,3},{2,0},{3,1},{4,6},{5,7},{6,4},{7,5},{8,10},{9,11},{10,... | collective-permute-start | bytes 3538952 | tf_op jit(solution)/shard_map/ppermute | solution.py:155
  880.0 41.2 %collective-permute-start.101 = (bf16[4,96,768]{2,1,0:T(8,128)(2,1)}, bf16[4,96,768]{2,1,0:T(8,128)(2,1)}, u32[]{:S(2)}, u32[]{:S(2)}) collective-permute-start(bf16[4,96,768]{2,1,0:T(8,128)(2,1)} %dynamic-slice_bitcast_fusion.16), channel_id=1, source_target_pairs={{0,2},{1,3},{2,0},{3,1},{4,6},{5,7},{6,4},{7,5},{8,10},{9,11},{10,... | collective-permute-start | bytes 1769480 | tf_op jit(solution)/shard_map/ppermute | solution.py:155
  885.6 37.1 %collective-permute-start.102 = (bf16[4,96,768]{2,1,0:T(8,128)(2,1)}, bf16[4,96,768]{2,1,0:T(8,128)(2,1)}, u32[]{:S(2)}, u32[]{:S(2)}) collective-permute-start(bf16[4,96,768]{2,1,0:T(8,128)(2,1)} %dynamic-slice_bitcast_fusion.15), channel_id=1, source_target_pairs={{0,1},{1,0},{2,3},{3,2},{4,5},{5,4},{6,7},{7,6},{8,9},{9,8},{10,11... | collective-permute-start | bytes 1769480 | tf_op jit(solution)/shard_map/ppermute | solution.py:155
  897.6 59.4 %collective-permute-start.78 = (bf16[768,2560]{1,0:T(8,128)(2,1)}, bf16[768,2560]{1,0:T(8,128)(2,1)}, u32[]{:S(2)}, u32[]{:S(2)}) collective-permute-start(bf16[768,2560]{1,0:T(8,128)(2,1)} %copy-done.19), channel_id=1, source_target_pairs={{0,16},{16,0},{1,17},{17,1},{2,18},{18,2},{3,19},{19,3},{4,20},{20... | collective-permute-start | bytes 11796488 | tf_op jit(solution)/shard_map/ppermute | solution.py:159
  957.0 231.1 %reduce-scatter.7.cloned.1.call-start = ((), (), s32[]{:S(2)}) async-start(), calls=%async_computation.5 | async-start | bytes 3686400 | tf_op jit(solution)/shard_map/reduce_scatter | solution.py:973
  986.7 57.4 %collective-permute-start.97 = (bf16[3840,384]{1,0:T(8,128)(2,1)}, bf16[3840,384]{1,0:T(8,128)(2,1)}, u32[]{:S(2)}, u32[]{:S(2)}) collective-permute-start(bf16[3840,384]{1,0:T(8,128)(2,1)} %outer_half.22.refs_1_), channel_id=1, source_target_pairs={{0,16},{16,0},{1,17},{17,1},{2,18},{18,2},{3,19},{19,3},{4,20},{20... | collective-permute-start | bytes 8847368 | tf_op jit(solution)/shard_map/ppermute | solution.py:159
  989.9 36.9 %collective-permute-start.83 = (bf16[4,2,48,2048]{3,2,0,1:T(8,128)(2,1)S(1)}, bf16[4,2,48,2048]{3,2,0,1:T(8,128)(2,1)}, u32[]{:S(2)}, u32[]{:S(2)}) collective-permute-start(bf16[4,2,48,2048]{3,2,0,1:T(8,128)(2,1)S(1)} %bitcast.644), channel_id=1, source_target_pairs={{0,1},{1,0},{2,3},{3,2},{4,5},{5,4},{6,7},{7,6},{8,9},{9,8},{10,11... | collective-permute-start | bytes 4718600 | tf_op jit(solution)/shard_map/ppermute | solution.py:155
  993.9 36.8 %collective-permute-start.84 = (bf16[4,2,48,2048]{3,2,0,1:T(8,128)(2,1)}, bf16[4,2,48,2048]{3,2,0,1:T(8,128)(2,1)}, u32[]{:S(2)}, u32[]{:S(2)}) collective-permute-start(bf16[4,2,48,2048]{3,2,0,1:T(8,128)(2,1)} %bitcast.538), channel_id=1, source_target_pairs={{0,2},{1,3},{2,0},{3,1},{4,6},{5,7},{6,4},{7,5},{8,10},{9,11},{10,... | collective-permute-start | bytes 4718600 | tf_op jit(solution)/shard_map/ppermute | solution.py:155
  1037.0 49.2 %collective-permute-start.88 = (bf16[2,192,1536]{2,1,0:T(8,128)(2,1)}, bf16[2,192,1536]{2,1,0:T(8,128)(2,1)}, u32[]{:S(2)}, u32[]{:S(2)}) collective-permute-start(bf16[2,192,1536]{2,1,0:T(8,128)(2,1)} %pad_maximum_fusion.35), channel_id=1, source_target_pairs={{0,2},{1,3},{2,0},{3,1},{4,6},{5,7},{6,4},{7,5},{8,10},{9,11},{10,... | collective-permute-start | bytes 3538952 | tf_op jit(solution)/shard_map/ppermute | solution.py:155
  1039.3 48.5 %collective-permute-start.85 = (bf16[2,192,1536]{2,1,0:T(8,128)(2,1)}, bf16[2,192,1536]{2,1,0:T(8,128)(2,1)}, u32[]{:S(2)}, u32[]{:S(2)}) collective-permute-start(bf16[2,192,1536]{2,1,0:T(8,128)(2,1)} %pad_maximum_fusion.34), channel_id=1, source_target_pairs={{0,1},{1,0},{2,3},{3,2},{4,5},{5,4},{6,7},{7,6},{8,9},{9,8},{10,11... | collective-permute-start | bytes 3538952 | tf_op jit(solution)/shard_map/ppermute | solution.py:155
  1041.0 40.6 %collective-permute-start.86 = (bf16[4,48,2048]{2,1,0:T(8,128)(2,1)}, bf16[4,48,2048]{2,1,0:T(8,128)(2,1)}, u32[]{:S(2)}, u32[]{:S(2)}) collective-permute-start(bf16[4,48,2048]{2,1,0:T(8,128)(2,1)} %dynamic-slice_bitcast_fusion.10), channel_id=1, source_target_pairs={{0,2},{1,3},{2,0},{3,1},{4,6},{5,7},{6,4},{7,5},{8,10},{9,11},{10,... | collective-permute-start | bytes 2359304 | tf_op jit(solution)/shard_map/ppermute | solution.py:155
  1043.2 40.7 %collective-permute-start.87 = (bf16[4,48,2048]{2,1,0:T(8,128)(2,1)}, bf16[4,48,2048]{2,1,0:T(8,128)(2,1)}, u32[]{:S(2)}, u32[]{:S(2)}) collective-permute-start(bf16[4,48,2048]{2,1,0:T(8,128)(2,1)} %dynamic-slice_bitcast_fusion.9), channel_id=1, source_target_pairs={{0,1},{1,0},{2,3},{3,2},{4,5},{5,4},{6,7},{7,6},{8,9},{9,8},{10,11... | collective-permute-start | bytes 2359304 | tf_op jit(solution)/shard_map/ppermute | solution.py:155
  1059.3 133.6 %reduce-scatter.9.cloned.1.call-start = ((), (), s32[]{:S(2)}) async-start(), calls=%async_computation.6 | async-start | bytes 1966080 | tf_op jit(solution)/shard_map/reduce_scatter | solution.py:970
  1103.9 66.2 %collective-permute-start.89 = (bf16[4,224,512]{2,1,0:T(8,128)(2,1)}, bf16[4,224,512]{2,1,0:T(8,128)(2,1)S(1)}, u32[]{:S(2)}, u32[]{:S(2)}) collective-permute-start(bf16[4,224,512]{2,1,0:T(8,128)(2,1)} %slice.393), channel_id=1, source_target_pairs={{16,0},{17,1},{18,2},{19,3},{20,4},{21,5},{22,6},{23,7},{24,8},{25... | collective-permute-start | bytes 2752520 | tf_op jit(solution)/shard_map/ppermute | solution.py:167
  (291 other events, 2946.5 us)
Sparse Core Ops, SparseCore 0:
  24.9 64.6 all-gather.8
  95.9 39.0 all-gather.10
  136.5 68.8 all-gather.12
  294.6 114.2 all-gather.14
  681.8 109.4 reduce-scatter.4
  957.1 64.8 reduce-scatter.10
  1059.4 55.4 reduce-scatter.6
  1139.6 37.4 reduce-scatter.8
